TPU v7x, 256 devices: a whole 4x4x8 slice. The times are simulated.
256 devices in a mesh: group: 2 (over y_lo), rows: 128 (over y_hi, z, x, core).
Axes of the slice: x: 4, y: 4 (y_hi: 2, y_lo: 2; y = y_hi * 2 + y_lo), z: 8, core: 2. Of those that a mesh axis runs over, the one named last changes fastest.
Arguments:
- embeds: bfloat16 [2, 16384, 768], P('group', 'rows'), may hold values from -8 to 8
- weights: bfloat16 [2, 768, 768], P('group', 'rows'), may hold values from -0.3 to 1.3
- pair_index: int32 [16384], replicated, may hold values from 0 to 16383, as said below
- scale: float32 [1], replicated, may hold values from 12 to 28
Outputs:
- embed_grad: bfloat16 [2, 16384, 768], P('group', 'rows')
- weight_grad: float32 [2, 768, 768], P('group', 'rows')
Inputs may be any that keep to these rules, and one draw needn't show every extreme that they name: `pair_index`: a permutation of the 16384 rows.
All inputs are finite; a program needn't handle non-finite values.
Results may differ from a plain program's by a relative error of at most 0.0062.
Values may be sent and summed in bfloat16 or wider, within the bound.
No kernel may reach another device: no remote copies, remote signals or barrier semaphores. Data moves between devices by JAX's collectives and lax.ppermute only.
A program may use at most 128 MiB of HBM per device.

v0:
```python
import jax
import jax.numpy as jnp
from jax import lax
from jax.experimental import pallas as pl
from jax.experimental.pallas import tpu as pltpu
from jax.sharding import Mesh, PartitionSpec as P

EPS = 1e-06
AXES = ("yl", "yh", "z", "x", "c")
SIZES = {"yl": 2, "yh": 2, "z": 8, "x": 4, "c": 2}
ROWS = ("yh", "z", "x", "c")
PLANE = ("yl", "yh", "x")
Y = ("yl", "yh")
F32 = jnp.float32
BF16 = jnp.bfloat16
LIMIT = 56 << 20
MEET = (0, 1, -1, -2, 2, 3, -3, -4)


def count(axes):
    total = 1
    for name in axes:
        total *= SIZES[name]
    return total


def mirror(value, axes, mask=1):
    return lax.ppermute(value, axes, [(i, i ^ mask) for i in range(count(axes))])


def pair(value, step):
    size = SIZES["z"]
    route = []
    for i in range(size):
        for core in range(2):
            kind = (core + step) % 2
            other = (((i + kind) ^ 1) - kind) % size
            route.append((2 * i + core, 2 * other + core))
    return lax.ppermute(value, ("z", "c"), route)


def meets(z, core):
    sign = 1 - 2 * ((z + core) & 1)
    return [(z + sign * step) & 7 for step in MEET]


def gather(value, axes):
    copies = jnp.broadcast_to(value[None], (count(axes),) + value.shape)
    return lax.all_to_all(copies, axes, 0, 0)


def stage(*values):
    return lax.optimization_barrier(values)


def wider(value):
    return value.astype(F32)


def column(row):
    return jnp.transpose(jnp.broadcast_to(row, (128, row.shape[1])))[:, :1]


def line(values):
    return jnp.transpose(jnp.broadcast_to(values, (values.shape[0], 128)))[:1]


def mover(sems):
    used = []

    def move(source, target):
        copy = pltpu.make_async_copy(source, target, sems.at[len(used)])
        used.append(copy)
        copy.start()
        return copy

    return move


def arrive(copies):
    for copy in copies:
        copy.wait()


def fill(tile, values, first):
    for k in range(values.shape[1] // 128):
        tile[first + k : first + k + 1, :] = values[:, k * 128 : (k + 1) * 128]


def spread(tile):
    return jnp.concatenate([tile[k : k + 1, :] for k in range(tile.shape[0])], axis=1)


def score_kernel(at, scale, h_img, *refs):
    met = [refs[:4], refs[4:8]]
    (
        row_sum, col_sum, inv_img, inv_mod, o_mod, o_low_img, o_low_mod, o_res_img, o_res_mod, o_power,
        o_weight,
        x_img, x_mod, w_img, w_mod, low_img, low_mod, res_img, res_mod, power, sems,
    ) = refs[8:]
    core, z, side = at[0], at[1], at[4]
    half, width = x_img.shape[1], x_img.shape[2]
    band = w_img.shape[2]
    block = 2 * band + half
    size = 4 * half
    move = mover(sems)

    modal, image = [], []
    for want in range(2):
        for own in range(2):
            c = core if own == 0 else 1 - core
            for i, k in enumerate(meets(z, c)):
                piece, start = met[own][i // 2], (i % 2) * block
                if want == 0:
                    modal.append(move(piece.at[pl.ds(start + band, band)], w_mod.at[c, k]))
                    modal.append(move(piece.at[pl.ds(start + 2 * band, half)], x_mod.at[c * 8 + k]))
                else:
                    image.append(move(piece.at[pl.ds(start, band)], w_img.at[c, k]))
    image.append(move(h_img, x_img))

    going = []
    for rows, w, low, rest, inverse, to, needs in (
        (x_mod, w_mod, low_mod, res_mod, inv_mod, (o_low_mod, o_res_mod), modal),
        (x_img, w_img, low_img, res_img, inv_img, (o_low_img, o_res_img), image),
    ):
        arrive(needs)
        if rows is x_mod:
            going.append(move(x_mod, o_mod))
        for i in range(4):
            take = slice(i * size, (i + 1) * size)
            proj = jnp.dot(
                rows[4 * i : 4 * i + 4].reshape(size, width),
                w[...].reshape(width, width),
                preferred_element_type=F32,
            )
            inv = lax.rsqrt(jnp.sum(proj * proj, axis=1, keepdims=True) + EPS)
            proj = proj * inv
            head = proj.astype(BF16)
            low[take] = head
            rest[take] = (proj - wider(head)).astype(BF16)
            inverse[:, take] = line(inv)
        going += [move(low, to[0]), move(rest, to[1])]

    own = sems.at[sems.shape[0] - 1]

    @pl.when(side == 0)
    def _():
        pltpu.make_async_copy(w_img, o_weight, own).start()

    @pl.when(side == 1)
    def _():
        pltpu.make_async_copy(w_mod, o_weight, own).start()

    factor = scale[0]
    cols = None
    for i in range(4):
        take = slice(i * size, (i + 1) * size)
        scores = lax.dot_general(
            low_img[take], low_mod[...], (((1,), (1,)), ((), ())), preferred_element_type=F32
        )
        value = jnp.exp(factor * scores)
        power[take] = value
        going.append(move(power.at[take], o_power.at[take]))
        fill(row_sum, line(jnp.sum(value, axis=1, keepdims=True)), i * size // 128)
        part = jnp.sum(value, axis=0, keepdims=True)
        cols = part if cols is None else cols + part
    fill(col_sum, cols, 0)
    arrive(going)
    pltpu.make_async_copy(w_img, o_weight, own).wait()


def gradient_kernel(
    at, scale, row_sum, row_came, col_sum, col_came, partner, inv_img, inv_mod,
    h_power, h_img, h_mod, h_low_img, h_low_mod, h_res_img, h_res_mod,
    o_img, o_keep, o_send,
    power, x_img, x_mod, low_img, low_mod, res_img, res_mod,
    weight_row, p_img, p_mod, keep, send, sems,
):
    core, z, y, x, side = [at[i] for i in range(5)]
    half, width = x_img.shape[1], x_img.shape[2]
    wide, band = width // 2, width // 16
    size = 4 * half
    factor = scale[0]
    move = mover(sems)
    parts = [slice(i * size, (i + 1) * size) for i in range(4)]

    def load(i):
        pairs = ((h_power, power), (h_low_img, low_img), (h_res_img, res_img))
        return [move(source.at[parts[i]], target.at[parts[i]]) for source, target in pairs]

    first = move(h_power.at[parts[0]], power.at[parts[0]])
    low = move(h_low_mod, low_mod)
    needs = [
        move(h_low_img.at[parts[0]], low_img.at[parts[0]]),
        move(h_res_img.at[parts[0]], res_img.at[parts[0]]),
    ]
    loads = [load(1)]

    j = lax.broadcasted_iota(jnp.int32, (1, 16 * half), 1)
    jz, jc, jr = (j // half) & 7, j // (8 * half), j & (half - 1)
    ids = ((((y // 2) * 8 + jz) * 4 + x) * 2 + jc) * (2 * half) + side * half + jr
    col = 1.0 / spread(col_sum[...] + col_came[...])
    row = 1.0 / spread(row_sum[...] + row_came[...])

    def weigh(i):
        take = parts[i]
        hit = column(partner[:, take]) == ids
        value = power[take] * (column(row[:, take]) + col)
        weight_row[take] = (value - jnp.where(hit, 2.0, 0.0)).astype(BF16)

    def tangent(grad, low, rest, inv):
        unit = wider(low) + wider(rest)
        along = jnp.sum(grad * unit, axis=1, keepdims=True)
        return (column(factor * inv) * (grad - unit * along)).astype(BF16).reshape(4, half, width)

    arrive([first])
    weigh(0)
    arrive([low] + needs)
    for i, take in enumerate(parts):
        if i < 2:
            loads.append(load(i + 2))
        if i == 2:
            modal = [move(h_res_mod, res_mod)]
            rest = [move(h_img, x_img), move(h_mod, x_mod)]
        if i < 3:
            arrive(loads[i])
        grad = jnp.dot(weight_row[take], low_mod[...], preferred_element_type=F32)
        if i < 3:
            weigh(i + 1)
        p_img[4 * i : 4 * i + 4] = tangent(grad, low_img[take], res_img[take], inv_img[:, take])
    going = [move(p_img, o_img)]
    arrive(modal)
    for i, take in enumerate(parts):
        grad = lax.dot_general(
            weight_row[:, take], low_img[...], (((0,), (0,)), ((), ())), preferred_element_type=F32
        )
        p_mod[4 * i : 4 * i + 4] = tangent(grad, low_mod[take], res_mod[take], inv_mod[:, take])
    for c, target in ((core, keep), (1 - core, send)):
        for i, k in enumerate(meets(z, c)):
            target[i, 2 * band :] = p_mod[c * 8 + k]
    arrive(rest)
    for s, (rows, p) in enumerate(((x_img, p_img), (x_mod, p_mod))):
        lines = slice(s * band, (s + 1) * band)
        for c in range(2):
            grad = lax.dot_general(
                rows[:, :, c * wide : (c + 1) * wide].reshape(16 * half, wide),
                p[...].reshape(16 * half, width),
                (((0,), (0,)), ((), ())),
                preferred_element_type=F32,
            ).astype(BF16)
            sign = 1 - 2 * ((z + c) & 1)

            def put(target):
                for k in range(8):
                    step = (sign * (k - z)) & 7
                    spot = jnp.where(step < 2, step, jnp.where(step < 4, step + 2, 9 - step))
                    spot = jnp.where(step == 4, 7, jnp.where(step == 5, 6, spot))
                    target[spot, lines] = grad[k * band : (k + 1) * band]

            @pl.when(core == c)
            def _():
                put(keep)

            @pl.when(core != c)
            def _():
                put(send)

        if s == 0:
            first, last = pl.ds(0, band), pl.ds(2 * band, half)
            for source, target in ((keep, o_keep), (send, o_send)):
                for lines in (first, last):
                    going.append(move(source.at[pl.ds(0, 8), lines], target.at[pl.ds(0, 8), lines]))
        else:
            lines = pl.ds(band, band)
            for source, target in ((keep, o_keep), (send, o_send)):
                going.append(move(source.at[pl.ds(0, 8), lines], target.at[pl.ds(0, 8), lines]))
    arrive(going)


def call(kernel, at, scale, operands, out, scratch, flops):
    spaces = {False: pl.BlockSpec(memory_space=pltpu.VMEM), True: pl.BlockSpec(memory_space=pl.ANY)}
    smem = pl.BlockSpec(memory_space=pltpu.SMEM)
    return pl.pallas_call(
        kernel,
        in_specs=[smem, smem] + [spaces[own] for _, own in operands],
        out_specs=[spaces[own] for _, own in out],
        out_shape=[jax.ShapeDtypeStruct(*one) for one, _ in out],
        scratch_shapes=[pltpu.VMEM(*one) for one in scratch] + [pltpu.SemaphoreType.DMA((96,))],
        compiler_params=pltpu.CompilerParams(vmem_limit_bytes=LIMIT),
        cost_estimate=pl.CostEstimate(flops=flops, bytes_accessed=8 << 20, transcendentals=0),
    )(at, scale, *[one for one, _ in operands])


def here_first(values, own):
    return [(one, own) for one in values]


def reorder(width):
    r = width // 128
    k = jnp.arange(width)
    low, c, x, z, yh = k % r, (k // r) % 2, (k // (2 * r)) % 4, (k // (8 * r)) % 8, k // (64 * r)
    to = (((c * 8 + z) * 2 + yh) * 4 + x) * r + low
    return (to[:, None] == k[None, :]).astype(BF16)


def per_device(embeds, weights, pair_index, scale):
    side = lax.axis_index("yl")
    yh, z, x, core = [lax.axis_index(name) for name in ROWS]
    at = jnp.stack([core, z, yh * 2 + side, x, side]).astype(jnp.int32)
    own, shard = embeds[0], weights[0]
    here, width = own.shape
    half, band, size = here // 2, 8 * shard.shape[0], 8 * here

    w0 = gather(shard, PLANE).reshape(2 * band, width)
    own = jnp.dot(own, reorder(width), preferred_element_type=F32).astype(BF16)

    keep = lax.dynamic_slice_in_dim(own, side * half, half, 0)
    send = lax.dynamic_slice_in_dim(own, (1 - side) * half, half, 0)
    came = mirror(send, ("yl",))
    image_x = jnp.where(side == 0, keep, came)
    modal_x = jnp.where(side == 0, came, keep)

    copies = jnp.broadcast_to(image_x[None], (16, half, width))
    near = [jnp.concatenate([w0, modal_x])]
    near = [jnp.concatenate([near[0], pair(near[0], 0)])]
    far = [mirror(near[0], ("c",))]
    for step in (1, 2, 3):
        near.append(pair(near[-1], step))
        far.append(mirror(near[-1], ("c",)))
    image_x = lax.all_to_all(copies, PLANE, 0, 0)
    pieces = [image_x, *near, *far]

    table = pair_index.reshape(2, 8, 4, 2, 2, half)
    table = lax.dynamic_index_in_dim(table, z, 1, False)
    table = lax.dynamic_index_in_dim(table, core, 2, False)
    partner = table.transpose(2, 0, 1, 3).reshape(1, size)

    rows, flat = ((16, half, width), BF16), ((size, width), BF16)
    tile, one_line, square = ((8, size // 8), F32), ((1, size), F32), ((size, size), F32)
    some = ((2, 8, band, width), BF16)
    row_sum, col_sum, inv_img, inv_mod, x_mod, low_img, low_mod, res_img, res_mod, power, weight = call(
        score_kernel,
        at,
        scale,
        here_first(pieces, True),
        here_first([tile, tile, one_line, one_line], False) + here_first([rows, flat, flat, flat, flat, square, some], True),
        [rows, rows, some, some, flat, flat, flat, flat, square],
        4 * size * width * width + 2 * size * size * width,
    )
    def exchange(row_sum, col_sum, step):
        axes, mask = ((("x",), 1), (("x",), 3), (Y, 2), (Y, 3))[step]
        if step == 0:
            came = mirror(col_sum, ("c",))
        elif step == 3:
            came = mirror(col_sum, ("z",), 4)
        else:
            came = pair(col_sum, step)
        return stage(mirror(row_sum, axes, mask), came)

    for step in range(3):
        row_came, col_came = exchange(row_sum, col_sum, step)
        row_sum, col_sum = row_sum + row_came, col_sum + col_came
    row_came, col_came = exchange(row_sum, col_sum, 3)

    block = (8, 2 * band + half, width)
    d_image, keep, send = call(
        gradient_kernel,
        at,
        scale,
        here_first([row_sum, row_came, col_sum, col_came, partner, inv_img, inv_mod], False)
        + here_first([power, image_x, x_mod, low_img, low_mod, res_img, res_mod], True),
        here_first([rows, (block, BF16), (block, BF16)], True),
        [square, rows, rows, flat, flat, flat, flat, ((size, size), BF16), rows, rows]
        + [(block, BF16), (block, BF16)],
        4 * size * width * width + 4 * size * size * width,
    )
    d_image = jnp.sum(wider(lax.all_to_all(d_image, PLANE, 0, 0)), axis=0)
    send = mirror(send, ("c",))
    mine = wider(keep[6:]) + wider(send[6:])
    for step, first in ((1, 4), (0, 2), (1, 0)):
        came = pair(mine.astype(BF16), step)
        mine = wider(keep[first : first + 2]) + wider(send[first : first + 2]) + wider(came)
    sums = mine[0] + wider(pair(mine[1].astype(BF16), 0))
    d_modal = sums[2 * band :]
    d_weight = sums[: 2 * band].reshape(16, band // 8, width)
    d_weight = jnp.sum(lax.all_to_all(d_weight, PLANE, 0, 0), axis=0)

    came = mirror(jnp.where(side == 0, d_modal, d_image), ("yl",))
    d_proj = jnp.where(
        side == 0,
        jnp.concatenate([d_image, came]),
        jnp.concatenate([came, d_modal]),
    ).astype(BF16)
    d_inputs = lax.dot_general(
        d_proj, weight.reshape(width, width), (((1,), (1,)), ((), ())), preferred_element_type=F32
    )
    d_inputs = lax.dot_general(
        d_inputs.astype(BF16), reorder(width), (((1,), (1,)), ((), ())), preferred_element_type=F32
    )
    return (d_inputs.astype(BF16)[None], d_weight[None])


def solution(mesh):
    devices = mesh.devices.reshape([SIZES[name] for name in AXES])
    return jax.shard_map(
        per_device,
        mesh=Mesh(devices, AXES),
        in_specs=(P("yl", ROWS, None), P("yl", ROWS, None), P(), P()),
        out_specs=(P("yl", ROWS, None), P("yl", ROWS, None)),
        check_vma=False,
    )
```

profile of v0, /device:TPU:2, one launch (start us, length us, event | category | flops | bytes accessed | tf_op | source)
XLA Modules:
  0.0 174.3 jit_solution(7005121062334380848)
XLA Ops:
  0.7 0.9 copy-done
  1.6 0.6 fusion.4
  2.2 1.7 collective-permute-start
  3.9 1.4 broadcast_in_dim.12
  5.3 7.2 %all-to-all-start.1 = ((bf16[16,6,768]{2,1,0:T(8,128)(2,1)}), bf16[16,6,768]{2,1,0:T(8,128)(2,1)S(1)}, u32[]{:S(2)}, u32[]{:S(2)}) async-start(bf16[16,6,768]{2,1,0:T(8,128)(2,1)} %broadcast_in_dim.12), calls=%async_computation.1 | async-start | bytes 393216 | tf_op jit(solution)/shard_map/all_to_all | solution.py:49
  12.5 6.9 %all-to-all-done.1 = bf16[16,6,768]{2,1,0:T(8,128)(2,1)S(1)} async-done(((bf16[16,6,768]{2,1,0:T(8,128)(2,1)}), bf16[16,6,768]{2,1,0:T(8,128)(2,1)S(1)}, u32[]{:S(2)}, u32[]{:S(2)}) %all-to-all-start.1) | async-done | bytes 147488 | tf_op jit(solution)/shard_map/all_to_all | solution.py:49
  19.5 2.0 %collective-permute-start.1 = (bf16[160,768]{1,0:T(8,128)(2,1)S(1)}, bf16[160,768]{1,0:T(8,128)(2,1)S(1)}, u32[]{:S(2)}, u32[]{:S(2)}) collective-permute-start(bf16[160,768]{1,0:T(8,128)(2,1)S(1)} %pad_maximum_fusion.1), channel_id=1, source_target_pairs={{0,8},{1,57},{8,0},{9,17},{16,24},{17,9},{24,16},{25,33},{32,40},{... | collective-permute-start | bytes 737288 | tf_op jit(solution)/shard_map/ppermute | solution.py:39
  21.5 4.3 %collective-permute-done.1 = bf16[160,768]{1,0:T(8,128)(2,1)S(1)} collective-permute-done((bf16[160,768]{1,0:T(8,128)(2,1)S(1)}, bf16[160,768]{1,0:T(8,128)(2,1)S(1)}, u32[]{:S(2)}, u32[]{:S(2)}) %collective-permute-start.1) | collective-permute-done | bytes 245792 | tf_op jit(solution)/shard_map/ppermute | solution.py:39
  25.8 5.9 %collective-permute-start.2 = (bf16[320,768]{1,0:T(8,128)(2,1)S(1)}, bf16[320,768]{1,0:T(8,128)(2,1)S(1)}, u32[]{:S(2)}, u32[]{:S(2)}) collective-permute-start(bf16[320,768]{1,0:T(8,128)(2,1)S(1)} %pad_maximum_fusion.refs_0_), channel_id=1, source_target_pairs={{0,56},{1,9},{8,16},{9,1},{16,8},{17,25},{24,32},{25,17},{32,24},{... | collective-permute-start | bytes 1474568 | tf_op jit(solution)/shard_map/ppermute | solution.py:39
  31.8 1.3 broadcast_in_dim.10
  33.1 5.0 %all-to-all-start = ((bf16[16,64,768]{2,1,0:T(8,128)(2,1)}), bf16[16,64,768]{2,1,0:T(8,128)(2,1)S(1)}, u32[]{:S(2)}, u32[]{:S(2)}) async-start(bf16[16,64,768]{2,1,0:T(8,128)(2,1)} %broadcast_in_dim.10), calls=%async_computation | async-start | bytes 3145728 | tf_op jit(solution)/shard_map/all_to_all | solution.py:330
  38.6 9.4 %collective-permute-done.3.refs_2_ = bf16[320,768]{1,0:T(8,128)(2,1)S(1)} collective-permute-done((bf16[320,768]{1,0:T(8,128)(2,1)S(1)}, bf16[320,768]{1,0:T(8,128)(2,1)S(1)}, u32[]{:S(2)}, u32[]{:S(2)}) %collective-permute-start.3) | collective-permute-done | bytes 491552 | tf_op jit(solution)/shard_map/ppermute | solution.py:39
  48.0 3.5 %collective-permute-start.4 = (bf16[320,768]{1,0:T(8,128)(2,1)S(1)}, bf16[320,768]{1,0:T(8,128)(2,1)}, u32[]{:S(2)}, u32[]{:S(2)}) collective-permute-start(bf16[320,768]{1,0:T(8,128)(2,1)S(1)} %collective-permute-done.3.refs_2_), channel_id=1, source_target_pairs={{0,56},{1,9},{8,16},{9,1},{16,8},{17,25},{24,32},{25,17},{32,24},{... | collective-permute-start | bytes 1474568 | tf_op jit(solution)/shard_map/ppermute | solution.py:39
  52.0 6.4 %collective-permute-done.4.refs_3_ = bf16[320,768]{1,0:T(8,128)(2,1)} collective-permute-done((bf16[320,768]{1,0:T(8,128)(2,1)S(1)}, bf16[320,768]{1,0:T(8,128)(2,1)}, u32[]{:S(2)}, u32[]{:S(2)}) %collective-permute-start.4) | collective-permute-done | bytes 491552 | tf_op jit(solution)/shard_map/ppermute | solution.py:39
  59.0 0.6 stack.23.at
  59.7 0.9 collective-permute-done.8.refs_7_
  60.8 10.5 %shard_map.59 = (f32[8,128]{1,0:T(8,128)}, f32[8,128]{1,0:T(8,128)}, f32[1,1024]{1,0:T(1,128)}, f32[1,1024]{1,0:T(1,128)}, bf16[16,64,768]{2,1,0:T(8,128)(2,1)},...) custom-call(s32[5]{0:T(128)} %stack.23.at, ...), custom_call_target="tpu_custom_call" | custom-call | flops 4026531840 | bytes 8388608 | tf_op jit(solution)/shard_map/pallas_call | solution.py:283
  71.4 1.6 collective-permute-start.9
  73.1 2.1 %collective-permute-done.9 = f32[8,128]{1,0:T(8,128)S(1)} collective-permute-done((f32[8,128]{1,0:T(8,128)}, f32[8,128]{1,0:T(8,128)S(1)}, u32[]{:S(2)}, u32[]{:S(2)}) %collective-permute-start.9) | collective-permute-done | bytes 4128 | tf_op jit(solution)/shard_map/ppermute | solution.py:28
  75.3 0.7 add.186
  76.0 0.7 add.187
  76.7 3.2 %collective-permute-start.12 = (f32[8,128]{1,0:T(8,128)S(1)}, f32[8,128]{1,0:T(8,128)S(1)}, u32[]{:S(2)}, u32[]{:S(2)}) collective-permute-start(f32[8,128]{1,0:T(8,128)S(1)} %add.187), channel_id=1, source_target_pairs={{0,56},{1,9},{8,16},{9,1},{16,8},{17,25},{24,32},{25,17},{32,24},{... | collective-permute-start | bytes 12296 | tf_op jit(solution)/shard_map/ppermute | solution.py:39
  80.5 1.0 collective-permute-done.12
  81.5 2.0 %collective-permute-done.11 = f32[8,128]{1,0:T(8,128)S(1)} collective-permute-done((f32[8,128]{1,0:T(8,128)S(1)}, f32[8,128]{1,0:T(8,128)S(1)}, u32[]{:S(2)}, u32[]{:S(2)}) %collective-permute-start.11) | collective-permute-done | bytes 4128 | tf_op jit(solution)/shard_map/ppermute | solution.py:28
  83.9 3.2 %collective-permute-done.14 = f32[8,128]{1,0:T(8,128)S(1)} collective-permute-done((f32[8,128]{1,0:T(8,128)S(1)}, f32[8,128]{1,0:T(8,128)S(1)}, u32[]{:S(2)}, u32[]{:S(2)}) %collective-permute-start.14) | collective-permute-done | bytes 4128 | tf_op jit(solution)/shard_map/ppermute | solution.py:39
  87.2 2.7 %collective-permute-start.16 = (f32[8,128]{1,0:T(8,128)S(1)}, f32[8,128]{1,0:T(8,128)S(1)}, u32[]{:S(2)}, u32[]{:S(2)}) collective-permute-start(f32[8,128]{1,0:T(8,128)S(1)} %add.191.col_sum), channel_id=1, source_target_pairs={{0,32},{8,40},{16,48},{24,56},{32,0},{40,8},{48,16},{56,24},{1,33}... | collective-permute-start | bytes 12296 | tf_op jit(solution)/shard_map/ppermute | solution.py:28
  90.0 1.7 collective-permute-start.15
  91.7 0.7 reshape.107.partner
  92.4 2.5 %collective-permute-done.16.col_came = f32[8,128]{1,0:T(8,128)S(1)} collective-permute-done((f32[8,128]{1,0:T(8,128)S(1)}, f32[8,128]{1,0:T(8,128)S(1)}, u32[]{:S(2)}, u32[]{:S(2)}) %collective-permute-start.16) | collective-permute-done | bytes 4128 | tf_op jit(solution)/shard_map/ppermute | solution.py:28
  95.4 15.0 %shard_map.60 = (bf16[16,64,768]{2,1,0:T(8,128)(2,1)}, bf16[8,160,768]{2,1,0:T(8,128)(2,1)}, bf16[8,160,768]{2,1,0:T(8,128)(2,1)}) custom-call(s32[5]{0:T(128)} %stack.23.at, f32[1]{0:T(128)S(6)} %copy.7.scale, f32[8,128]{1,0:T(8,128)} %copy-done.5, f32[8,128]{1,0:T(8,128)} %copy-done.10, f32[8,128]{1,0:T(8,128)} %copy-done.6, f32[8,128]{1,0:T(8,128)} %copy-done.9, ...), custom_call_target="tpu_custom_call" | custom-call | flops 5637144576 | bytes 8388608 | tf_op jit(solution)/shard_map/pallas_call | solution.py:283
  110.7 4.2 %collective-permute-done.17 = bf16[8,160,768]{2,1,0:T(8,128)(2,1)S(1)} collective-permute-done((bf16[8,160,768]{2,1,0:T(8,128)(2,1)}, bf16[8,160,768]{2,1,0:T(8,128)(2,1)S(1)}, u32[]{:S(2)}, u32[]{:S(2)}) %collective-permute-start.17) | collective-permute-done | bytes 1966112 | tf_op jit(solution)/shard_map/ppermute | solution.py:28
  114.9 1.5 add_convert_fusion.2
  116.4 1.9 %collective-permute-start.18 = (bf16[2,160,768]{2,1,0:T(8,128)(2,1)S(1)}, bf16[2,160,768]{2,1,0:T(8,128)(2,1)S(1)}, u32[]{:S(2)}, u32[]{:S(2)}) collective-permute-start(bf16[2,160,768]{2,1,0:T(8,128)(2,1)S(1)} %add_convert_fusion.2), channel_id=1, source_target_pairs={{0,56},{1,9},{8,16},{9,1},{16,8},{17,25},{24,32},{25,17},{32,24},{... | collective-permute-start | bytes 1474568 | tf_op jit(solution)/shard_map/ppermute | solution.py:39
  118.3 8.2 %collective-permute-done.18 = bf16[2,160,768]{2,1,0:T(8,128)(2,1)S(1)} collective-permute-done((bf16[2,160,768]{2,1,0:T(8,128)(2,1)S(1)}, bf16[2,160,768]{2,1,0:T(8,128)(2,1)S(1)}, u32[]{:S(2)}, u32[]{:S(2)}) %collective-permute-start.18) | collective-permute-done | bytes 491552 | tf_op jit(solution)/shard_map/ppermute | solution.py:39
  126.5 1.2 add_convert_fusion.1
  127.7 0.8 collective-permute-start.19
  128.6 7.4 %all-to-all-start.2 = ((bf16[16,64,768]{2,1,0:T(8,128)(2,1)}), bf16[16,64,768]{2,1,0:T(8,128)(2,1)S(1)}, u32[]{:S(2)}, u32[]{:S(2)}) async-start(bf16[16,64,768]{2,1,0:T(8,128)(2,1)} %get-tuple-element.42), calls=%async_computation.2 | async-start | bytes 3145728 | tf_op jit(solution)/shard_map/all_to_all | solution.py:377
  136.0 0.7 collective-permute-done.19
  136.7 1.4 add_convert_fusion
  138.0 1.9 %collective-permute-start.20 = (bf16[2,160,768]{2,1,0:T(8,128)(2,1)S(1)}, bf16[2,160,768]{2,1,0:T(8,128)(2,1)S(1)}, u32[]{:S(2)}, u32[]{:S(2)}) collective-permute-start(bf16[2,160,768]{2,1,0:T(8,128)(2,1)S(1)} %add_convert_fusion), channel_id=1, source_target_pairs={{0,56},{1,9},{8,16},{9,1},{16,8},{17,25},{24,32},{25,17},{32,24},{... | collective-permute-start | bytes 1474568 | tf_op jit(solution)/shard_map/ppermute | solution.py:39
  140.0 8.2 %collective-permute-done.20 = bf16[2,160,768]{2,1,0:T(8,128)(2,1)S(1)} collective-permute-done((bf16[2,160,768]{2,1,0:T(8,128)(2,1)S(1)}, bf16[2,160,768]{2,1,0:T(8,128)(2,1)S(1)}, u32[]{:S(2)}, u32[]{:S(2)}) %collective-permute-start.20) | collective-permute-done | bytes 491552 | tf_op jit(solution)/shard_map/ppermute | solution.py:39
  148.2 1.3 convert_add_fusion
  149.6 6.9 %all-to-all-done.2 = bf16[16,64,768]{2,1,0:T(8,128)(2,1)S(1)} async-done(((bf16[16,64,768]{2,1,0:T(8,128)(2,1)}), bf16[16,64,768]{2,1,0:T(8,128)(2,1)S(1)}, u32[]{:S(2)}, u32[]{:S(2)}) %all-to-all-start.2) | async-done | bytes 1572896 | tf_op jit(solution)/shard_map/all_to_all | solution.py:377
  157.3 0.8 reshape.109
  158.1 7.6 %all-to-all-start.3 = ((f32[16,6,768]{2,1,0:T(8,128)}), f32[16,6,768]{2,1,0:T(8,128)S(1)}, u32[]{:S(2)}, u32[]{:S(2)}) async-start(f32[16,6,768]{2,1,0:T(8,128)} %reshape.109), calls=%async_computation.3 | async-start | bytes 786432 | tf_op jit(solution)/shard_map/all_to_all | solution.py:386
  165.6 2.9 %fusion.6 = bf16[1,128,768]{2,1,0:T(8,128)(2,1)} fusion(s32[768]{0:T(1024)S(1)} %fusion.25, bf16[768,768]{1,0:T(8,128)(2,1)} %bitcast.29, bf16[64,768]{1,0:T(8,128)(2,1)S(1)} %collective-permute-done.22, bf16[64,768]{1,0:T(8,128)(2,1)S(1)} %convert_reduce_fusion, bf16[64,768]{1,0:T(8,128)(2,1)S(1)} %get-tuple-element.46, pred[]{:T(512)S(6)} %eq.41), kind=kOutput, calls=%fused_computation.9 | convolution fusion | flops 303661056 | bytes 1674241 | tf_op jit(solution)/shard_map/dot_general | solution.py:397
  168.6 5.1 %all-to-all-done.3 = f32[16,6,768]{2,1,0:T(8,128)S(1)} async-done(((f32[16,6,768]{2,1,0:T(8,128)}), f32[16,6,768]{2,1,0:T(8,128)S(1)}, u32[]{:S(2)}, u32[]{:S(2)}) %all-to-all-start.3) | async-done | bytes 294944 | tf_op jit(solution)/shard_map/all_to_all | solution.py:386
  173.7 0.6 broadcast_in_dim.27
  (63 shorter events, 4.7 us)
Async XLA Ops:
  0.6 0.9 copy-start
  2.2 10.2 %collective-permute-start = (bf16[64,768]{1,0:T(8,128)(2,1)S(1)}, bf16[64,768]{1,0:T(8,128)(2,1)S(1)}, u32[]{:S(2)}, u32[]{:S(2)}) collective-permute-start(bf16[64,768]{1,0:T(8,128)(2,1)S(1)} %dynamic-slice_bitcast_fusion), channel_id=1, source_target_pairs={{0,128},{128,0},{1,129},{129,1},{2,130},{130,2},{3,131},{131,3},{4... | collective-permute-start | bytes 294920 | tf_op jit(solution)/shard_map/ppermute | solution.py:28
  5.3 14.2 %all-to-all-start.1 = ((bf16[16,6,768]{2,1,0:T(8,128)(2,1)}), bf16[16,6,768]{2,1,0:T(8,128)(2,1)S(1)}, u32[]{:S(2)}, u32[]{:S(2)}) async-start(bf16[16,6,768]{2,1,0:T(8,128)(2,1)} %broadcast_in_dim.12), calls=%async_computation.1 | async-start | bytes 393216 | tf_op jit(solution)/shard_map/all_to_all | solution.py:49
  19.5 6.3 %collective-permute-start.1 = (bf16[160,768]{1,0:T(8,128)(2,1)S(1)}, bf16[160,768]{1,0:T(8,128)(2,1)S(1)}, u32[]{:S(2)}, u32[]{:S(2)}) collective-permute-start(bf16[160,768]{1,0:T(8,128)(2,1)S(1)} %pad_maximum_fusion.1), channel_id=1, source_target_pairs={{0,8},{1,57},{8,0},{9,17},{16,24},{17,9},{24,16},{25,33},{32,40},{... | collective-permute-start | bytes 737288 | tf_op jit(solution)/shard_map/ppermute | solution.py:39
  25.8 25.6 %copy-start.3 = (bf16[320,768]{1,0:T(8,128)(2,1)}, bf16[320,768]{1,0:T(8,128)(2,1)S(1)}, u32[]{:S(2)}) copy-start(bf16[320,768]{1,0:T(8,128)(2,1)S(1)} %pad_maximum_fusion.refs_0_) | copy-start | bytes 1474564
  25.8 12.8 %collective-permute-start.2 = (bf16[320,768]{1,0:T(8,128)(2,1)S(1)}, bf16[320,768]{1,0:T(8,128)(2,1)S(1)}, u32[]{:S(2)}, u32[]{:S(2)}) collective-permute-start(bf16[320,768]{1,0:T(8,128)(2,1)S(1)} %pad_maximum_fusion.refs_0_), channel_id=1, source_target_pairs={{0,56},{1,9},{8,16},{9,1},{16,8},{17,25},{24,32},{25,17},{32,24},{... | collective-permute-start | bytes 1474568 | tf_op jit(solution)/shard_map/ppermute | solution.py:39
  33.1 26.5 %all-to-all-start = ((bf16[16,64,768]{2,1,0:T(8,128)(2,1)}), bf16[16,64,768]{2,1,0:T(8,128)(2,1)S(1)}, u32[]{:S(2)}, u32[]{:S(2)}) async-start(bf16[16,64,768]{2,1,0:T(8,128)(2,1)} %broadcast_in_dim.10), calls=%async_computation | async-start | bytes 3145728 | tf_op jit(solution)/shard_map/all_to_all | solution.py:330
  38.6 22.0 %copy-start.7 = (bf16[320,768]{1,0:T(8,128)(2,1)}, bf16[320,768]{1,0:T(8,128)(2,1)S(1)}, u32[]{:S(2)}) copy-start(bf16[320,768]{1,0:T(8,128)(2,1)S(1)} %collective-permute-done.2.refs_1_) | copy-start | bytes 1474564
  38.6 9.4 %collective-permute-start.3 = (bf16[320,768]{1,0:T(8,128)(2,1)S(1)}, bf16[320,768]{1,0:T(8,128)(2,1)S(1)}, u32[]{:S(2)}, u32[]{:S(2)}) collective-permute-start(bf16[320,768]{1,0:T(8,128)(2,1)S(1)} %collective-permute-done.2.refs_1_), channel_id=1, source_target_pairs={{0,8},{1,57},{8,0},{9,17},{16,24},{17,9},{24,16},{25,33},{32,40},{... | collective-permute-start | bytes 1474568 | tf_op jit(solution)/shard_map/ppermute | solution.py:39
  48.0 12.6 %copy-start.8 = (bf16[320,768]{1,0:T(8,128)(2,1)}, bf16[320,768]{1,0:T(8,128)(2,1)S(1)}, u32[]{:S(2)}) copy-start(bf16[320,768]{1,0:T(8,128)(2,1)S(1)} %collective-permute-done.3.refs_2_) | copy-start | bytes 1474564
  48.0 10.4 %collective-permute-start.4 = (bf16[320,768]{1,0:T(8,128)(2,1)S(1)}, bf16[320,768]{1,0:T(8,128)(2,1)}, u32[]{:S(2)}, u32[]{:S(2)}) collective-permute-start(bf16[320,768]{1,0:T(8,128)(2,1)S(1)} %collective-permute-done.3.refs_2_), channel_id=1, source_target_pairs={{0,56},{1,9},{8,16},{9,1},{16,8},{17,25},{24,32},{25,17},{32,24},{... | collective-permute-start | bytes 1474568 | tf_op jit(solution)/shard_map/ppermute | solution.py:39
  51.4 8.2 %collective-permute-start.5 = (bf16[320,768]{1,0:T(8,128)(2,1)S(1)}, bf16[320,768]{1,0:T(8,128)(2,1)}, u32[]{:S(2)}, u32[]{:S(2)}) collective-permute-start(bf16[320,768]{1,0:T(8,128)(2,1)S(1)} %pad_maximum_fusion.refs_0_), channel_id=1, source_target_pairs={{0,1},{1,0},{2,3},{3,2},{4,5},{5,4},{6,7},{7,6},{8,9},{9,8},{10,11... | collective-permute-start | bytes 1474568 | tf_op jit(solution)/shard_map/ppermute | solution.py:28
  51.4 8.2 %collective-permute-start.6 = (bf16[320,768]{1,0:T(8,128)(2,1)S(1)}, bf16[320,768]{1,0:T(8,128)(2,1)}, u32[]{:S(2)}, u32[]{:S(2)}) collective-permute-start(bf16[320,768]{1,0:T(8,128)(2,1)S(1)} %collective-permute-done.2.refs_1_), channel_id=1, source_target_pairs={{0,1},{1,0},{2,3},{3,2},{4,5},{5,4},{6,7},{7,6},{8,9},{9,8},{10,11... | collective-permute-start | bytes 1474568 | tf_op jit(solution)/shard_map/ppermute | solution.py:28
  52.0 7.7 %collective-permute-start.7 = (bf16[320,768]{1,0:T(8,128)(2,1)S(1)}, bf16[320,768]{1,0:T(8,128)(2,1)}, u32[]{:S(2)}, u32[]{:S(2)}) collective-permute-start(bf16[320,768]{1,0:T(8,128)(2,1)S(1)} %collective-permute-done.3.refs_2_), channel_id=1, source_target_pairs={{0,1},{1,0},{2,3},{3,2},{4,5},{5,4},{6,7},{7,6},{8,9},{9,8},{10,11... | collective-permute-start | bytes 1474568 | tf_op jit(solution)/shard_map/ppermute | solution.py:28
  58.4 2.2 %collective-permute-start.8 = (bf16[320,768]{1,0:T(8,128)(2,1)}, bf16[320,768]{1,0:T(8,128)(2,1)}, u32[]{:S(2)}, u32[]{:S(2)}) collective-permute-start(bf16[320,768]{1,0:T(8,128)(2,1)} %collective-permute-done.4.refs_3_), channel_id=1, source_target_pairs={{0,1},{1,0},{2,3},{3,2},{4,5},{5,4},{6,7},{7,6},{8,9},{9,8},{10,11... | collective-permute-start | bytes 1474568 | tf_op jit(solution)/shard_map/ppermute | solution.py:28
  59.6 24.1 %copy-start.4 = (s32[16384]{0:T(1024)S(1)}, s32[16384]{0:T(1024)}, u32[]{:S(2)}) copy-start(s32[16384]{0:T(1024)} %param.6) | copy-start | bytes 196612
  59.6 1.2 copy-start.2
  71.4 3.9 %collective-permute-start.9 = (f32[8,128]{1,0:T(8,128)}, f32[8,128]{1,0:T(8,128)S(1)}, u32[]{:S(2)}, u32[]{:S(2)}) collective-permute-start(f32[8,128]{1,0:T(8,128)} %get-tuple-element.24), channel_id=1, source_target_pairs={{0,2},{2,0},{4,6},{6,4},{1,3},{3,1},{5,7},{7,5},{8,10},{10,8},{12,... | collective-permute-start | bytes 12296 | tf_op jit(solution)/shard_map/ppermute | solution.py:28
  72.9 2.3 %collective-permute-start.10 = (f32[8,128]{1,0:T(8,128)}, f32[8,128]{1,0:T(8,128)S(1)}, u32[]{:S(2)}, u32[]{:S(2)}) collective-permute-start(f32[8,128]{1,0:T(8,128)} %get-tuple-element.25), channel_id=1, source_target_pairs={{0,1},{1,0},{2,3},{3,2},{4,5},{5,4},{6,7},{7,6},{8,9},{9,8},{10,11... | collective-permute-start | bytes 12296 | tf_op jit(solution)/shard_map/ppermute | solution.py:28
  76.7 4.8 %collective-permute-start.12 = (f32[8,128]{1,0:T(8,128)S(1)}, f32[8,128]{1,0:T(8,128)S(1)}, u32[]{:S(2)}, u32[]{:S(2)}) collective-permute-start(f32[8,128]{1,0:T(8,128)S(1)} %add.187), channel_id=1, source_target_pairs={{0,56},{1,9},{8,16},{9,1},{16,8},{17,25},{24,32},{25,17},{32,24},{... | collective-permute-start | bytes 12296 | tf_op jit(solution)/shard_map/ppermute | solution.py:39
  79.9 3.6 %collective-permute-start.11 = (f32[8,128]{1,0:T(8,128)S(1)}, f32[8,128]{1,0:T(8,128)S(1)}, u32[]{:S(2)}, u32[]{:S(2)}) collective-permute-start(f32[8,128]{1,0:T(8,128)S(1)} %add.186), channel_id=1, source_target_pairs={{0,6},{2,4},{4,2},{6,0},{1,7},{3,5},{5,3},{7,1},{8,14},{10,12},{12... | collective-permute-start | bytes 12296 | tf_op jit(solution)/shard_map/ppermute | solution.py:28
  83.5 3.6 %collective-permute-start.14 = (f32[8,128]{1,0:T(8,128)S(1)}, f32[8,128]{1,0:T(8,128)S(1)}, u32[]{:S(2)}, u32[]{:S(2)}) collective-permute-start(f32[8,128]{1,0:T(8,128)S(1)} %add.189), channel_id=1, source_target_pairs={{0,8},{1,57},{8,0},{9,17},{16,24},{17,9},{24,16},{25,33},{32,40},{... | collective-permute-start | bytes 12296 | tf_op jit(solution)/shard_map/ppermute | solution.py:39
  83.5 3.7 %collective-permute-start.13 = (f32[8,128]{1,0:T(8,128)S(1)}, f32[8,128]{1,0:T(8,128)S(1)}, u32[]{:S(2)}, u32[]{:S(2)}) collective-permute-start(f32[8,128]{1,0:T(8,128)S(1)} %add.188), channel_id=1, source_target_pairs={{0,128},{64,192},{128,0},{192,64},{1,129},{65,193},{129,1},{193,65... | collective-permute-start | bytes 12296 | tf_op jit(solution)/shard_map/ppermute | solution.py:28
  87.2 7.6 %copy-start.5 = (f32[8,128]{1,0:T(8,128)}, f32[8,128]{1,0:T(8,128)S(1)}, u32[]{:S(2)}) copy-start(f32[8,128]{1,0:T(8,128)S(1)} %add.190.row_sum) | copy-start | bytes 12292
  87.2 7.6 %copy-start.6 = (f32[8,128]{1,0:T(8,128)}, f32[8,128]{1,0:T(8,128)S(1)}, u32[]{:S(2)}) copy-start(f32[8,128]{1,0:T(8,128)S(1)} %add.191.col_sum) | copy-start | bytes 12292
  87.2 7.6 %collective-permute-start.16 = (f32[8,128]{1,0:T(8,128)S(1)}, f32[8,128]{1,0:T(8,128)S(1)}, u32[]{:S(2)}, u32[]{:S(2)}) collective-permute-start(f32[8,128]{1,0:T(8,128)S(1)} %add.191.col_sum), channel_id=1, source_target_pairs={{0,32},{8,40},{16,48},{24,56},{32,0},{40,8},{48,16},{56,24},{1,33}... | collective-permute-start | bytes 12296 | tf_op jit(solution)/shard_map/ppermute | solution.py:28
  90.0 4.9 %collective-permute-start.15 = (f32[8,128]{1,0:T(8,128)S(1)}, f32[8,128]{1,0:T(8,128)S(1)}, u32[]{:S(2)}, u32[]{:S(2)}) collective-permute-start(f32[8,128]{1,0:T(8,128)S(1)} %add.190.row_sum), channel_id=1, source_target_pairs={{0,192},{64,128},{128,64},{192,0},{1,193},{65,129},{129,65},{193,1... | collective-permute-start | bytes 12296 | tf_op jit(solution)/shard_map/ppermute | solution.py:28
  94.8 0.6 copy-start.9
  94.8 0.6 copy-start.10
  110.4 4.5 %collective-permute-start.17 = (bf16[8,160,768]{2,1,0:T(8,128)(2,1)}, bf16[8,160,768]{2,1,0:T(8,128)(2,1)S(1)}, u32[]{:S(2)}, u32[]{:S(2)}) collective-permute-start(bf16[8,160,768]{2,1,0:T(8,128)(2,1)} %get-tuple-element.44), channel_id=1, source_target_pairs={{0,1},{1,0},{2,3},{3,2},{4,5},{5,4},{6,7},{7,6},{8,9},{9,8},{10,11... | collective-permute-start | bytes 5898248 | tf_op jit(solution)/shard_map/ppermute | solution.py:28
  114.9 11.6 %copy-start.1 = (bf16[8,160,768]{2,1,0:T(8,128)(2,1)}, bf16[8,160,768]{2,1,0:T(8,128)(2,1)S(1)}, u32[]{:S(2)}) copy-start(bf16[8,160,768]{2,1,0:T(8,128)(2,1)S(1)} %collective-permute-done.17) | copy-start | bytes 5898244
  116.4 10.1 %collective-permute-start.18 = (bf16[2,160,768]{2,1,0:T(8,128)(2,1)S(1)}, bf16[2,160,768]{2,1,0:T(8,128)(2,1)S(1)}, u32[]{:S(2)}, u32[]{:S(2)}) collective-permute-start(bf16[2,160,768]{2,1,0:T(8,128)(2,1)S(1)} %add_convert_fusion.2), channel_id=1, source_target_pairs={{0,56},{1,9},{8,16},{9,1},{16,8},{17,25},{24,32},{25,17},{32,24},{... | collective-permute-start | bytes 1474568 | tf_op jit(solution)/shard_map/ppermute | solution.py:39
  127.7 8.9 %collective-permute-start.19 = (bf16[2,160,768]{2,1,0:T(8,128)(2,1)S(1)}, bf16[2,160,768]{2,1,0:T(8,128)(2,1)S(1)}, u32[]{:S(2)}, u32[]{:S(2)}) collective-permute-start(bf16[2,160,768]{2,1,0:T(8,128)(2,1)S(1)} %add_convert_fusion.1), channel_id=1, source_target_pairs={{0,8},{1,57},{8,0},{9,17},{16,24},{17,9},{24,16},{25,33},{32,40},{... | collective-permute-start | bytes 1474568 | tf_op jit(solution)/shard_map/ppermute | solution.py:39
  128.6 28.0 %all-to-all-start.2 = ((bf16[16,64,768]{2,1,0:T(8,128)(2,1)}), bf16[16,64,768]{2,1,0:T(8,128)(2,1)S(1)}, u32[]{:S(2)}, u32[]{:S(2)}) async-start(bf16[16,64,768]{2,1,0:T(8,128)(2,1)} %get-tuple-element.42), calls=%async_computation.2 | async-start | bytes 3145728 | tf_op jit(solution)/shard_map/all_to_all | solution.py:377
  138.0 10.1 %collective-permute-start.20 = (bf16[2,160,768]{2,1,0:T(8,128)(2,1)S(1)}, bf16[2,160,768]{2,1,0:T(8,128)(2,1)S(1)}, u32[]{:S(2)}, u32[]{:S(2)}) collective-permute-start(bf16[2,160,768]{2,1,0:T(8,128)(2,1)S(1)} %add_convert_fusion), channel_id=1, source_target_pairs={{0,56},{1,9},{8,16},{9,1},{16,8},{17,25},{24,32},{25,17},{32,24},{... | collective-permute-start | bytes 1474568 | tf_op jit(solution)/shard_map/ppermute | solution.py:39
  149.5 7.2 %collective-permute-start.21 = (bf16[160,768]{1,0:T(8,128)(2,1)S(1)}, bf16[160,768]{1,0:T(8,128)(2,1)S(1)}, u32[]{:S(2)}, u32[]{:S(2)}) collective-permute-start(bf16[160,768]{1,0:T(8,128)(2,1)S(1)} %fusion.9), channel_id=1, source_target_pairs={{0,8},{1,57},{8,0},{9,17},{16,24},{17,9},{24,16},{25,33},{32,40},{... | collective-permute-start | bytes 737288 | tf_op jit(solution)/shard_map/ppermute | solution.py:39
  156.8 8.8 %collective-permute-start.22 = (bf16[64,768]{1,0:T(8,128)(2,1)S(1)}, bf16[64,768]{1,0:T(8,128)(2,1)S(1)}, u32[]{:S(2)}, u32[]{:S(2)}) collective-permute-start(bf16[64,768]{1,0:T(8,128)(2,1)S(1)} %get-tuple-element.47), channel_id=1, source_target_pairs={{0,128},{128,0},{1,129},{129,1},{2,130},{130,2},{3,131},{131,3},{4... | collective-permute-start | bytes 294920 | tf_op jit(solution)/shard_map/ppermute | solution.py:28
  158.1 15.6 %all-to-all-start.3 = ((f32[16,6,768]{2,1,0:T(8,128)}), f32[16,6,768]{2,1,0:T(8,128)S(1)}, u32[]{:S(2)}, u32[]{:S(2)}) async-start(f32[16,6,768]{2,1,0:T(8,128)} %reshape.109), calls=%async_computation.3 | async-start | bytes 786432 | tf_op jit(solution)/shard_map/all_to_all | solution.py:386
where the time goes:
time: 175 us; the launch traced here: 174 us
  waiting for transfers between devices  72.5 us (41%)
  starting transfers between devices  56.6 us (32%)
  Pallas kernels  25.5 us (15%)
  local copies, waits for them, and re-layouts  7.46 us (4%)
  other arithmetic  7.23 us (4%)
  matrix products  3.53 us (2%)
    ppermute x10, waiting for transfers between devices, pair(): return lax.ppermute(value, ('z', 'c'), route)  41.8 us
    pallas_call x2, Pallas kernels, call(): pl.pallas_call(kernel, in_specs=[smem, smem] + [spaces[own] for _, own in...  25.5 us
    ppermute x10, starting transfers between devices, pair(): return lax.ppermute(value, ('z', 'c'), route)  19.4 us
    ppermute x13, waiting for transfers between devices, mirror(): lax.ppermute(value, axes, [(i, i ^ mask) for i in range(count(axes))])  11.8 us
    ppermute x13, starting transfers between devices, mirror(): lax.ppermute(value, axes, [(i, i ^ mask) for i in range(count(axes))])  10 us
    all_to_all x1, starting transfers between devices, per_device(): d_weight = jnp.sum(lax.all_to_all(d_weight, PLANE, 0, 0), axis=0)  7.57 us
    all_to_all x1, starting transfers between devices, per_device(): d_image = jnp.sum(wider(lax.all_to_all(d_image, PLANE, 0, 0)), axis=0)  7.4 us
    all_to_all x1, starting transfers between devices, gather(): return lax.all_to_all(copies, axes, 0, 0)  7.18 us
  transfers between devices with their start and end apart: 27, of which 18 were waited for; matrix products, arithmetic and copies ran while one was open for 6% of the time, Pallas kernels for 0%

commit v1 on v0

--- a/solution.py
+++ b/solution.py
@@ -13,7 +13,7 @@
 Y = ("yl", "yh")
 F32 = jnp.float32
 BF16 = jnp.bfloat16
-LIMIT = 56 << 20
+LIMIT = 52 << 20
 MEET = (0, 1, -1, -2, 2, 3, -3, -4)
 
 
@@ -106,7 +106,8 @@
     move = mover(sems)
 
     modal, image = [], []
-    for want in range(2):
+    image.append(move(h_img, x_img))
+    for want in (0, 1):
         for own in range(2):
             c = core if own == 0 else 1 - core
             for i, k in enumerate(meets(z, c)):
@@ -116,7 +117,6 @@
                     modal.append(move(piece.at[pl.ds(start + 2 * band, half)], x_mod.at[c * 8 + k]))
                 else:
                     image.append(move(piece.at[pl.ds(start, band)], w_img.at[c, k]))
-    image.append(move(h_img, x_img))
 
     going = []
     for rows, w, low, rest, inverse, to, needs in (
@@ -172,7 +172,7 @@
 def gradient_kernel(
     at, scale, row_sum, row_came, col_sum, col_came, partner, inv_img, inv_mod,
     h_power, h_img, h_mod, h_low_img, h_low_mod, h_res_img, h_res_mod,
-    o_img, o_keep, o_send,
+    o_img, o_keep, o_far, o_send,
     power, x_img, x_mod, low_img, low_mod, res_img, res_mod,
     weight_row, p_img, p_mod, keep, send, sems,
 ):
@@ -194,7 +194,9 @@
         move(h_low_img.at[parts[0]], low_img.at[parts[0]]),
         move(h_res_img.at[parts[0]], res_img.at[parts[0]]),
     ]
-    loads = [load(1)]
+    loads = [load(1), load(2), load(3)]
+    modal = [move(h_res_mod, res_mod)]
+    rest = [move(h_img, x_img), move(h_mod, x_mod)]
 
     j = lax.broadcasted_iota(jnp.int32, (1, 16 * half), 1)
     jz, jc, jr = (j // half) & 7, j // (8 * half), j & (half - 1)
@@ -217,11 +219,6 @@
     weigh(0)
     arrive([low] + needs)
     for i, take in enumerate(parts):
-        if i < 2:
-            loads.append(load(i + 2))
-        if i == 2:
-            modal = [move(h_res_mod, res_mod)]
-            rest = [move(h_img, x_img), move(h_mod, x_mod)]
         if i < 3:
             arrive(loads[i])
         grad = jnp.dot(weight_row[take], low_mod[...], preferred_element_type=F32)
@@ -265,15 +262,10 @@
             def _():
                 put(send)
 
-        if s == 0:
-            first, last = pl.ds(0, band), pl.ds(2 * band, half)
-            for source, target in ((keep, o_keep), (send, o_send)):
-                for lines in (first, last):
-                    going.append(move(source.at[pl.ds(0, 8), lines], target.at[pl.ds(0, 8), lines]))
-        else:
-            lines = pl.ds(band, band)
+        for lines in (pl.ds(0, band), pl.ds(2 * band, half)) if s == 0 else (pl.ds(band, band),):
             for source, target in ((keep, o_keep), (send, o_send)):
                 going.append(move(source.at[pl.ds(0, 8), lines], target.at[pl.ds(0, 8), lines]))
+            going.append(move(send.at[pl.ds(6, 2), lines], o_far.at[pl.ds(0, 2), lines]))
     arrive(going)
 
 
@@ -363,27 +355,31 @@
     row_came, col_came = exchange(row_sum, col_sum, 3)
 
     block = (8, 2 * band + half, width)
-    d_image, keep, send = call(
+    d_image, keep, far, send = call(
         gradient_kernel,
         at,
         scale,
         here_first([row_sum, row_came, col_sum, col_came, partner, inv_img, inv_mod], False)
         + here_first([power, image_x, x_mod, low_img, low_mod, res_img, res_mod], True),
-        here_first([rows, (block, BF16), (block, BF16)], True),
+        here_first([rows, (block, BF16), ((2, *block[1:]), BF16), (block, BF16)], True),
         [square, rows, rows, flat, flat, flat, flat, ((size, size), BF16), rows, rows]
         + [(block, BF16), (block, BF16)],
         4 * size * width * width + 4 * size * size * width,
     )
-    d_image = jnp.sum(wider(lax.all_to_all(d_image, PLANE, 0, 0)), axis=0)
+    d_image = lax.all_to_all(d_image, PLANE, 0, 0)
+    far, send = stage(mirror(far, ("c",)), send)
+    mine = wider(keep[6:]) + wider(far)
     send = mirror(send, ("c",))
-    mine = wider(keep[6:]) + wider(send[6:])
     for step, first in ((1, 4), (0, 2), (1, 0)):
         came = pair(mine.astype(BF16), step)
+        if first == 0:
+            came, d_image = stage(came, d_image)
         mine = wider(keep[first : first + 2]) + wider(send[first : first + 2]) + wider(came)
     sums = mine[0] + wider(pair(mine[1].astype(BF16), 0))
+    d_image = jnp.sum(wider(d_image), axis=0)
     d_modal = sums[2 * band :]
     d_weight = sums[: 2 * band].reshape(16, band // 8, width)
-    d_weight = jnp.sum(lax.all_to_all(d_weight, PLANE, 0, 0), axis=0)
+    d_weight = jnp.sum(lax.all_to_all(d_weight, PLANE, 0, 0), axis=0, keepdims=True)
 
     came = mirror(jnp.where(side == 0, d_modal, d_image), ("yl",))
     d_proj = jnp.where(
@@ -397,7 +393,7 @@
     d_inputs = lax.dot_general(
         d_inputs.astype(BF16), reorder(width), (((1,), (1,)), ((), ())), preferred_element_type=F32
     )
-    return (d_inputs.astype(BF16)[None], d_weight[None])
+    return (d_inputs.astype(BF16)[None], d_weight)
 
 
 def solution(mesh):

time: 175 us -> 171 us (0.977)
  starting transfers between devices: 56.6 us -> 59.4 us
  waiting for transfers between devices: 72.5 us -> 70 us
  local copies, waits for them, and re-layouts: 7.46 us -> 5.46 us
    ppermute x10, waiting for transfers between devices: 41.8 us -> 38.2 us  [pair(): return lax.ppermute(value, ('z', 'c'), route)]
    all_to_all x2, waiting for transfers between devices: 12 us -> 15.6 us  [the longest x1 9.2 us: per_device(): d_image = lax.all_to_all(d_image, PLANE, 0, 0)]
    ppermute x13 -> x14, waiting for transfers between devices: 11.8 us -> 9.28 us  [mirror(): lax.ppermute(value, axes, [(i, i ^ mask) for i in range(count(axes))])]
    ppermute x13 -> x14, starting transfers between devices: 10 us -> 11.7 us  [mirror(): lax.ppermute(value, axes, [(i, i ^ mask) for i in range(count(axes))])]
  transfers between devices with their start and end apart: 27 -> 28, of which waited for: 18 -> 17; matrix products, arithmetic and copies ran while one was open for 6% -> 6% of each run, Pallas kernels for 0% -> 0%
where the time goes in v1:
time: 171 us; the launch traced here: 170 us
  waiting for transfers between devices  70 us (41%)
  starting transfers between devices  59.4 us (35%)
  Pallas kernels  25.9 us (15%)
  other arithmetic  5.68 us (3%)
  local copies, waits for them, and re-layouts  5.46 us (3%)
  matrix products  2.26 us (1%)
    ppermute x10, waiting for transfers between devices, pair(): return lax.ppermute(value, ('z', 'c'), route)  38.2 us
    pallas_call x2, Pallas kernels, call(): pl.pallas_call(kernel, in_specs=[smem, smem] + [spaces[own] for _, own in...  25.9 us
    ppermute x10, starting transfers between devices, pair(): return lax.ppermute(value, ('z', 'c'), route)  19.2 us
    ppermute x14, starting transfers between devices, mirror(): lax.ppermute(value, axes, [(i, i ^ mask) for i in range(count(axes))])  11.7 us
    ppermute x14, waiting for transfers between devices, mirror(): lax.ppermute(value, axes, [(i, i ^ mask) for i in range(count(axes))])  9.28 us
    all_to_all x1, waiting for transfers between devices, per_device(): d_image = lax.all_to_all(d_image, PLANE, 0, 0)  9.2 us
    all_to_all x1, starting transfers between devices, per_device(): lax.all_to_all(d_weight, PLANE, 0, 0)  7.91 us
    all_to_all x1, starting transfers between devices, per_device(): d_image = lax.all_to_all(d_image, PLANE, 0, 0)  7.75 us
  transfers between devices with their start and end apart: 28, of which 17 were waited for; matrix products, arithmetic and copies ran while one was open for 6% of the time, Pallas kernels for 0%

profile of v1, /device:TPU:2, one launch (start us, length us, event | category | flops | bytes accessed | tf_op | source)
XLA Modules:
  0.0 170.2 jit_solution(9400893360550694235)
XLA Ops:
  0.7 0.9 copy-done
  1.6 0.6 fusion.4
  2.2 1.7 collective-permute-start
  3.9 1.4 broadcast_in_dim.12
  5.3 7.2 %all-to-all-start.1 = ((bf16[16,6,768]{2,1,0:T(8,128)(2,1)}), bf16[16,6,768]{2,1,0:T(8,128)(2,1)S(1)}, u32[]{:S(2)}, u32[]{:S(2)}) async-start(bf16[16,6,768]{2,1,0:T(8,128)(2,1)} %broadcast_in_dim.12), calls=%async_computation.1 | async-start | bytes 393216 | tf_op jit(solution)/shard_map/all_to_all | solution.py:49
  12.5 6.9 %all-to-all-done.1 = bf16[16,6,768]{2,1,0:T(8,128)(2,1)S(1)} async-done(((bf16[16,6,768]{2,1,0:T(8,128)(2,1)}), bf16[16,6,768]{2,1,0:T(8,128)(2,1)S(1)}, u32[]{:S(2)}, u32[]{:S(2)}) %all-to-all-start.1) | async-done | bytes 147488 | tf_op jit(solution)/shard_map/all_to_all | solution.py:49
  19.5 2.0 %collective-permute-start.1 = (bf16[160,768]{1,0:T(8,128)(2,1)S(1)}, bf16[160,768]{1,0:T(8,128)(2,1)S(1)}, u32[]{:S(2)}, u32[]{:S(2)}) collective-permute-start(bf16[160,768]{1,0:T(8,128)(2,1)S(1)} %pad_maximum_fusion.1), channel_id=1, source_target_pairs={{0,8},{1,57},{8,0},{9,17},{16,24},{17,9},{24,16},{25,33},{32,40},{... | collective-permute-start | bytes 737288 | tf_op jit(solution)/shard_map/ppermute | solution.py:39
  21.5 4.3 %collective-permute-done.1 = bf16[160,768]{1,0:T(8,128)(2,1)S(1)} collective-permute-done((bf16[160,768]{1,0:T(8,128)(2,1)S(1)}, bf16[160,768]{1,0:T(8,128)(2,1)S(1)}, u32[]{:S(2)}, u32[]{:S(2)}) %collective-permute-start.1) | collective-permute-done | bytes 245792 | tf_op jit(solution)/shard_map/ppermute | solution.py:39
  25.8 5.9 %collective-permute-start.2 = (bf16[320,768]{1,0:T(8,128)(2,1)S(1)}, bf16[320,768]{1,0:T(8,128)(2,1)S(1)}, u32[]{:S(2)}, u32[]{:S(2)}) collective-permute-start(bf16[320,768]{1,0:T(8,128)(2,1)S(1)} %pad_maximum_fusion.refs_0_), channel_id=1, source_target_pairs={{0,56},{1,9},{8,16},{9,1},{16,8},{17,25},{24,32},{25,17},{32,24},{... | collective-permute-start | bytes 1474568 | tf_op jit(solution)/shard_map/ppermute | solution.py:39
  31.8 1.3 broadcast_in_dim.10
  33.1 5.6 %all-to-all-start = ((bf16[16,64,768]{2,1,0:T(8,128)(2,1)}), bf16[16,64,768]{2,1,0:T(8,128)(2,1)}, u32[]{:S(2)}, u32[]{:S(2)}) async-start(bf16[16,64,768]{2,1,0:T(8,128)(2,1)} %broadcast_in_dim.10), calls=%async_computation | async-start | bytes 3145728 | tf_op jit(solution)/shard_map/all_to_all | solution.py:322
  38.8 9.5 %collective-permute-done.3.refs_2_ = bf16[320,768]{1,0:T(8,128)(2,1)S(1)} collective-permute-done((bf16[320,768]{1,0:T(8,128)(2,1)S(1)}, bf16[320,768]{1,0:T(8,128)(2,1)S(1)}, u32[]{:S(2)}, u32[]{:S(2)}) %collective-permute-start.3) | collective-permute-done | bytes 491552 | tf_op jit(solution)/shard_map/ppermute | solution.py:39
  48.3 3.0 %collective-permute-start.4 = (bf16[320,768]{1,0:T(8,128)(2,1)S(1)}, bf16[320,768]{1,0:T(8,128)(2,1)S(1)}, u32[]{:S(2)}, u32[]{:S(2)}) collective-permute-start(bf16[320,768]{1,0:T(8,128)(2,1)S(1)} %collective-permute-done.3.refs_2_), channel_id=1, source_target_pairs={{0,56},{1,9},{8,16},{9,1},{16,8},{17,25},{24,32},{25,17},{32,24},{... | collective-permute-start | bytes 1474568 | tf_op jit(solution)/shard_map/ppermute | solution.py:39
  51.3 0.5 collective-permute-start.6
  51.8 6.5 %collective-permute-done.4.refs_3_ = bf16[320,768]{1,0:T(8,128)(2,1)S(1)} collective-permute-done((bf16[320,768]{1,0:T(8,128)(2,1)S(1)}, bf16[320,768]{1,0:T(8,128)(2,1)S(1)}, u32[]{:S(2)}, u32[]{:S(2)}) %collective-permute-start.4) | collective-permute-done | bytes 491552 | tf_op jit(solution)/shard_map/ppermute | solution.py:39
  59.1 1.2 collective-permute-done.8.refs_7_
  60.3 11.4 %shard_map.59 = (f32[8,128]{1,0:T(8,128)S(1)}, f32[8,128]{1,0:T(8,128)S(1)}, f32[1,1024]{1,0:T(1,128)S(1)}, f32[1,1024]{1,0:T(1,128)S(1)}, bf16[16,64,768]{2,1,0...) custom-call(s32[5]{0:T(128)S(1)} %stack.23.at, ...), custom_call_target="tpu_custom_call" | custom-call | flops 4026531840 | bytes 8388608 | tf_op jit(solution)/shard_map/pallas_call | solution.py:275
  71.8 1.4 collective-permute-start.9
  73.1 2.3 %collective-permute-done.9 = f32[8,128]{1,0:T(8,128)S(1)} collective-permute-done((f32[8,128]{1,0:T(8,128)S(1)}, f32[8,128]{1,0:T(8,128)S(1)}, u32[]{:S(2)}, u32[]{:S(2)}) %collective-permute-start.9) | collective-permute-done | bytes 4128 | tf_op jit(solution)/shard_map/ppermute | solution.py:28
  75.5 3.1 %collective-permute-start.12 = (f32[8,128]{1,0:T(8,128)S(1)}, f32[8,128]{1,0:T(8,128)S(1)}, u32[]{:S(2)}, u32[]{:S(2)}) collective-permute-start(f32[8,128]{1,0:T(8,128)S(1)} %add.187), channel_id=1, source_target_pairs={{0,56},{1,9},{8,16},{9,1},{16,8},{17,25},{24,32},{25,17},{32,24},{... | collective-permute-start | bytes 12296 | tf_op jit(solution)/shard_map/ppermute | solution.py:39
  78.6 0.6 collective-permute-start.11
  79.2 1.2 collective-permute-done.12
  80.4 1.8 %collective-permute-done.11 = f32[8,128]{1,0:T(8,128)S(1)} collective-permute-done((f32[8,128]{1,0:T(8,128)S(1)}, f32[8,128]{1,0:T(8,128)S(1)}, u32[]{:S(2)}, u32[]{:S(2)}) %collective-permute-start.11) | collective-permute-done | bytes 4128 | tf_op jit(solution)/shard_map/ppermute | solution.py:28
  82.2 1.0 collective-permute-start.13
  83.4 2.5 %collective-permute-done.14 = f32[8,128]{1,0:T(8,128)S(1)} collective-permute-done((f32[8,128]{1,0:T(8,128)S(1)}, f32[8,128]{1,0:T(8,128)S(1)}, u32[]{:S(2)}, u32[]{:S(2)}) %collective-permute-start.14) | collective-permute-done | bytes 4128 | tf_op jit(solution)/shard_map/ppermute | solution.py:39
  85.9 2.7 %collective-permute-start.16 = (f32[8,128]{1,0:T(8,128)S(1)}, f32[8,128]{1,0:T(8,128)S(1)}, u32[]{:S(2)}, u32[]{:S(2)}) collective-permute-start(f32[8,128]{1,0:T(8,128)S(1)} %add.191.col_sum), channel_id=1, source_target_pairs={{0,32},{8,40},{16,48},{24,56},{32,0},{40,8},{48,16},{56,24},{1,33}... | collective-permute-start | bytes 12296 | tf_op jit(solution)/shard_map/ppermute | solution.py:28
  88.6 2.8 %collective-permute-start.15 = (f32[8,128]{1,0:T(8,128)S(1)}, f32[8,128]{1,0:T(8,128)S(1)}, u32[]{:S(2)}, u32[]{:S(2)}) collective-permute-start(f32[8,128]{1,0:T(8,128)S(1)} %add.190.row_sum), channel_id=1, source_target_pairs={{0,192},{64,128},{128,64},{192,0},{1,193},{65,129},{129,65},{193,1... | collective-permute-start | bytes 12296 | tf_op jit(solution)/shard_map/ppermute | solution.py:28
  91.5 2.0 %collective-permute-done.16.col_came = f32[8,128]{1,0:T(8,128)S(1)} collective-permute-done((f32[8,128]{1,0:T(8,128)S(1)}, f32[8,128]{1,0:T(8,128)S(1)}, u32[]{:S(2)}, u32[]{:S(2)}) %collective-permute-start.16) | collective-permute-done | bytes 4128 | tf_op jit(solution)/shard_map/ppermute | solution.py:28
  93.5 14.5 %shard_map.60 = (bf16[16,64,768]{2,1,0:T(8,128)(2,1)}, bf16[8,160,768]{2,1,0:T(8,128)(2,1)}, bf16[2,160,768]{2,1,0:T(8,128)(2,1)S(1)}, bf16[8,160,768]{2,1,0:T(8,128)(2,1)}) custom-call(s32[5]{0:T(128)S(1)} %stack.23.at, f32[1]{0:T(128)S(6)} %copy.7.scale, f32[8,128]{1,0:T(8,128)S(1)} %add.190.row_sum, f32[8,128]{1,0:T(8,128)S(1)} %collective-permute-done.15.row_came, ...), custom_call_target="tpu_custom_call" | custom-call | flops 5637144576 | bytes 8388608 | tf_op jit(solution)/shard_map/pallas_call | solution.py:275
  108.3 1.9 %collective-permute-done.17 = bf16[2,160,768]{2,1,0:T(8,128)(2,1)S(1)} collective-permute-done((bf16[2,160,768]{2,1,0:T(8,128)(2,1)S(1)}, bf16[2,160,768]{2,1,0:T(8,128)(2,1)S(1)}, u32[]{:S(2)}, u32[]{:S(2)}) %collective-permute-start.17) | collective-permute-done | bytes 491552 | tf_op jit(solution)/shard_map/ppermute | solution.py:28
  110.3 1.2 add_convert_fusion.2
  111.5 1.9 %collective-permute-start.19 = (bf16[2,160,768]{2,1,0:T(8,128)(2,1)S(1)}, bf16[2,160,768]{2,1,0:T(8,128)(2,1)S(1)}, u32[]{:S(2)}, u32[]{:S(2)}) collective-permute-start(bf16[2,160,768]{2,1,0:T(8,128)(2,1)S(1)} %add_convert_fusion.2), channel_id=1, source_target_pairs={{0,56},{1,9},{8,16},{9,1},{16,8},{17,25},{24,32},{25,17},{32,24},{... | collective-permute-start | bytes 1474568 | tf_op jit(solution)/shard_map/ppermute | solution.py:39
  113.4 7.8 %all-to-all-start.2 = ((bf16[16,64,768]{2,1,0:T(8,128)(2,1)}), bf16[16,64,768]{2,1,0:T(8,128)(2,1)S(1)}, u32[]{:S(2)}, u32[]{:S(2)}) async-start(bf16[16,64,768]{2,1,0:T(8,128)(2,1)} %get-tuple-element.52), calls=%async_computation.2 | async-start | bytes 3145728 | tf_op jit(solution)/shard_map/all_to_all | solution.py:369
  121.2 0.4 collective-permute-done.19
  121.6 1.4 add_convert_fusion.1
  123.0 1.0 collective-permute-start.20
  124.0 7.9 %collective-permute-done.20 = bf16[2,160,768]{2,1,0:T(8,128)(2,1)S(1)} collective-permute-done((bf16[2,160,768]{2,1,0:T(8,128)(2,1)S(1)}, bf16[2,160,768]{2,1,0:T(8,128)(2,1)S(1)}, u32[]{:S(2)}, u32[]{:S(2)}) %collective-permute-start.20) | collective-permute-done | bytes 491552 | tf_op jit(solution)/shard_map/ppermute | solution.py:39
  131.9 1.4 add_convert_fusion
  133.3 1.9 %collective-permute-start.21 = (bf16[2,160,768]{2,1,0:T(8,128)(2,1)S(1)}, bf16[2,160,768]{2,1,0:T(8,128)(2,1)S(1)}, u32[]{:S(2)}, u32[]{:S(2)}) collective-permute-start(bf16[2,160,768]{2,1,0:T(8,128)(2,1)S(1)} %add_convert_fusion), channel_id=1, source_target_pairs={{0,56},{1,9},{8,16},{9,1},{16,8},{17,25},{24,32},{25,17},{32,24},{... | collective-permute-start | bytes 1474568 | tf_op jit(solution)/shard_map/ppermute | solution.py:39
  135.2 9.2 %all-to-all-done.2 = bf16[16,64,768]{2,1,0:T(8,128)(2,1)S(1)} async-done(((bf16[16,64,768]{2,1,0:T(8,128)(2,1)}), bf16[16,64,768]{2,1,0:T(8,128)(2,1)S(1)}, u32[]{:S(2)}, u32[]{:S(2)}) %all-to-all-start.2) | async-done | bytes 1572896 | tf_op jit(solution)/shard_map/all_to_all | solution.py:369
  144.4 1.3 convert_add_fusion
  146.1 6.0 %collective-permute-done.22 = bf16[160,768]{1,0:T(8,128)(2,1)S(1)} collective-permute-done((bf16[160,768]{1,0:T(8,128)(2,1)S(1)}, bf16[160,768]{1,0:T(8,128)(2,1)S(1)}, u32[]{:S(2)}, u32[]{:S(2)}) %collective-permute-start.22) | collective-permute-done | bytes 245792 | tf_op jit(solution)/shard_map/ppermute | solution.py:39
  152.1 0.6 collective-permute-start.23
  152.8 0.8 reshape.109
  153.6 7.9 %all-to-all-start.3 = ((f32[16,6,768]{2,1,0:T(8,128)}), f32[16,6,768]{2,1,0:T(8,128)S(1)}, u32[]{:S(2)}, u32[]{:S(2)}) async-start(f32[16,6,768]{2,1,0:T(8,128)} %reshape.109), calls=%async_computation.3 | async-start | bytes 786432 | tf_op jit(solution)/shard_map/all_to_all | solution.py:382
  161.5 1.7 fusion.6
  163.2 6.4 %all-to-all-done.3 = f32[16,6,768]{2,1,0:T(8,128)S(1)} async-done(((f32[16,6,768]{2,1,0:T(8,128)}), f32[16,6,768]{2,1,0:T(8,128)S(1)}, u32[]{:S(2)}, u32[]{:S(2)}) %all-to-all-start.3) | async-done | bytes 294944 | tf_op jit(solution)/shard_map/all_to_all | solution.py:382
  169.6 0.6 broadcast_in_dim.27
  (53 shorter events, 1.7 us)
Async XLA Ops:
  0.6 0.9 copy-start
  2.2 10.2 %collective-permute-start = (bf16[64,768]{1,0:T(8,128)(2,1)S(1)}, bf16[64,768]{1,0:T(8,128)(2,1)S(1)}, u32[]{:S(2)}, u32[]{:S(2)}) collective-permute-start(bf16[64,768]{1,0:T(8,128)(2,1)S(1)} %dynamic-slice_bitcast_fusion), channel_id=1, source_target_pairs={{0,128},{128,0},{1,129},{129,1},{2,130},{130,2},{3,131},{131,3},{4... | collective-permute-start | bytes 294920 | tf_op jit(solution)/shard_map/ppermute | solution.py:28
  5.3 14.2 %all-to-all-start.1 = ((bf16[16,6,768]{2,1,0:T(8,128)(2,1)}), bf16[16,6,768]{2,1,0:T(8,128)(2,1)S(1)}, u32[]{:S(2)}, u32[]{:S(2)}) async-start(bf16[16,6,768]{2,1,0:T(8,128)(2,1)} %broadcast_in_dim.12), calls=%async_computation.1 | async-start | bytes 393216 | tf_op jit(solution)/shard_map/all_to_all | solution.py:49
  19.5 6.3 %collective-permute-start.1 = (bf16[160,768]{1,0:T(8,128)(2,1)S(1)}, bf16[160,768]{1,0:T(8,128)(2,1)S(1)}, u32[]{:S(2)}, u32[]{:S(2)}) collective-permute-start(bf16[160,768]{1,0:T(8,128)(2,1)S(1)} %pad_maximum_fusion.1), channel_id=1, source_target_pairs={{0,8},{1,57},{8,0},{9,17},{16,24},{17,9},{24,16},{25,33},{32,40},{... | collective-permute-start | bytes 737288 | tf_op jit(solution)/shard_map/ppermute | solution.py:39
  25.8 12.9 %collective-permute-start.2 = (bf16[320,768]{1,0:T(8,128)(2,1)S(1)}, bf16[320,768]{1,0:T(8,128)(2,1)S(1)}, u32[]{:S(2)}, u32[]{:S(2)}) collective-permute-start(bf16[320,768]{1,0:T(8,128)(2,1)S(1)} %pad_maximum_fusion.refs_0_), channel_id=1, source_target_pairs={{0,56},{1,9},{8,16},{9,1},{16,8},{17,25},{24,32},{25,17},{32,24},{... | collective-permute-start | bytes 1474568 | tf_op jit(solution)/shard_map/ppermute | solution.py:39
  33.1 26.0 %all-to-all-start = ((bf16[16,64,768]{2,1,0:T(8,128)(2,1)}), bf16[16,64,768]{2,1,0:T(8,128)(2,1)}, u32[]{:S(2)}, u32[]{:S(2)}) async-start(bf16[16,64,768]{2,1,0:T(8,128)(2,1)} %broadcast_in_dim.10), calls=%async_computation | async-start | bytes 3145728 | tf_op jit(solution)/shard_map/all_to_all | solution.py:322
  38.7 9.6 %collective-permute-start.3 = (bf16[320,768]{1,0:T(8,128)(2,1)S(1)}, bf16[320,768]{1,0:T(8,128)(2,1)S(1)}, u32[]{:S(2)}, u32[]{:S(2)}) collective-permute-start(bf16[320,768]{1,0:T(8,128)(2,1)S(1)} %collective-permute-done.2.refs_1_), channel_id=1, source_target_pairs={{0,8},{1,57},{8,0},{9,17},{16,24},{17,9},{24,16},{25,33},{32,40},{... | collective-permute-start | bytes 1474568 | tf_op jit(solution)/shard_map/ppermute | solution.py:39
  48.3 10.0 %collective-permute-start.4 = (bf16[320,768]{1,0:T(8,128)(2,1)S(1)}, bf16[320,768]{1,0:T(8,128)(2,1)S(1)}, u32[]{:S(2)}, u32[]{:S(2)}) collective-permute-start(bf16[320,768]{1,0:T(8,128)(2,1)S(1)} %collective-permute-done.3.refs_2_), channel_id=1, source_target_pairs={{0,56},{1,9},{8,16},{9,1},{16,8},{17,25},{24,32},{25,17},{32,24},{... | collective-permute-start | bytes 1474568 | tf_op jit(solution)/shard_map/ppermute | solution.py:39
  51.3 7.7 %collective-permute-start.5 = (bf16[320,768]{1,0:T(8,128)(2,1)S(1)}, bf16[320,768]{1,0:T(8,128)(2,1)S(1)}, u32[]{:S(2)}, u32[]{:S(2)}) collective-permute-start(bf16[320,768]{1,0:T(8,128)(2,1)S(1)} %pad_maximum_fusion.refs_0_), channel_id=1, source_target_pairs={{0,1},{1,0},{2,3},{3,2},{4,5},{5,4},{6,7},{7,6},{8,9},{9,8},{10,11... | collective-permute-start | bytes 1474568 | tf_op jit(solution)/shard_map/ppermute | solution.py:28
  51.3 7.7 %collective-permute-start.6 = (bf16[320,768]{1,0:T(8,128)(2,1)S(1)}, bf16[320,768]{1,0:T(8,128)(2,1)S(1)}, u32[]{:S(2)}, u32[]{:S(2)}) collective-permute-start(bf16[320,768]{1,0:T(8,128)(2,1)S(1)} %collective-permute-done.2.refs_1_), channel_id=1, source_target_pairs={{0,1},{1,0},{2,3},{3,2},{4,5},{5,4},{6,7},{7,6},{8,9},{9,8},{10,11... | collective-permute-start | bytes 1474568 | tf_op jit(solution)/shard_map/ppermute | solution.py:28
  51.8 7.3 %collective-permute-start.7 = (bf16[320,768]{1,0:T(8,128)(2,1)S(1)}, bf16[320,768]{1,0:T(8,128)(2,1)}, u32[]{:S(2)}, u32[]{:S(2)}) collective-permute-start(bf16[320,768]{1,0:T(8,128)(2,1)S(1)} %collective-permute-done.3.refs_2_), channel_id=1, source_target_pairs={{0,1},{1,0},{2,3},{3,2},{4,5},{5,4},{6,7},{7,6},{8,9},{9,8},{10,11... | collective-permute-start | bytes 1474568 | tf_op jit(solution)/shard_map/ppermute | solution.py:28
  58.3 2.0 %collective-permute-start.8 = (bf16[320,768]{1,0:T(8,128)(2,1)S(1)}, bf16[320,768]{1,0:T(8,128)(2,1)}, u32[]{:S(2)}, u32[]{:S(2)}) collective-permute-start(bf16[320,768]{1,0:T(8,128)(2,1)S(1)} %collective-permute-done.4.refs_3_), channel_id=1, source_target_pairs={{0,1},{1,0},{2,3},{3,2},{4,5},{5,4},{6,7},{7,6},{8,9},{9,8},{10,11... | collective-permute-start | bytes 1474568 | tf_op jit(solution)/shard_map/ppermute | solution.py:28
  59.1 24.2 %copy-start.1 = (s32[16384]{0:T(1024)S(1)}, s32[16384]{0:T(1024)}, u32[]{:S(2)}) copy-start(s32[16384]{0:T(1024)} %param.6) | copy-start | bytes 196612
  59.1 1.3 copy-start.2
  59.1 1.2 copy-start.3
  71.8 3.7 %collective-permute-start.9 = (f32[8,128]{1,0:T(8,128)S(1)}, f32[8,128]{1,0:T(8,128)S(1)}, u32[]{:S(2)}, u32[]{:S(2)}) collective-permute-start(f32[8,128]{1,0:T(8,128)S(1)} %get-tuple-element.29), channel_id=1, source_target_pairs={{0,2},{2,0},{4,6},{6,4},{1,3},{3,1},{5,7},{7,5},{8,10},{10,8},{12,... | collective-permute-start | bytes 12296 | tf_op jit(solution)/shard_map/ppermute | solution.py:28
  73.1 2.3 %collective-permute-start.10 = (f32[8,128]{1,0:T(8,128)S(1)}, f32[8,128]{1,0:T(8,128)S(1)}, u32[]{:S(2)}, u32[]{:S(2)}) collective-permute-start(f32[8,128]{1,0:T(8,128)S(1)} %get-tuple-element.30), channel_id=1, source_target_pairs={{0,1},{1,0},{2,3},{3,2},{4,5},{5,4},{6,7},{7,6},{8,9},{9,8},{10,11... | collective-permute-start | bytes 12296 | tf_op jit(solution)/shard_map/ppermute | solution.py:28
  75.5 4.9 %collective-permute-start.12 = (f32[8,128]{1,0:T(8,128)S(1)}, f32[8,128]{1,0:T(8,128)S(1)}, u32[]{:S(2)}, u32[]{:S(2)}) collective-permute-start(f32[8,128]{1,0:T(8,128)S(1)} %add.187), channel_id=1, source_target_pairs={{0,56},{1,9},{8,16},{9,1},{16,8},{17,25},{24,32},{25,17},{32,24},{... | collective-permute-start | bytes 12296 | tf_op jit(solution)/shard_map/ppermute | solution.py:39
  78.6 3.6 %collective-permute-start.11 = (f32[8,128]{1,0:T(8,128)S(1)}, f32[8,128]{1,0:T(8,128)S(1)}, u32[]{:S(2)}, u32[]{:S(2)}) collective-permute-start(f32[8,128]{1,0:T(8,128)S(1)} %add.186), channel_id=1, source_target_pairs={{0,6},{2,4},{4,2},{6,0},{1,7},{3,5},{5,3},{7,1},{8,14},{10,12},{12... | collective-permute-start | bytes 12296 | tf_op jit(solution)/shard_map/ppermute | solution.py:28
  82.2 3.6 %collective-permute-start.14 = (f32[8,128]{1,0:T(8,128)S(1)}, f32[8,128]{1,0:T(8,128)S(1)}, u32[]{:S(2)}, u32[]{:S(2)}) collective-permute-start(f32[8,128]{1,0:T(8,128)S(1)} %add.189), channel_id=1, source_target_pairs={{0,8},{1,57},{8,0},{9,17},{16,24},{17,9},{24,16},{25,33},{32,40},{... | collective-permute-start | bytes 12296 | tf_op jit(solution)/shard_map/ppermute | solution.py:39
  82.2 3.7 %collective-permute-start.13 = (f32[8,128]{1,0:T(8,128)S(1)}, f32[8,128]{1,0:T(8,128)S(1)}, u32[]{:S(2)}, u32[]{:S(2)}) collective-permute-start(f32[8,128]{1,0:T(8,128)S(1)} %add.188), channel_id=1, source_target_pairs={{0,128},{64,192},{128,0},{192,64},{1,129},{65,193},{129,1},{193,65... | collective-permute-start | bytes 12296 | tf_op jit(solution)/shard_map/ppermute | solution.py:28
  85.9 7.6 %collective-permute-start.16 = (f32[8,128]{1,0:T(8,128)S(1)}, f32[8,128]{1,0:T(8,128)S(1)}, u32[]{:S(2)}, u32[]{:S(2)}) collective-permute-start(f32[8,128]{1,0:T(8,128)S(1)} %add.191.col_sum), channel_id=1, source_target_pairs={{0,32},{8,40},{16,48},{24,56},{32,0},{40,8},{48,16},{56,24},{1,33}... | collective-permute-start | bytes 12296 | tf_op jit(solution)/shard_map/ppermute | solution.py:28
  88.6 4.9 %collective-permute-start.15 = (f32[8,128]{1,0:T(8,128)S(1)}, f32[8,128]{1,0:T(8,128)S(1)}, u32[]{:S(2)}, u32[]{:S(2)}) collective-permute-start(f32[8,128]{1,0:T(8,128)S(1)} %add.190.row_sum), channel_id=1, source_target_pairs={{0,192},{64,128},{128,64},{192,0},{1,193},{65,129},{129,65},{193,1... | collective-permute-start | bytes 12296 | tf_op jit(solution)/shard_map/ppermute | solution.py:28
  108.0 2.2 %collective-permute-start.17 = (bf16[2,160,768]{2,1,0:T(8,128)(2,1)S(1)}, bf16[2,160,768]{2,1,0:T(8,128)(2,1)S(1)}, u32[]{:S(2)}, u32[]{:S(2)}) collective-permute-start(bf16[2,160,768]{2,1,0:T(8,128)(2,1)S(1)} %get-tuple-element.48), channel_id=1, source_target_pairs={{0,1},{1,0},{2,3},{3,2},{4,5},{5,4},{6,7},{7,6},{8,9},{9,8},{10,11... | collective-permute-start | bytes 1474568 | tf_op jit(solution)/shard_map/ppermute | solution.py:28
  110.2 11.4 %collective-permute-start.18 = (bf16[8,160,768]{2,1,0:T(8,128)(2,1)}, bf16[8,160,768]{2,1,0:T(8,128)(2,1)}, u32[]{:S(2)}, u32[]{:S(2)}) collective-permute-start(bf16[8,160,768]{2,1,0:T(8,128)(2,1)} %get-tuple-element.50), channel_id=1, source_target_pairs={{0,1},{1,0},{2,3},{3,2},{4,5},{5,4},{6,7},{7,6},{8,9},{9,8},{10,11... | collective-permute-start | bytes 5898248 | tf_op jit(solution)/shard_map/ppermute | solution.py:28
  111.5 10.1 %collective-permute-start.19 = (bf16[2,160,768]{2,1,0:T(8,128)(2,1)S(1)}, bf16[2,160,768]{2,1,0:T(8,128)(2,1)S(1)}, u32[]{:S(2)}, u32[]{:S(2)}) collective-permute-start(bf16[2,160,768]{2,1,0:T(8,128)(2,1)S(1)} %add_convert_fusion.2), channel_id=1, source_target_pairs={{0,56},{1,9},{8,16},{9,1},{16,8},{17,25},{24,32},{25,17},{32,24},{... | collective-permute-start | bytes 1474568 | tf_op jit(solution)/shard_map/ppermute | solution.py:39
  113.4 31.0 %all-to-all-start.2 = ((bf16[16,64,768]{2,1,0:T(8,128)(2,1)}), bf16[16,64,768]{2,1,0:T(8,128)(2,1)S(1)}, u32[]{:S(2)}, u32[]{:S(2)}) async-start(bf16[16,64,768]{2,1,0:T(8,128)(2,1)} %get-tuple-element.52), calls=%async_computation.2 | async-start | bytes 3145728 | tf_op jit(solution)/shard_map/all_to_all | solution.py:369
  123.0 8.9 %collective-permute-start.20 = (bf16[2,160,768]{2,1,0:T(8,128)(2,1)S(1)}, bf16[2,160,768]{2,1,0:T(8,128)(2,1)S(1)}, u32[]{:S(2)}, u32[]{:S(2)}) collective-permute-start(bf16[2,160,768]{2,1,0:T(8,128)(2,1)S(1)} %add_convert_fusion.1), channel_id=1, source_target_pairs={{0,8},{1,57},{8,0},{9,17},{16,24},{17,9},{24,16},{25,33},{32,40},{... | collective-permute-start | bytes 1474568 | tf_op jit(solution)/shard_map/ppermute | solution.py:39
  133.3 11.2 %collective-permute-start.21 = (bf16[2,160,768]{2,1,0:T(8,128)(2,1)S(1)}, bf16[2,160,768]{2,1,0:T(8,128)(2,1)S(1)}, u32[]{:S(2)}, u32[]{:S(2)}) collective-permute-start(bf16[2,160,768]{2,1,0:T(8,128)(2,1)S(1)} %add_convert_fusion), channel_id=1, source_target_pairs={{0,56},{1,9},{8,16},{9,1},{16,8},{17,25},{24,32},{25,17},{32,24},{... | collective-permute-start | bytes 1474568 | tf_op jit(solution)/shard_map/ppermute | solution.py:39
  145.8 6.3 %collective-permute-start.22 = (bf16[160,768]{1,0:T(8,128)(2,1)S(1)}, bf16[160,768]{1,0:T(8,128)(2,1)S(1)}, u32[]{:S(2)}, u32[]{:S(2)}) collective-permute-start(bf16[160,768]{1,0:T(8,128)(2,1)S(1)} %fusion.9), channel_id=1, source_target_pairs={{0,8},{1,57},{8,0},{9,17},{16,24},{17,9},{24,16},{25,33},{32,40},{... | collective-permute-start | bytes 737288 | tf_op jit(solution)/shard_map/ppermute | solution.py:39
  146.1 15.4 %copy-start.4 = (bf16[2,8,48,768]{3,2,1,0:T(8,128)(2,1)S(1)}, bf16[2,8,48,768]{3,2,1,0:T(8,128)(2,1)}, u32[]{:S(2)}) copy-start(bf16[2,8,48,768]{3,2,1,0:T(8,128)(2,1)} %get-tuple-element.55) | copy-start | bytes 3538948
  152.1 9.4 %collective-permute-start.23 = (bf16[64,768]{1,0:T(8,128)(2,1)S(1)}, bf16[64,768]{1,0:T(8,128)(2,1)S(1)}, u32[]{:S(2)}, u32[]{:S(2)}) collective-permute-start(bf16[64,768]{1,0:T(8,128)(2,1)S(1)} %get-tuple-element.57), channel_id=1, source_target_pairs={{0,128},{128,0},{1,129},{129,1},{2,130},{130,2},{3,131},{131,3},{4... | collective-permute-start | bytes 294920 | tf_op jit(solution)/shard_map/ppermute | solution.py:28
  153.6 15.9 %all-to-all-start.3 = ((f32[16,6,768]{2,1,0:T(8,128)}), f32[16,6,768]{2,1,0:T(8,128)S(1)}, u32[]{:S(2)}, u32[]{:S(2)}) async-start(f32[16,6,768]{2,1,0:T(8,128)} %reshape.109), calls=%async_computation.3 | async-start | bytes 786432 | tf_op jit(solution)/shard_map/all_to_all | solution.py:382

commit v2 on v1

--- a/solution.py
+++ b/solution.py
@@ -36,6 +36,16 @@
             kind = (core + step) % 2
             other = (((i + kind) ^ 1) - kind) % size
             route.append((2 * i + core, 2 * other + core))
+    return lax.ppermute(value, ("z", "c"), route)
+
+
+def across(value):
+    size = SIZES["z"]
+    route = []
+    for i in range(size):
+        for core in range(2):
+            step = 3 if (i + core) % 2 else -3
+            route.append((2 * i + core, 2 * ((i + step) % size) + core))
     return lax.ppermute(value, ("z", "c"), route)
 
 
@@ -313,6 +323,7 @@
     modal_x = jnp.where(side == 0, came, keep)
 
     copies = jnp.broadcast_to(image_x[None], (16, half, width))
+    copies, modal_x = stage(copies, modal_x)
     near = [jnp.concatenate([w0, modal_x])]
     near = [jnp.concatenate([near[0], pair(near[0], 0)])]
     far = [mirror(near[0], ("c",))]
@@ -344,7 +355,7 @@
         if step == 0:
             came = mirror(col_sum, ("c",))
         elif step == 3:
-            came = mirror(col_sum, ("z",), 4)
+            came = across(col_sum)
         else:
             came = pair(col_sum, step)
         return stage(mirror(row_sum, axes, mask), came)

time: 171 us -> 170 us (level)
  starting transfers between devices: 59.4 us -> 56.2 us
  waiting for transfers between devices: 70 us -> 72.1 us
    ppermute x10, waiting for transfers between devices: 38.2 us -> 44.3 us  [pair(): return lax.ppermute(value, ('z', 'c'), route)]
    ppermute x14 -> x13, starting transfers between devices: 11.7 us -> 6.53 us  [mirror(): lax.ppermute(value, axes, [(i, i ^ mask) for i in range(count(axes))])]
    all_to_all x1, waiting for transfers between devices: 9.2 us -> 5.29 us  [per_device(): d_image = lax.all_to_all(d_image, PLANE, 0, 0)]
    ppermute x0 -> x1, starting transfers between devices: none -> 3.11 us  [across(): return lax.ppermute(value, ('z', 'c'), route)]
    ppermute x0 -> x1, waiting for transfers between devices: none -> 2.06 us  [across(): return lax.ppermute(value, ('z', 'c'), route)]
    ppermute x14 -> x13, waiting for transfers between devices: 9.28 us -> 8.58 us  [mirror(): lax.ppermute(value, axes, [(i, i ^ mask) for i in range(count(axes))])]
  transfers between devices with their start and end apart: 28 -> 28, of which waited for: 17 -> 20; matrix products, arithmetic and copies ran while one was open for 6% -> 6% of each run, Pallas kernels for 0% -> 0%
where the time goes in v2:
time: 170 us; the launch traced here: 169 us
  waiting for transfers between devices  72.1 us (42%)
  starting transfers between devices  56.2 us (33%)
  Pallas kernels  25.9 us (15%)
  other arithmetic  5.65 us (3%)
  local copies, waits for them, and re-layouts  5.5 us (3%)
  matrix products  2.26 us (1%)
    ppermute x10, waiting for transfers between devices, pair(): return lax.ppermute(value, ('z', 'c'), route)  44.3 us
    pallas_call x2, Pallas kernels, call(): pl.pallas_call(kernel, in_specs=[smem, smem] + [spaces[own] for _, own in...  25.9 us
    ppermute x10, starting transfers between devices, pair(): return lax.ppermute(value, ('z', 'c'), route)  19.4 us
    ppermute x13, waiting for transfers between devices, mirror(): lax.ppermute(value, axes, [(i, i ^ mask) for i in range(count(axes))])  8.58 us
    all_to_all x1, starting transfers between devices, per_device(): lax.all_to_all(d_weight, PLANE, 0, 0)  8.15 us
    all_to_all x1, starting transfers between devices, gather(): return lax.all_to_all(copies, axes, 0, 0)  7.18 us
    ppermute x13, starting transfers between devices, mirror(): lax.ppermute(value, axes, [(i, i ^ mask) for i in range(count(axes))])  6.53 us
    all_to_all x1, waiting for transfers between devices, per_device(): lax.all_to_all(d_weight, PLANE, 0, 0)  6.36 us
  transfers between devices with their start and end apart: 28, of which 20 were waited for; matrix products, arithmetic and copies ran while one was open for 6% of the time, Pallas kernels for 0%

profile of v2, /device:TPU:2, one launch (start us, length us, event | category | flops | bytes accessed | tf_op | source)
XLA Modules:
  0.0 169.2 jit_solution(12189769408771008928)
XLA Ops:
  0.7 0.9 copy-done
  1.6 0.6 fusion.4
  2.2 1.7 collective-permute-start
  3.9 1.4 broadcast_in_dim.12
  5.3 7.2 %all-to-all-start.1 = ((bf16[16,6,768]{2,1,0:T(8,128)(2,1)}), bf16[16,6,768]{2,1,0:T(8,128)(2,1)S(1)}, u32[]{:S(2)}, u32[]{:S(2)}) async-start(bf16[16,6,768]{2,1,0:T(8,128)(2,1)} %broadcast_in_dim.12), calls=%async_computation.1 | async-start | bytes 393216 | tf_op jit(solution)/shard_map/all_to_all | solution.py:59
  12.5 1.3 broadcast_in_dim.10
  13.8 5.6 %all-to-all-done.1 = bf16[16,6,768]{2,1,0:T(8,128)(2,1)S(1)} async-done(((bf16[16,6,768]{2,1,0:T(8,128)(2,1)}), bf16[16,6,768]{2,1,0:T(8,128)(2,1)S(1)}, u32[]{:S(2)}, u32[]{:S(2)}) %all-to-all-start.1) | async-done | bytes 147488 | tf_op jit(solution)/shard_map/all_to_all | solution.py:59
  19.5 2.0 %collective-permute-start.1 = (bf16[160,768]{1,0:T(8,128)(2,1)S(1)}, bf16[160,768]{1,0:T(8,128)(2,1)S(1)}, u32[]{:S(2)}, u32[]{:S(2)}) collective-permute-start(bf16[160,768]{1,0:T(8,128)(2,1)S(1)} %pad_maximum_fusion), channel_id=1, source_target_pairs={{0,8},{1,57},{8,0},{9,17},{16,24},{17,9},{24,16},{25,33},{32,40},{... | collective-permute-start | bytes 737288 | tf_op jit(solution)/shard_map/ppermute | solution.py:39
  21.5 4.3 %collective-permute-done.1 = bf16[160,768]{1,0:T(8,128)(2,1)S(1)} collective-permute-done((bf16[160,768]{1,0:T(8,128)(2,1)S(1)}, bf16[160,768]{1,0:T(8,128)(2,1)S(1)}, u32[]{:S(2)}, u32[]{:S(2)}) %collective-permute-start.1) | collective-permute-done | bytes 245792 | tf_op jit(solution)/shard_map/ppermute | solution.py:39
  25.8 5.9 %collective-permute-start.2 = (bf16[320,768]{1,0:T(8,128)(2,1)S(1)}, bf16[320,768]{1,0:T(8,128)(2,1)S(1)}, u32[]{:S(2)}, u32[]{:S(2)}) collective-permute-start(bf16[320,768]{1,0:T(8,128)(2,1)S(1)} %constant_dynamic-update-slice_fusion.refs_0_), channel_id=1, source_target_pairs={{0,56},{1,9},{8,16},{9,1},{16,8},{17,25},{24,32},{25,17},{32,24},{... | collective-permute-start | bytes 1474568 | tf_op jit(solution)/shard_map/ppermute | solution.py:39
  31.8 5.6 %all-to-all-start = ((bf16[16,64,768]{2,1,0:T(8,128)(2,1)}), bf16[16,64,768]{2,1,0:T(8,128)(2,1)}, u32[]{:S(2)}, u32[]{:S(2)}) async-start(bf16[16,64,768]{2,1,0:T(8,128)(2,1)} %broadcast_in_dim.10), calls=%async_computation | async-start | bytes 3145728 | tf_op jit(solution)/shard_map/all_to_all | solution.py:333
  37.4 1.2 collective-permute-done.2.refs_1_
  38.6 9.3 %collective-permute-done.3.refs_2_ = bf16[320,768]{1,0:T(8,128)(2,1)S(1)} collective-permute-done((bf16[320,768]{1,0:T(8,128)(2,1)S(1)}, bf16[320,768]{1,0:T(8,128)(2,1)S(1)}, u32[]{:S(2)}, u32[]{:S(2)}) %collective-permute-start.3) | collective-permute-done | bytes 491552 | tf_op jit(solution)/shard_map/ppermute | solution.py:39
  47.8 3.5 %collective-permute-start.4 = (bf16[320,768]{1,0:T(8,128)(2,1)S(1)}, bf16[320,768]{1,0:T(8,128)(2,1)S(1)}, u32[]{:S(2)}, u32[]{:S(2)}) collective-permute-start(bf16[320,768]{1,0:T(8,128)(2,1)S(1)} %collective-permute-done.3.refs_2_), channel_id=1, source_target_pairs={{0,56},{1,9},{8,16},{9,1},{16,8},{17,25},{24,32},{25,17},{32,24},{... | collective-permute-start | bytes 1474568 | tf_op jit(solution)/shard_map/ppermute | solution.py:39
  51.8 6.3 %collective-permute-done.4.refs_3_ = bf16[320,768]{1,0:T(8,128)(2,1)S(1)} collective-permute-done((bf16[320,768]{1,0:T(8,128)(2,1)S(1)}, bf16[320,768]{1,0:T(8,128)(2,1)S(1)}, u32[]{:S(2)}, u32[]{:S(2)}) %collective-permute-start.4) | collective-permute-done | bytes 491552 | tf_op jit(solution)/shard_map/ppermute | solution.py:39
  58.9 1.2 collective-permute-done.8.refs_7_
  60.1 11.4 %shard_map.59 = (f32[8,128]{1,0:T(8,128)S(1)}, f32[8,128]{1,0:T(8,128)S(1)}, f32[1,1024]{1,0:T(1,128)S(1)}, f32[1,1024]{1,0:T(1,128)S(1)}, bf16[16,64,768]{2,1,0...) custom-call(s32[5]{0:T(128)S(1)} %stack.23.at, ...), custom_call_target="tpu_custom_call" | custom-call | flops 4026531840 | bytes 8388608 | tf_op jit(solution)/shard_map/pallas_call | solution.py:285
  71.6 1.6 collective-permute-start.9
  73.1 2.1 %collective-permute-done.9 = f32[8,128]{1,0:T(8,128)S(1)} collective-permute-done((f32[8,128]{1,0:T(8,128)S(1)}, f32[8,128]{1,0:T(8,128)S(1)}, u32[]{:S(2)}, u32[]{:S(2)}) %collective-permute-start.9) | collective-permute-done | bytes 4128 | tf_op jit(solution)/shard_map/ppermute | solution.py:28
  75.3 3.3 %collective-permute-start.12 = (f32[8,128]{1,0:T(8,128)S(1)}, f32[8,128]{1,0:T(8,128)S(1)}, u32[]{:S(2)}, u32[]{:S(2)}) collective-permute-start(f32[8,128]{1,0:T(8,128)S(1)} %add.187), channel_id=1, source_target_pairs={{0,56},{1,9},{8,16},{9,1},{16,8},{17,25},{24,32},{25,17},{32,24},{... | collective-permute-start | bytes 12296 | tf_op jit(solution)/shard_map/ppermute | solution.py:39
  78.6 0.6 collective-permute-start.11
  79.2 1.0 collective-permute-done.12
  80.2 2.0 %collective-permute-done.11 = f32[8,128]{1,0:T(8,128)S(1)} collective-permute-done((f32[8,128]{1,0:T(8,128)S(1)}, f32[8,128]{1,0:T(8,128)S(1)}, u32[]{:S(2)}, u32[]{:S(2)}) %collective-permute-start.11) | collective-permute-done | bytes 4128 | tf_op jit(solution)/shard_map/ppermute | solution.py:28
  82.6 3.2 %collective-permute-done.14 = f32[8,128]{1,0:T(8,128)S(1)} collective-permute-done((f32[8,128]{1,0:T(8,128)S(1)}, f32[8,128]{1,0:T(8,128)S(1)}, u32[]{:S(2)}, u32[]{:S(2)}) %collective-permute-start.14) | collective-permute-done | bytes 4128 | tf_op jit(solution)/shard_map/ppermute | solution.py:39
  85.9 3.1 %collective-permute-start.16 = (f32[8,128]{1,0:T(8,128)S(1)}, f32[8,128]{1,0:T(8,128)S(1)}, u32[]{:S(2)}, u32[]{:S(2)}) collective-permute-start(f32[8,128]{1,0:T(8,128)S(1)} %add.191.col_sum), channel_id=1, source_target_pairs={{0,40},{1,25},{8,32},{9,49},{16,56},{17,41},{24,48},{25,1},{32,8},... | collective-permute-start | bytes 12296 | tf_op jit(solution)/shard_map/ppermute | solution.py:49
  89.0 1.4 collective-permute-start.15
  90.5 2.1 %collective-permute-done.16.col_came = f32[8,128]{1,0:T(8,128)S(1)} collective-permute-done((f32[8,128]{1,0:T(8,128)S(1)}, f32[8,128]{1,0:T(8,128)S(1)}, u32[]{:S(2)}, u32[]{:S(2)}) %collective-permute-start.16) | collective-permute-done | bytes 4128 | tf_op jit(solution)/shard_map/ppermute | solution.py:49
  92.6 1.3 collective-permute-done.15.row_came
  93.8 14.5 %shard_map.60 = (bf16[16,64,768]{2,1,0:T(8,128)(2,1)}, bf16[8,160,768]{2,1,0:T(8,128)(2,1)}, bf16[2,160,768]{2,1,0:T(8,128)(2,1)S(1)}, bf16[8,160,768]{2,1,0:T(8,128)(2,1)}) custom-call(s32[5]{0:T(128)S(1)} %stack.23.at, f32[1]{0:T(128)S(6)} %copy.9.scale, f32[8,128]{1,0:T(8,128)S(1)} %add.190.row_sum, f32[8,128]{1,0:T(8,128)S(1)} %collective-permute-done.15.row_came, ...), custom_call_target="tpu_custom_call" | custom-call | flops 5637144576 | bytes 8388608 | tf_op jit(solution)/shard_map/pallas_call | solution.py:285
  108.7 1.9 %collective-permute-done.17 = bf16[2,160,768]{2,1,0:T(8,128)(2,1)S(1)} collective-permute-done((bf16[2,160,768]{2,1,0:T(8,128)(2,1)S(1)}, bf16[2,160,768]{2,1,0:T(8,128)(2,1)S(1)}, u32[]{:S(2)}, u32[]{:S(2)}) %collective-permute-start.17) | collective-permute-done | bytes 491552 | tf_op jit(solution)/shard_map/ppermute | solution.py:28
  110.7 1.2 add_convert_fusion.2
  111.8 2.0 %collective-permute-start.19 = (bf16[2,160,768]{2,1,0:T(8,128)(2,1)S(1)}, bf16[2,160,768]{2,1,0:T(8,128)(2,1)S(1)}, u32[]{:S(2)}, u32[]{:S(2)}) collective-permute-start(bf16[2,160,768]{2,1,0:T(8,128)(2,1)S(1)} %add_convert_fusion.2), channel_id=1, source_target_pairs={{0,56},{1,9},{8,16},{9,1},{16,8},{17,25},{24,32},{25,17},{32,24},{... | collective-permute-start | bytes 1474568 | tf_op jit(solution)/shard_map/ppermute | solution.py:39
  113.8 6.2 %all-to-all-start.2 = ((bf16[16,64,768]{2,1,0:T(8,128)(2,1)}), bf16[16,64,768]{2,1,0:T(8,128)(2,1)S(1)}, u32[]{:S(2)}, u32[]{:S(2)}) async-start(bf16[16,64,768]{2,1,0:T(8,128)(2,1)} %get-tuple-element.56), calls=%async_computation.2 | async-start | bytes 3145728 | tf_op jit(solution)/shard_map/all_to_all | solution.py:380
  120.0 1.9 %collective-permute-done.19 = bf16[2,160,768]{2,1,0:T(8,128)(2,1)S(1)} collective-permute-done((bf16[2,160,768]{2,1,0:T(8,128)(2,1)S(1)}, bf16[2,160,768]{2,1,0:T(8,128)(2,1)S(1)}, u32[]{:S(2)}, u32[]{:S(2)}) %collective-permute-start.19) | collective-permute-done | bytes 491552 | tf_op jit(solution)/shard_map/ppermute | solution.py:39
  122.0 1.4 add_convert_fusion.1
  123.4 8.8 %collective-permute-done.20 = bf16[2,160,768]{2,1,0:T(8,128)(2,1)S(1)} collective-permute-done((bf16[2,160,768]{2,1,0:T(8,128)(2,1)S(1)}, bf16[2,160,768]{2,1,0:T(8,128)(2,1)S(1)}, u32[]{:S(2)}, u32[]{:S(2)}) %collective-permute-start.20) | collective-permute-done | bytes 491552 | tf_op jit(solution)/shard_map/ppermute | solution.py:39
  132.2 1.4 add_convert_fusion
  133.6 2.0 %collective-permute-start.21 = (bf16[2,160,768]{2,1,0:T(8,128)(2,1)S(1)}, bf16[2,160,768]{2,1,0:T(8,128)(2,1)S(1)}, u32[]{:S(2)}, u32[]{:S(2)}) collective-permute-start(bf16[2,160,768]{2,1,0:T(8,128)(2,1)S(1)} %add_convert_fusion), channel_id=1, source_target_pairs={{0,56},{1,9},{8,16},{9,1},{16,8},{17,25},{24,32},{25,17},{32,24},{... | collective-permute-start | bytes 1474568 | tf_op jit(solution)/shard_map/ppermute | solution.py:39
  135.6 5.3 %all-to-all-done.2 = bf16[16,64,768]{2,1,0:T(8,128)(2,1)S(1)} async-done(((bf16[16,64,768]{2,1,0:T(8,128)(2,1)}), bf16[16,64,768]{2,1,0:T(8,128)(2,1)S(1)}, u32[]{:S(2)}, u32[]{:S(2)}) %all-to-all-start.2) | async-done | bytes 1572896 | tf_op jit(solution)/shard_map/all_to_all | solution.py:380
  140.9 2.8 %collective-permute-done.21 = bf16[2,160,768]{2,1,0:T(8,128)(2,1)S(1)} collective-permute-done((bf16[2,160,768]{2,1,0:T(8,128)(2,1)S(1)}, bf16[2,160,768]{2,1,0:T(8,128)(2,1)S(1)}, u32[]{:S(2)}, u32[]{:S(2)}) %collective-permute-start.21) | collective-permute-done | bytes 491552 | tf_op jit(solution)/shard_map/ppermute | solution.py:39
  143.7 1.3 convert_add_fusion
  145.1 0.6 collective-permute-start.22
  145.9 5.5 %collective-permute-done.22 = bf16[160,768]{1,0:T(8,128)(2,1)S(1)} collective-permute-done((bf16[160,768]{1,0:T(8,128)(2,1)S(1)}, bf16[160,768]{1,0:T(8,128)(2,1)S(1)}, u32[]{:S(2)}, u32[]{:S(2)}) %collective-permute-start.22) | collective-permute-done | bytes 245792 | tf_op jit(solution)/shard_map/ppermute | solution.py:39
  151.6 0.8 reshape.109
  152.4 8.2 %all-to-all-start.3 = ((f32[16,6,768]{2,1,0:T(8,128)}), f32[16,6,768]{2,1,0:T(8,128)S(1)}, u32[]{:S(2)}, u32[]{:S(2)}) async-start(f32[16,6,768]{2,1,0:T(8,128)} %reshape.109), calls=%async_computation.3 | async-start | bytes 786432 | tf_op jit(solution)/shard_map/all_to_all | solution.py:393
  160.6 1.7 fusion.6
  162.2 6.4 %all-to-all-done.3 = f32[16,6,768]{2,1,0:T(8,128)S(1)} async-done(((f32[16,6,768]{2,1,0:T(8,128)}), f32[16,6,768]{2,1,0:T(8,128)S(1)}, u32[]{:S(2)}, u32[]{:S(2)}) %all-to-all-start.3) | async-done | bytes 294944 | tf_op jit(solution)/shard_map/all_to_all | solution.py:393
  168.6 0.6 broadcast_in_dim.27
  (55 shorter events, 2.4 us)
Async XLA Ops:
  0.6 0.9 copy-start
  2.2 10.2 %collective-permute-start = (bf16[64,768]{1,0:T(8,128)(2,1)S(1)}, bf16[64,768]{1,0:T(8,128)(2,1)S(1)}, u32[]{:S(2)}, u32[]{:S(2)}) collective-permute-start(bf16[64,768]{1,0:T(8,128)(2,1)S(1)} %dynamic-slice_bitcast_fusion), channel_id=1, source_target_pairs={{0,128},{128,0},{1,129},{129,1},{2,130},{130,2},{3,131},{131,3},{4... | collective-permute-start | bytes 294920 | tf_op jit(solution)/shard_map/ppermute | solution.py:28
  5.3 14.2 %all-to-all-start.1 = ((bf16[16,6,768]{2,1,0:T(8,128)(2,1)}), bf16[16,6,768]{2,1,0:T(8,128)(2,1)S(1)}, u32[]{:S(2)}, u32[]{:S(2)}) async-start(bf16[16,6,768]{2,1,0:T(8,128)(2,1)} %broadcast_in_dim.12), calls=%async_computation.1 | async-start | bytes 393216 | tf_op jit(solution)/shard_map/all_to_all | solution.py:59
  19.5 6.3 %collective-permute-start.1 = (bf16[160,768]{1,0:T(8,128)(2,1)S(1)}, bf16[160,768]{1,0:T(8,128)(2,1)S(1)}, u32[]{:S(2)}, u32[]{:S(2)}) collective-permute-start(bf16[160,768]{1,0:T(8,128)(2,1)S(1)} %pad_maximum_fusion), channel_id=1, source_target_pairs={{0,8},{1,57},{8,0},{9,17},{16,24},{17,9},{24,16},{25,33},{32,40},{... | collective-permute-start | bytes 737288 | tf_op jit(solution)/shard_map/ppermute | solution.py:39
  25.8 12.8 %collective-permute-start.2 = (bf16[320,768]{1,0:T(8,128)(2,1)S(1)}, bf16[320,768]{1,0:T(8,128)(2,1)S(1)}, u32[]{:S(2)}, u32[]{:S(2)}) collective-permute-start(bf16[320,768]{1,0:T(8,128)(2,1)S(1)} %constant_dynamic-update-slice_fusion.refs_0_), channel_id=1, source_target_pairs={{0,56},{1,9},{8,16},{9,1},{16,8},{17,25},{24,32},{25,17},{32,24},{... | collective-permute-start | bytes 1474568 | tf_op jit(solution)/shard_map/ppermute | solution.py:39
  31.8 27.1 %all-to-all-start = ((bf16[16,64,768]{2,1,0:T(8,128)(2,1)}), bf16[16,64,768]{2,1,0:T(8,128)(2,1)}, u32[]{:S(2)}, u32[]{:S(2)}) async-start(bf16[16,64,768]{2,1,0:T(8,128)(2,1)} %broadcast_in_dim.10), calls=%async_computation | async-start | bytes 3145728 | tf_op jit(solution)/shard_map/all_to_all | solution.py:333
  38.6 9.3 %collective-permute-start.3 = (bf16[320,768]{1,0:T(8,128)(2,1)S(1)}, bf16[320,768]{1,0:T(8,128)(2,1)S(1)}, u32[]{:S(2)}, u32[]{:S(2)}) collective-permute-start(bf16[320,768]{1,0:T(8,128)(2,1)S(1)} %collective-permute-done.2.refs_1_), channel_id=1, source_target_pairs={{0,8},{1,57},{8,0},{9,17},{16,24},{17,9},{24,16},{25,33},{32,40},{... | collective-permute-start | bytes 1474568 | tf_op jit(solution)/shard_map/ppermute | solution.py:39
  47.8 10.3 %collective-permute-start.4 = (bf16[320,768]{1,0:T(8,128)(2,1)S(1)}, bf16[320,768]{1,0:T(8,128)(2,1)S(1)}, u32[]{:S(2)}, u32[]{:S(2)}) collective-permute-start(bf16[320,768]{1,0:T(8,128)(2,1)S(1)} %collective-permute-done.3.refs_2_), channel_id=1, source_target_pairs={{0,56},{1,9},{8,16},{9,1},{16,8},{17,25},{24,32},{25,17},{32,24},{... | collective-permute-start | bytes 1474568 | tf_op jit(solution)/shard_map/ppermute | solution.py:39
  51.3 7.6 %collective-permute-start.5 = (bf16[320,768]{1,0:T(8,128)(2,1)S(1)}, bf16[320,768]{1,0:T(8,128)(2,1)S(1)}, u32[]{:S(2)}, u32[]{:S(2)}) collective-permute-start(bf16[320,768]{1,0:T(8,128)(2,1)S(1)} %constant_dynamic-update-slice_fusion.refs_0_), channel_id=1, source_target_pairs={{0,1},{1,0},{2,3},{3,2},{4,5},{5,4},{6,7},{7,6},{8,9},{9,8},{10,11... | collective-permute-start | bytes 1474568 | tf_op jit(solution)/shard_map/ppermute | solution.py:28
  51.3 7.6 %collective-permute-start.6 = (bf16[320,768]{1,0:T(8,128)(2,1)S(1)}, bf16[320,768]{1,0:T(8,128)(2,1)S(1)}, u32[]{:S(2)}, u32[]{:S(2)}) collective-permute-start(bf16[320,768]{1,0:T(8,128)(2,1)S(1)} %collective-permute-done.2.refs_1_), channel_id=1, source_target_pairs={{0,1},{1,0},{2,3},{3,2},{4,5},{5,4},{6,7},{7,6},{8,9},{9,8},{10,11... | collective-permute-start | bytes 1474568 | tf_op jit(solution)/shard_map/ppermute | solution.py:28
  51.8 7.1 %collective-permute-start.7 = (bf16[320,768]{1,0:T(8,128)(2,1)S(1)}, bf16[320,768]{1,0:T(8,128)(2,1)}, u32[]{:S(2)}, u32[]{:S(2)}) collective-permute-start(bf16[320,768]{1,0:T(8,128)(2,1)S(1)} %collective-permute-done.3.refs_2_), channel_id=1, source_target_pairs={{0,1},{1,0},{2,3},{3,2},{4,5},{5,4},{6,7},{7,6},{8,9},{9,8},{10,11... | collective-permute-start | bytes 1474568 | tf_op jit(solution)/shard_map/ppermute | solution.py:28
  58.1 2.0 %collective-permute-start.8 = (bf16[320,768]{1,0:T(8,128)(2,1)S(1)}, bf16[320,768]{1,0:T(8,128)(2,1)}, u32[]{:S(2)}, u32[]{:S(2)}) collective-permute-start(bf16[320,768]{1,0:T(8,128)(2,1)S(1)} %collective-permute-done.4.refs_3_), channel_id=1, source_target_pairs={{0,1},{1,0},{2,3},{3,2},{4,5},{5,4},{6,7},{7,6},{8,9},{9,8},{10,11... | collective-permute-start | bytes 1474568 | tf_op jit(solution)/shard_map/ppermute | solution.py:28
  58.9 23.6 %copy-start.1 = (s32[16384]{0:T(1024)S(1)}, s32[16384]{0:T(1024)}, u32[]{:S(2)}) copy-start(s32[16384]{0:T(1024)} %param.6) | copy-start | bytes 196612
  58.9 1.3 copy-start.2
  58.9 1.2 copy-start.3
  71.6 3.7 %collective-permute-start.9 = (f32[8,128]{1,0:T(8,128)S(1)}, f32[8,128]{1,0:T(8,128)S(1)}, u32[]{:S(2)}, u32[]{:S(2)}) collective-permute-start(f32[8,128]{1,0:T(8,128)S(1)} %get-tuple-element.33), channel_id=1, source_target_pairs={{0,2},{2,0},{4,6},{6,4},{1,3},{3,1},{5,7},{7,5},{8,10},{10,8},{12,... | collective-permute-start | bytes 12296 | tf_op jit(solution)/shard_map/ppermute | solution.py:28
  73.1 2.1 %collective-permute-start.10 = (f32[8,128]{1,0:T(8,128)S(1)}, f32[8,128]{1,0:T(8,128)S(1)}, u32[]{:S(2)}, u32[]{:S(2)}) collective-permute-start(f32[8,128]{1,0:T(8,128)S(1)} %get-tuple-element.34), channel_id=1, source_target_pairs={{0,1},{1,0},{2,3},{3,2},{4,5},{5,4},{6,7},{7,6},{8,9},{9,8},{10,11... | collective-permute-start | bytes 12296 | tf_op jit(solution)/shard_map/ppermute | solution.py:28
  75.3 4.9 %collective-permute-start.12 = (f32[8,128]{1,0:T(8,128)S(1)}, f32[8,128]{1,0:T(8,128)S(1)}, u32[]{:S(2)}, u32[]{:S(2)}) collective-permute-start(f32[8,128]{1,0:T(8,128)S(1)} %add.187), channel_id=1, source_target_pairs={{0,56},{1,9},{8,16},{9,1},{16,8},{17,25},{24,32},{25,17},{32,24},{... | collective-permute-start | bytes 12296 | tf_op jit(solution)/shard_map/ppermute | solution.py:39
  78.6 3.6 %collective-permute-start.11 = (f32[8,128]{1,0:T(8,128)S(1)}, f32[8,128]{1,0:T(8,128)S(1)}, u32[]{:S(2)}, u32[]{:S(2)}) collective-permute-start(f32[8,128]{1,0:T(8,128)S(1)} %add.186), channel_id=1, source_target_pairs={{0,6},{2,4},{4,2},{6,0},{1,7},{3,5},{5,3},{7,1},{8,14},{10,12},{12... | collective-permute-start | bytes 12296 | tf_op jit(solution)/shard_map/ppermute | solution.py:28
  82.2 3.6 %collective-permute-start.14 = (f32[8,128]{1,0:T(8,128)S(1)}, f32[8,128]{1,0:T(8,128)S(1)}, u32[]{:S(2)}, u32[]{:S(2)}) collective-permute-start(f32[8,128]{1,0:T(8,128)S(1)} %add.189), channel_id=1, source_target_pairs={{0,8},{1,57},{8,0},{9,17},{16,24},{17,9},{24,16},{25,33},{32,40},{... | collective-permute-start | bytes 12296 | tf_op jit(solution)/shard_map/ppermute | solution.py:39
  82.2 3.7 %collective-permute-start.13 = (f32[8,128]{1,0:T(8,128)S(1)}, f32[8,128]{1,0:T(8,128)S(1)}, u32[]{:S(2)}, u32[]{:S(2)}) collective-permute-start(f32[8,128]{1,0:T(8,128)S(1)} %add.188), channel_id=1, source_target_pairs={{0,128},{64,192},{128,0},{192,64},{1,129},{65,193},{129,1},{193,65... | collective-permute-start | bytes 12296 | tf_op jit(solution)/shard_map/ppermute | solution.py:28
  85.9 6.7 %collective-permute-start.16 = (f32[8,128]{1,0:T(8,128)S(1)}, f32[8,128]{1,0:T(8,128)S(1)}, u32[]{:S(2)}, u32[]{:S(2)}) collective-permute-start(f32[8,128]{1,0:T(8,128)S(1)} %add.191.col_sum), channel_id=1, source_target_pairs={{0,40},{1,25},{8,32},{9,49},{16,56},{17,41},{24,48},{25,1},{32,8},... | collective-permute-start | bytes 12296 | tf_op jit(solution)/shard_map/ppermute | solution.py:49
  89.0 4.8 %collective-permute-start.15 = (f32[8,128]{1,0:T(8,128)S(1)}, f32[8,128]{1,0:T(8,128)S(1)}, u32[]{:S(2)}, u32[]{:S(2)}) collective-permute-start(f32[8,128]{1,0:T(8,128)S(1)} %add.190.row_sum), channel_id=1, source_target_pairs={{0,192},{64,128},{128,64},{192,0},{1,193},{65,129},{129,65},{193,1... | collective-permute-start | bytes 12296 | tf_op jit(solution)/shard_map/ppermute | solution.py:28
  108.4 2.2 %collective-permute-start.17 = (bf16[2,160,768]{2,1,0:T(8,128)(2,1)S(1)}, bf16[2,160,768]{2,1,0:T(8,128)(2,1)S(1)}, u32[]{:S(2)}, u32[]{:S(2)}) collective-permute-start(bf16[2,160,768]{2,1,0:T(8,128)(2,1)S(1)} %get-tuple-element.52), channel_id=1, source_target_pairs={{0,1},{1,0},{2,3},{3,2},{4,5},{5,4},{6,7},{7,6},{8,9},{9,8},{10,11... | collective-permute-start | bytes 1474568 | tf_op jit(solution)/shard_map/ppermute | solution.py:28
  110.5 11.4 %collective-permute-start.18 = (bf16[8,160,768]{2,1,0:T(8,128)(2,1)}, bf16[8,160,768]{2,1,0:T(8,128)(2,1)}, u32[]{:S(2)}, u32[]{:S(2)}) collective-permute-start(bf16[8,160,768]{2,1,0:T(8,128)(2,1)} %get-tuple-element.54), channel_id=1, source_target_pairs={{0,1},{1,0},{2,3},{3,2},{4,5},{5,4},{6,7},{7,6},{8,9},{9,8},{10,11... | collective-permute-start | bytes 5898248 | tf_op jit(solution)/shard_map/ppermute | solution.py:28
  111.8 10.1 %collective-permute-start.19 = (bf16[2,160,768]{2,1,0:T(8,128)(2,1)S(1)}, bf16[2,160,768]{2,1,0:T(8,128)(2,1)S(1)}, u32[]{:S(2)}, u32[]{:S(2)}) collective-permute-start(bf16[2,160,768]{2,1,0:T(8,128)(2,1)S(1)} %add_convert_fusion.2), channel_id=1, source_target_pairs={{0,56},{1,9},{8,16},{9,1},{16,8},{17,25},{24,32},{25,17},{32,24},{... | collective-permute-start | bytes 1474568 | tf_op jit(solution)/shard_map/ppermute | solution.py:39
  113.8 27.1 %all-to-all-start.2 = ((bf16[16,64,768]{2,1,0:T(8,128)(2,1)}), bf16[16,64,768]{2,1,0:T(8,128)(2,1)S(1)}, u32[]{:S(2)}, u32[]{:S(2)}) async-start(bf16[16,64,768]{2,1,0:T(8,128)(2,1)} %get-tuple-element.56), calls=%async_computation.2 | async-start | bytes 3145728 | tf_op jit(solution)/shard_map/all_to_all | solution.py:380
  123.3 8.9 %collective-permute-start.20 = (bf16[2,160,768]{2,1,0:T(8,128)(2,1)S(1)}, bf16[2,160,768]{2,1,0:T(8,128)(2,1)S(1)}, u32[]{:S(2)}, u32[]{:S(2)}) collective-permute-start(bf16[2,160,768]{2,1,0:T(8,128)(2,1)S(1)} %add_convert_fusion.1), channel_id=1, source_target_pairs={{0,8},{1,57},{8,0},{9,17},{16,24},{17,9},{24,16},{25,33},{32,40},{... | collective-permute-start | bytes 1474568 | tf_op jit(solution)/shard_map/ppermute | solution.py:39
  133.6 10.1 %collective-permute-start.21 = (bf16[2,160,768]{2,1,0:T(8,128)(2,1)S(1)}, bf16[2,160,768]{2,1,0:T(8,128)(2,1)S(1)}, u32[]{:S(2)}, u32[]{:S(2)}) collective-permute-start(bf16[2,160,768]{2,1,0:T(8,128)(2,1)S(1)} %add_convert_fusion), channel_id=1, source_target_pairs={{0,56},{1,9},{8,16},{9,1},{16,8},{17,25},{24,32},{25,17},{32,24},{... | collective-permute-start | bytes 1474568 | tf_op jit(solution)/shard_map/ppermute | solution.py:39
  145.1 6.3 %collective-permute-start.22 = (bf16[160,768]{1,0:T(8,128)(2,1)S(1)}, bf16[160,768]{1,0:T(8,128)(2,1)S(1)}, u32[]{:S(2)}, u32[]{:S(2)}) collective-permute-start(bf16[160,768]{1,0:T(8,128)(2,1)S(1)} %fusion.9), channel_id=1, source_target_pairs={{0,8},{1,57},{8,0},{9,17},{16,24},{17,9},{24,16},{25,33},{32,40},{... | collective-permute-start | bytes 737288 | tf_op jit(solution)/shard_map/ppermute | solution.py:39
  145.9 14.6 %copy-start.4 = (bf16[2,8,48,768]{3,2,1,0:T(8,128)(2,1)S(1)}, bf16[2,8,48,768]{3,2,1,0:T(8,128)(2,1)}, u32[]{:S(2)}) copy-start(bf16[2,8,48,768]{3,2,1,0:T(8,128)(2,1)} %get-tuple-element.59) | copy-start | bytes 3538948
  151.5 9.1 %collective-permute-start.23 = (bf16[64,768]{1,0:T(8,128)(2,1)S(1)}, bf16[64,768]{1,0:T(8,128)(2,1)S(1)}, u32[]{:S(2)}, u32[]{:S(2)}) collective-permute-start(bf16[64,768]{1,0:T(8,128)(2,1)S(1)} %get-tuple-element.61), channel_id=1, source_target_pairs={{0,128},{128,0},{1,129},{129,1},{2,130},{130,2},{3,131},{131,3},{4... | collective-permute-start | bytes 294920 | tf_op jit(solution)/shard_map/ppermute | solution.py:28
  152.4 16.2 %all-to-all-start.3 = ((f32[16,6,768]{2,1,0:T(8,128)}), f32[16,6,768]{2,1,0:T(8,128)S(1)}, u32[]{:S(2)}, u32[]{:S(2)}) async-start(f32[16,6,768]{2,1,0:T(8,128)} %reshape.109), calls=%async_computation.3 | async-start | bytes 786432 | tf_op jit(solution)/shard_map/all_to_all | solution.py:393

commit v3 on v2

--- a/solution.py
+++ b/solution.py
@@ -381,12 +381,13 @@
     far, send = stage(mirror(far, ("c",)), send)
     mine = wider(keep[6:]) + wider(far)
     send = mirror(send, ("c",))
-    for step, first in ((1, 4), (0, 2), (1, 0)):
+    for step, first in ((1, 4), (0, 2)):
         came = pair(mine.astype(BF16), step)
-        if first == 0:
-            came, d_image = stage(came, d_image)
         mine = wider(keep[first : first + 2]) + wider(send[first : first + 2]) + wider(came)
-    sums = mine[0] + wider(pair(mine[1].astype(BF16), 0))
+    came, d_image = stage(pair(mine.astype(BF16), 1), d_image)
+    mine = wider(keep[1]) + wider(send[1]) + wider(came[1])
+    last, came = stage(pair(mine.astype(BF16), 0), came)
+    sums = wider(keep[0]) + wider(send[0]) + wider(came[0]) + wider(last)
     d_image = jnp.sum(wider(d_image), axis=0)
     d_modal = sums[2 * band :]
     d_weight = sums[: 2 * band].reshape(16, band // 8, width)

time: 170 us -> 171 us (level)
    convert_element_type x0 -> x2, other arithmetic: none -> 2.53 us  [the longest x1 1.36 us: per_device(): came, d_image = stage(pair(mine.astype(BF16), 1), d_image)]
    convert_element_type x3 -> x2, other arithmetic: 3.89 us -> 2.53 us  [per_device(): came = pair(mine.astype(BF16), step)]
where the time goes in v3:
time: 171 us; the launch traced here: 170 us
  waiting for transfers between devices  72.1 us (42%)
  starting transfers between devices  56.2 us (33%)
  Pallas kernels  25.9 us (15%)
  other arithmetic  6.63 us (4%)
  local copies, waits for them, and re-layouts  5.47 us (3%)
  matrix products  2.26 us (1%)
    ppermute x10, waiting for transfers between devices, pair(): return lax.ppermute(value, ('z', 'c'), route)  44.3 us
    pallas_call x2, Pallas kernels, call(): pl.pallas_call(kernel, in_specs=[smem, smem] + [spaces[own] for _, own in...  25.9 us
    ppermute x10, starting transfers between devices, pair(): return lax.ppermute(value, ('z', 'c'), route)  19.4 us
    ppermute x13, waiting for transfers between devices, mirror(): lax.ppermute(value, axes, [(i, i ^ mask) for i in range(count(axes))])  8.58 us
    all_to_all x1, starting transfers between devices, per_device(): lax.all_to_all(d_weight, PLANE, 0, 0)  8.15 us
    all_to_all x1, starting transfers between devices, gather(): return lax.all_to_all(copies, axes, 0, 0)  7.18 us
    ppermute x13, starting transfers between devices, mirror(): lax.ppermute(value, axes, [(i, i ^ mask) for i in range(count(axes))])  6.53 us
    all_to_all x1, waiting for transfers between devices, per_device(): lax.all_to_all(d_weight, PLANE, 0, 0)  6.36 us
  transfers between devices with their start and end apart: 28, of which 20 were waited for; matrix products, arithmetic and copies ran while one was open for 6% of the time, Pallas kernels for 0%

profile of v3, /device:TPU:2, one launch (start us, length us, event | category | flops | bytes accessed | tf_op | source)
XLA Modules:
  0.0 170.2 jit_solution(15764927174075325468)
XLA Ops:
  0.7 0.9 copy-done
  1.6 0.6 fusion.4
  2.2 1.7 collective-permute-start
  3.9 1.4 broadcast_in_dim.12
  5.3 7.2 %all-to-all-start.1 = ((bf16[16,6,768]{2,1,0:T(8,128)(2,1)}), bf16[16,6,768]{2,1,0:T(8,128)(2,1)S(1)}, u32[]{:S(2)}, u32[]{:S(2)}) async-start(bf16[16,6,768]{2,1,0:T(8,128)(2,1)} %broadcast_in_dim.12), calls=%async_computation.1 | async-start | bytes 393216 | tf_op jit(solution)/shard_map/all_to_all | solution.py:59
  12.5 1.3 broadcast_in_dim.10
  13.8 5.6 %all-to-all-done.1 = bf16[16,6,768]{2,1,0:T(8,128)(2,1)S(1)} async-done(((bf16[16,6,768]{2,1,0:T(8,128)(2,1)}), bf16[16,6,768]{2,1,0:T(8,128)(2,1)S(1)}, u32[]{:S(2)}, u32[]{:S(2)}) %all-to-all-start.1) | async-done | bytes 147488 | tf_op jit(solution)/shard_map/all_to_all | solution.py:59
  19.5 2.0 %collective-permute-start.1 = (bf16[160,768]{1,0:T(8,128)(2,1)S(1)}, bf16[160,768]{1,0:T(8,128)(2,1)S(1)}, u32[]{:S(2)}, u32[]{:S(2)}) collective-permute-start(bf16[160,768]{1,0:T(8,128)(2,1)S(1)} %pad_maximum_fusion), channel_id=1, source_target_pairs={{0,8},{1,57},{8,0},{9,17},{16,24},{17,9},{24,16},{25,33},{32,40},{... | collective-permute-start | bytes 737288 | tf_op jit(solution)/shard_map/ppermute | solution.py:39
  21.5 4.3 %collective-permute-done.1 = bf16[160,768]{1,0:T(8,128)(2,1)S(1)} collective-permute-done((bf16[160,768]{1,0:T(8,128)(2,1)S(1)}, bf16[160,768]{1,0:T(8,128)(2,1)S(1)}, u32[]{:S(2)}, u32[]{:S(2)}) %collective-permute-start.1) | collective-permute-done | bytes 245792 | tf_op jit(solution)/shard_map/ppermute | solution.py:39
  25.8 5.9 %collective-permute-start.2 = (bf16[320,768]{1,0:T(8,128)(2,1)S(1)}, bf16[320,768]{1,0:T(8,128)(2,1)S(1)}, u32[]{:S(2)}, u32[]{:S(2)}) collective-permute-start(bf16[320,768]{1,0:T(8,128)(2,1)S(1)} %constant_dynamic-update-slice_fusion.refs_0_), channel_id=1, source_target_pairs={{0,56},{1,9},{8,16},{9,1},{16,8},{17,25},{24,32},{25,17},{32,24},{... | collective-permute-start | bytes 1474568 | tf_op jit(solution)/shard_map/ppermute | solution.py:39
  31.8 5.6 %all-to-all-start = ((bf16[16,64,768]{2,1,0:T(8,128)(2,1)}), bf16[16,64,768]{2,1,0:T(8,128)(2,1)}, u32[]{:S(2)}, u32[]{:S(2)}) async-start(bf16[16,64,768]{2,1,0:T(8,128)(2,1)} %broadcast_in_dim.10), calls=%async_computation | async-start | bytes 3145728 | tf_op jit(solution)/shard_map/all_to_all | solution.py:333
  37.4 1.2 collective-permute-done.2.refs_1_
  38.6 9.3 %collective-permute-done.3.refs_2_ = bf16[320,768]{1,0:T(8,128)(2,1)S(1)} collective-permute-done((bf16[320,768]{1,0:T(8,128)(2,1)S(1)}, bf16[320,768]{1,0:T(8,128)(2,1)S(1)}, u32[]{:S(2)}, u32[]{:S(2)}) %collective-permute-start.3) | collective-permute-done | bytes 491552 | tf_op jit(solution)/shard_map/ppermute | solution.py:39
  47.8 3.5 %collective-permute-start.4 = (bf16[320,768]{1,0:T(8,128)(2,1)S(1)}, bf16[320,768]{1,0:T(8,128)(2,1)S(1)}, u32[]{:S(2)}, u32[]{:S(2)}) collective-permute-start(bf16[320,768]{1,0:T(8,128)(2,1)S(1)} %collective-permute-done.3.refs_2_), channel_id=1, source_target_pairs={{0,56},{1,9},{8,16},{9,1},{16,8},{17,25},{24,32},{25,17},{32,24},{... | collective-permute-start | bytes 1474568 | tf_op jit(solution)/shard_map/ppermute | solution.py:39
  51.8 6.3 %collective-permute-done.4.refs_3_ = bf16[320,768]{1,0:T(8,128)(2,1)S(1)} collective-permute-done((bf16[320,768]{1,0:T(8,128)(2,1)S(1)}, bf16[320,768]{1,0:T(8,128)(2,1)S(1)}, u32[]{:S(2)}, u32[]{:S(2)}) %collective-permute-start.4) | collective-permute-done | bytes 491552 | tf_op jit(solution)/shard_map/ppermute | solution.py:39
  58.9 1.2 collective-permute-done.8.refs_7_
  60.1 11.4 %shard_map.59 = (f32[8,128]{1,0:T(8,128)S(1)}, f32[8,128]{1,0:T(8,128)S(1)}, f32[1,1024]{1,0:T(1,128)S(1)}, f32[1,1024]{1,0:T(1,128)S(1)}, bf16[16,64,768]{2,1,0...) custom-call(s32[5]{0:T(128)S(1)} %stack.23.at, ...), custom_call_target="tpu_custom_call" | custom-call | flops 4026531840 | bytes 8388608 | tf_op jit(solution)/shard_map/pallas_call | solution.py:285
  71.6 1.6 collective-permute-start.9
  73.1 2.1 %collective-permute-done.9 = f32[8,128]{1,0:T(8,128)S(1)} collective-permute-done((f32[8,128]{1,0:T(8,128)S(1)}, f32[8,128]{1,0:T(8,128)S(1)}, u32[]{:S(2)}, u32[]{:S(2)}) %collective-permute-start.9) | collective-permute-done | bytes 4128 | tf_op jit(solution)/shard_map/ppermute | solution.py:28
  75.3 3.3 %collective-permute-start.12 = (f32[8,128]{1,0:T(8,128)S(1)}, f32[8,128]{1,0:T(8,128)S(1)}, u32[]{:S(2)}, u32[]{:S(2)}) collective-permute-start(f32[8,128]{1,0:T(8,128)S(1)} %add.199), channel_id=1, source_target_pairs={{0,56},{1,9},{8,16},{9,1},{16,8},{17,25},{24,32},{25,17},{32,24},{... | collective-permute-start | bytes 12296 | tf_op jit(solution)/shard_map/ppermute | solution.py:39
  79.2 1.0 collective-permute-done.12
  80.2 2.0 %collective-permute-done.11 = f32[8,128]{1,0:T(8,128)S(1)} collective-permute-done((f32[8,128]{1,0:T(8,128)S(1)}, f32[8,128]{1,0:T(8,128)S(1)}, u32[]{:S(2)}, u32[]{:S(2)}) %collective-permute-start.11) | collective-permute-done | bytes 4128 | tf_op jit(solution)/shard_map/ppermute | solution.py:28
  82.6 3.2 %collective-permute-done.14 = f32[8,128]{1,0:T(8,128)S(1)} collective-permute-done((f32[8,128]{1,0:T(8,128)S(1)}, f32[8,128]{1,0:T(8,128)S(1)}, u32[]{:S(2)}, u32[]{:S(2)}) %collective-permute-start.14) | collective-permute-done | bytes 4128 | tf_op jit(solution)/shard_map/ppermute | solution.py:39
  85.9 3.1 %collective-permute-start.16 = (f32[8,128]{1,0:T(8,128)S(1)}, f32[8,128]{1,0:T(8,128)S(1)}, u32[]{:S(2)}, u32[]{:S(2)}) collective-permute-start(f32[8,128]{1,0:T(8,128)S(1)} %add.203.col_sum), channel_id=1, source_target_pairs={{0,40},{1,25},{8,32},{9,49},{16,56},{17,41},{24,48},{25,1},{32,8},... | collective-permute-start | bytes 12296 | tf_op jit(solution)/shard_map/ppermute | solution.py:49
  89.0 1.4 collective-permute-start.15
  90.5 2.1 %collective-permute-done.16.col_came = f32[8,128]{1,0:T(8,128)S(1)} collective-permute-done((f32[8,128]{1,0:T(8,128)S(1)}, f32[8,128]{1,0:T(8,128)S(1)}, u32[]{:S(2)}, u32[]{:S(2)}) %collective-permute-start.16) | collective-permute-done | bytes 4128 | tf_op jit(solution)/shard_map/ppermute | solution.py:49
  92.6 1.3 collective-permute-done.15.row_came
  93.8 14.5 %shard_map.60 = (bf16[16,64,768]{2,1,0:T(8,128)(2,1)}, bf16[8,160,768]{2,1,0:T(8,128)(2,1)}, bf16[2,160,768]{2,1,0:T(8,128)(2,1)S(1)}, bf16[8,160,768]{2,1,0:T(8,128)(2,1)}) custom-call(s32[5]{0:T(128)S(1)} %stack.23.at, f32[1]{0:T(128)S(6)} %copy.9.scale, f32[8,128]{1,0:T(8,128)S(1)} %add.202.row_sum, f32[8,128]{1,0:T(8,128)S(1)} %collective-permute-done.15.row_came, ...), custom_call_target="tpu_custom_call" | custom-call | flops 5637144576 | bytes 8388608 | tf_op jit(solution)/shard_map/pallas_call | solution.py:285
  108.7 1.9 %collective-permute-done.17 = bf16[2,160,768]{2,1,0:T(8,128)(2,1)S(1)} collective-permute-done((bf16[2,160,768]{2,1,0:T(8,128)(2,1)S(1)}, bf16[2,160,768]{2,1,0:T(8,128)(2,1)S(1)}, u32[]{:S(2)}, u32[]{:S(2)}) %collective-permute-start.17) | collective-permute-done | bytes 491552 | tf_op jit(solution)/shard_map/ppermute | solution.py:28
  110.7 1.2 add_convert_fusion.2
  111.8 2.0 %collective-permute-start.19 = (bf16[2,160,768]{2,1,0:T(8,128)(2,1)S(1)}, bf16[2,160,768]{2,1,0:T(8,128)(2,1)S(1)}, u32[]{:S(2)}, u32[]{:S(2)}) collective-permute-start(bf16[2,160,768]{2,1,0:T(8,128)(2,1)S(1)} %add_convert_fusion.2), channel_id=1, source_target_pairs={{0,56},{1,9},{8,16},{9,1},{16,8},{17,25},{24,32},{25,17},{32,24},{... | collective-permute-start | bytes 1474568 | tf_op jit(solution)/shard_map/ppermute | solution.py:39
  113.8 6.2 %all-to-all-start.2 = ((bf16[16,64,768]{2,1,0:T(8,128)(2,1)}), bf16[16,64,768]{2,1,0:T(8,128)(2,1)S(1)}, u32[]{:S(2)}, u32[]{:S(2)}) async-start(bf16[16,64,768]{2,1,0:T(8,128)(2,1)} %get-tuple-element.58), calls=%async_computation.2 | async-start | bytes 3145728 | tf_op jit(solution)/shard_map/all_to_all | solution.py:380
  120.0 1.9 %collective-permute-done.19 = bf16[2,160,768]{2,1,0:T(8,128)(2,1)S(1)} collective-permute-done((bf16[2,160,768]{2,1,0:T(8,128)(2,1)S(1)}, bf16[2,160,768]{2,1,0:T(8,128)(2,1)S(1)}, u32[]{:S(2)}, u32[]{:S(2)}) %collective-permute-start.19) | collective-permute-done | bytes 491552 | tf_op jit(solution)/shard_map/ppermute | solution.py:39
  122.0 1.4 add_convert_fusion.1
  123.4 8.8 %collective-permute-done.20 = bf16[2,160,768]{2,1,0:T(8,128)(2,1)S(1)} collective-permute-done((bf16[2,160,768]{2,1,0:T(8,128)(2,1)S(1)}, bf16[2,160,768]{2,1,0:T(8,128)(2,1)S(1)}, u32[]{:S(2)}, u32[]{:S(2)}) %collective-permute-start.20) | collective-permute-done | bytes 491552 | tf_op jit(solution)/shard_map/ppermute | solution.py:39
  132.2 1.4 add_convert_fusion
  133.6 2.0 %collective-permute-start.21 = (bf16[2,160,768]{2,1,0:T(8,128)(2,1)S(1)}, bf16[2,160,768]{2,1,0:T(8,128)(2,1)S(1)}, u32[]{:S(2)}, u32[]{:S(2)}) collective-permute-start(bf16[2,160,768]{2,1,0:T(8,128)(2,1)S(1)} %add_convert_fusion), channel_id=1, source_target_pairs={{0,56},{1,9},{8,16},{9,1},{16,8},{17,25},{24,32},{25,17},{32,24},{... | collective-permute-start | bytes 1474568 | tf_op jit(solution)/shard_map/ppermute | solution.py:39
  135.6 5.3 %all-to-all-done.2 = bf16[16,64,768]{2,1,0:T(8,128)(2,1)S(1)} async-done(((bf16[16,64,768]{2,1,0:T(8,128)(2,1)}), bf16[16,64,768]{2,1,0:T(8,128)(2,1)S(1)}, u32[]{:S(2)}, u32[]{:S(2)}) %all-to-all-start.2) | async-done | bytes 1572896 | tf_op jit(solution)/shard_map/all_to_all | solution.py:380
  140.9 2.8 %collective-permute-done.21 = bf16[2,160,768]{2,1,0:T(8,128)(2,1)S(1)} collective-permute-done((bf16[2,160,768]{2,1,0:T(8,128)(2,1)S(1)}, bf16[2,160,768]{2,1,0:T(8,128)(2,1)S(1)}, u32[]{:S(2)}, u32[]{:S(2)}) %collective-permute-start.21) | collective-permute-done | bytes 491552 | tf_op jit(solution)/shard_map/ppermute | solution.py:39
  143.7 1.2 fusion.8
  144.9 0.6 collective-permute-start.22
  145.7 5.5 %collective-permute-done.22 = bf16[160,768]{1,0:T(8,128)(2,1)S(1)} collective-permute-done((bf16[160,768]{1,0:T(8,128)(2,1)S(1)}, bf16[160,768]{1,0:T(8,128)(2,1)S(1)}, u32[]{:S(2)}, u32[]{:S(2)}) %collective-permute-start.22) | collective-permute-done | bytes 245792 | tf_op jit(solution)/shard_map/ppermute | solution.py:39
  151.2 1.2 bitcast_add_fusion
  152.5 0.8 reshape.119
  153.3 8.2 %all-to-all-start.3 = ((f32[16,6,768]{2,1,0:T(8,128)}), f32[16,6,768]{2,1,0:T(8,128)S(1)}, u32[]{:S(2)}, u32[]{:S(2)}) async-start(f32[16,6,768]{2,1,0:T(8,128)} %reshape.119), calls=%async_computation.3 | async-start | bytes 786432 | tf_op jit(solution)/shard_map/all_to_all | solution.py:394
  161.5 1.7 fusion.6
  163.2 6.4 %all-to-all-done.3 = f32[16,6,768]{2,1,0:T(8,128)S(1)} async-done(((f32[16,6,768]{2,1,0:T(8,128)}), f32[16,6,768]{2,1,0:T(8,128)S(1)}, u32[]{:S(2)}, u32[]{:S(2)}) %all-to-all-start.3) | async-done | bytes 294944 | tf_op jit(solution)/shard_map/all_to_all | solution.py:394
  169.6 0.6 broadcast_in_dim.27
  (54 shorter events, 3.0 us)
Async XLA Ops:
  0.6 0.9 copy-start
  2.2 10.2 %collective-permute-start = (bf16[64,768]{1,0:T(8,128)(2,1)S(1)}, bf16[64,768]{1,0:T(8,128)(2,1)S(1)}, u32[]{:S(2)}, u32[]{:S(2)}) collective-permute-start(bf16[64,768]{1,0:T(8,128)(2,1)S(1)} %dynamic-slice_bitcast_fusion), channel_id=1, source_target_pairs={{0,128},{128,0},{1,129},{129,1},{2,130},{130,2},{3,131},{131,3},{4... | collective-permute-start | bytes 294920 | tf_op jit(solution)/shard_map/ppermute | solution.py:28
  5.3 14.2 %all-to-all-start.1 = ((bf16[16,6,768]{2,1,0:T(8,128)(2,1)}), bf16[16,6,768]{2,1,0:T(8,128)(2,1)S(1)}, u32[]{:S(2)}, u32[]{:S(2)}) async-start(bf16[16,6,768]{2,1,0:T(8,128)(2,1)} %broadcast_in_dim.12), calls=%async_computation.1 | async-start | bytes 393216 | tf_op jit(solution)/shard_map/all_to_all | solution.py:59
  19.5 6.3 %collective-permute-start.1 = (bf16[160,768]{1,0:T(8,128)(2,1)S(1)}, bf16[160,768]{1,0:T(8,128)(2,1)S(1)}, u32[]{:S(2)}, u32[]{:S(2)}) collective-permute-start(bf16[160,768]{1,0:T(8,128)(2,1)S(1)} %pad_maximum_fusion), channel_id=1, source_target_pairs={{0,8},{1,57},{8,0},{9,17},{16,24},{17,9},{24,16},{25,33},{32,40},{... | collective-permute-start | bytes 737288 | tf_op jit(solution)/shard_map/ppermute | solution.py:39
  25.8 12.8 %collective-permute-start.2 = (bf16[320,768]{1,0:T(8,128)(2,1)S(1)}, bf16[320,768]{1,0:T(8,128)(2,1)S(1)}, u32[]{:S(2)}, u32[]{:S(2)}) collective-permute-start(bf16[320,768]{1,0:T(8,128)(2,1)S(1)} %constant_dynamic-update-slice_fusion.refs_0_), channel_id=1, source_target_pairs={{0,56},{1,9},{8,16},{9,1},{16,8},{17,25},{24,32},{25,17},{32,24},{... | collective-permute-start | bytes 1474568 | tf_op jit(solution)/shard_map/ppermute | solution.py:39
  31.8 27.1 %all-to-all-start = ((bf16[16,64,768]{2,1,0:T(8,128)(2,1)}), bf16[16,64,768]{2,1,0:T(8,128)(2,1)}, u32[]{:S(2)}, u32[]{:S(2)}) async-start(bf16[16,64,768]{2,1,0:T(8,128)(2,1)} %broadcast_in_dim.10), calls=%async_computation | async-start | bytes 3145728 | tf_op jit(solution)/shard_map/all_to_all | solution.py:333
  38.6 9.3 %collective-permute-start.3 = (bf16[320,768]{1,0:T(8,128)(2,1)S(1)}, bf16[320,768]{1,0:T(8,128)(2,1)S(1)}, u32[]{:S(2)}, u32[]{:S(2)}) collective-permute-start(bf16[320,768]{1,0:T(8,128)(2,1)S(1)} %collective-permute-done.2.refs_1_), channel_id=1, source_target_pairs={{0,8},{1,57},{8,0},{9,17},{16,24},{17,9},{24,16},{25,33},{32,40},{... | collective-permute-start | bytes 1474568 | tf_op jit(solution)/shard_map/ppermute | solution.py:39
  47.8 10.3 %collective-permute-start.4 = (bf16[320,768]{1,0:T(8,128)(2,1)S(1)}, bf16[320,768]{1,0:T(8,128)(2,1)S(1)}, u32[]{:S(2)}, u32[]{:S(2)}) collective-permute-start(bf16[320,768]{1,0:T(8,128)(2,1)S(1)} %collective-permute-done.3.refs_2_), channel_id=1, source_target_pairs={{0,56},{1,9},{8,16},{9,1},{16,8},{17,25},{24,32},{25,17},{32,24},{... | collective-permute-start | bytes 1474568 | tf_op jit(solution)/shard_map/ppermute | solution.py:39
  51.3 7.6 %collective-permute-start.5 = (bf16[320,768]{1,0:T(8,128)(2,1)S(1)}, bf16[320,768]{1,0:T(8,128)(2,1)S(1)}, u32[]{:S(2)}, u32[]{:S(2)}) collective-permute-start(bf16[320,768]{1,0:T(8,128)(2,1)S(1)} %constant_dynamic-update-slice_fusion.refs_0_), channel_id=1, source_target_pairs={{0,1},{1,0},{2,3},{3,2},{4,5},{5,4},{6,7},{7,6},{8,9},{9,8},{10,11... | collective-permute-start | bytes 1474568 | tf_op jit(solution)/shard_map/ppermute | solution.py:28
  51.3 7.6 %collective-permute-start.6 = (bf16[320,768]{1,0:T(8,128)(2,1)S(1)}, bf16[320,768]{1,0:T(8,128)(2,1)S(1)}, u32[]{:S(2)}, u32[]{:S(2)}) collective-permute-start(bf16[320,768]{1,0:T(8,128)(2,1)S(1)} %collective-permute-done.2.refs_1_), channel_id=1, source_target_pairs={{0,1},{1,0},{2,3},{3,2},{4,5},{5,4},{6,7},{7,6},{8,9},{9,8},{10,11... | collective-permute-start | bytes 1474568 | tf_op jit(solution)/shard_map/ppermute | solution.py:28
  51.8 7.1 %collective-permute-start.7 = (bf16[320,768]{1,0:T(8,128)(2,1)S(1)}, bf16[320,768]{1,0:T(8,128)(2,1)}, u32[]{:S(2)}, u32[]{:S(2)}) collective-permute-start(bf16[320,768]{1,0:T(8,128)(2,1)S(1)} %collective-permute-done.3.refs_2_), channel_id=1, source_target_pairs={{0,1},{1,0},{2,3},{3,2},{4,5},{5,4},{6,7},{7,6},{8,9},{9,8},{10,11... | collective-permute-start | bytes 1474568 | tf_op jit(solution)/shard_map/ppermute | solution.py:28
  58.1 2.0 %collective-permute-start.8 = (bf16[320,768]{1,0:T(8,128)(2,1)S(1)}, bf16[320,768]{1,0:T(8,128)(2,1)}, u32[]{:S(2)}, u32[]{:S(2)}) collective-permute-start(bf16[320,768]{1,0:T(8,128)(2,1)S(1)} %collective-permute-done.4.refs_3_), channel_id=1, source_target_pairs={{0,1},{1,0},{2,3},{3,2},{4,5},{5,4},{6,7},{7,6},{8,9},{9,8},{10,11... | collective-permute-start | bytes 1474568 | tf_op jit(solution)/shard_map/ppermute | solution.py:28
  58.9 23.6 %copy-start.1 = (s32[16384]{0:T(1024)S(1)}, s32[16384]{0:T(1024)}, u32[]{:S(2)}) copy-start(s32[16384]{0:T(1024)} %param.6) | copy-start | bytes 196612
  58.9 1.3 copy-start.2
  58.9 1.2 copy-start.3
  71.6 3.7 %collective-permute-start.9 = (f32[8,128]{1,0:T(8,128)S(1)}, f32[8,128]{1,0:T(8,128)S(1)}, u32[]{:S(2)}, u32[]{:S(2)}) collective-permute-start(f32[8,128]{1,0:T(8,128)S(1)} %get-tuple-element.35), channel_id=1, source_target_pairs={{0,2},{2,0},{4,6},{6,4},{1,3},{3,1},{5,7},{7,5},{8,10},{10,8},{12,... | collective-permute-start | bytes 12296 | tf_op jit(solution)/shard_map/ppermute | solution.py:28
  73.1 2.1 %collective-permute-start.10 = (f32[8,128]{1,0:T(8,128)S(1)}, f32[8,128]{1,0:T(8,128)S(1)}, u32[]{:S(2)}, u32[]{:S(2)}) collective-permute-start(f32[8,128]{1,0:T(8,128)S(1)} %get-tuple-element.36), channel_id=1, source_target_pairs={{0,1},{1,0},{2,3},{3,2},{4,5},{5,4},{6,7},{7,6},{8,9},{9,8},{10,11... | collective-permute-start | bytes 12296 | tf_op jit(solution)/shard_map/ppermute | solution.py:28
  75.3 4.9 %collective-permute-start.12 = (f32[8,128]{1,0:T(8,128)S(1)}, f32[8,128]{1,0:T(8,128)S(1)}, u32[]{:S(2)}, u32[]{:S(2)}) collective-permute-start(f32[8,128]{1,0:T(8,128)S(1)} %add.199), channel_id=1, source_target_pairs={{0,56},{1,9},{8,16},{9,1},{16,8},{17,25},{24,32},{25,17},{32,24},{... | collective-permute-start | bytes 12296 | tf_op jit(solution)/shard_map/ppermute | solution.py:39
  78.6 3.6 %collective-permute-start.11 = (f32[8,128]{1,0:T(8,128)S(1)}, f32[8,128]{1,0:T(8,128)S(1)}, u32[]{:S(2)}, u32[]{:S(2)}) collective-permute-start(f32[8,128]{1,0:T(8,128)S(1)} %add.198), channel_id=1, source_target_pairs={{0,6},{2,4},{4,2},{6,0},{1,7},{3,5},{5,3},{7,1},{8,14},{10,12},{12... | collective-permute-start | bytes 12296 | tf_op jit(solution)/shard_map/ppermute | solution.py:28
  82.2 3.6 %collective-permute-start.14 = (f32[8,128]{1,0:T(8,128)S(1)}, f32[8,128]{1,0:T(8,128)S(1)}, u32[]{:S(2)}, u32[]{:S(2)}) collective-permute-start(f32[8,128]{1,0:T(8,128)S(1)} %add.201), channel_id=1, source_target_pairs={{0,8},{1,57},{8,0},{9,17},{16,24},{17,9},{24,16},{25,33},{32,40},{... | collective-permute-start | bytes 12296 | tf_op jit(solution)/shard_map/ppermute | solution.py:39
  82.2 3.7 %collective-permute-start.13 = (f32[8,128]{1,0:T(8,128)S(1)}, f32[8,128]{1,0:T(8,128)S(1)}, u32[]{:S(2)}, u32[]{:S(2)}) collective-permute-start(f32[8,128]{1,0:T(8,128)S(1)} %add.200), channel_id=1, source_target_pairs={{0,128},{64,192},{128,0},{192,64},{1,129},{65,193},{129,1},{193,65... | collective-permute-start | bytes 12296 | tf_op jit(solution)/shard_map/ppermute | solution.py:28
  85.9 6.7 %collective-permute-start.16 = (f32[8,128]{1,0:T(8,128)S(1)}, f32[8,128]{1,0:T(8,128)S(1)}, u32[]{:S(2)}, u32[]{:S(2)}) collective-permute-start(f32[8,128]{1,0:T(8,128)S(1)} %add.203.col_sum), channel_id=1, source_target_pairs={{0,40},{1,25},{8,32},{9,49},{16,56},{17,41},{24,48},{25,1},{32,8},... | collective-permute-start | bytes 12296 | tf_op jit(solution)/shard_map/ppermute | solution.py:49
  89.0 4.8 %collective-permute-start.15 = (f32[8,128]{1,0:T(8,128)S(1)}, f32[8,128]{1,0:T(8,128)S(1)}, u32[]{:S(2)}, u32[]{:S(2)}) collective-permute-start(f32[8,128]{1,0:T(8,128)S(1)} %add.202.row_sum), channel_id=1, source_target_pairs={{0,192},{64,128},{128,64},{192,0},{1,193},{65,129},{129,65},{193,1... | collective-permute-start | bytes 12296 | tf_op jit(solution)/shard_map/ppermute | solution.py:28
  108.4 2.2 %collective-permute-start.17 = (bf16[2,160,768]{2,1,0:T(8,128)(2,1)S(1)}, bf16[2,160,768]{2,1,0:T(8,128)(2,1)S(1)}, u32[]{:S(2)}, u32[]{:S(2)}) collective-permute-start(bf16[2,160,768]{2,1,0:T(8,128)(2,1)S(1)} %get-tuple-element.54), channel_id=1, source_target_pairs={{0,1},{1,0},{2,3},{3,2},{4,5},{5,4},{6,7},{7,6},{8,9},{9,8},{10,11... | collective-permute-start | bytes 1474568 | tf_op jit(solution)/shard_map/ppermute | solution.py:28
  110.5 11.4 %collective-permute-start.18 = (bf16[8,160,768]{2,1,0:T(8,128)(2,1)}, bf16[8,160,768]{2,1,0:T(8,128)(2,1)}, u32[]{:S(2)}, u32[]{:S(2)}) collective-permute-start(bf16[8,160,768]{2,1,0:T(8,128)(2,1)} %get-tuple-element.56), channel_id=1, source_target_pairs={{0,1},{1,0},{2,3},{3,2},{4,5},{5,4},{6,7},{7,6},{8,9},{9,8},{10,11... | collective-permute-start | bytes 5898248 | tf_op jit(solution)/shard_map/ppermute | solution.py:28
  111.8 10.1 %collective-permute-start.19 = (bf16[2,160,768]{2,1,0:T(8,128)(2,1)S(1)}, bf16[2,160,768]{2,1,0:T(8,128)(2,1)S(1)}, u32[]{:S(2)}, u32[]{:S(2)}) collective-permute-start(bf16[2,160,768]{2,1,0:T(8,128)(2,1)S(1)} %add_convert_fusion.2), channel_id=1, source_target_pairs={{0,56},{1,9},{8,16},{9,1},{16,8},{17,25},{24,32},{25,17},{32,24},{... | collective-permute-start | bytes 1474568 | tf_op jit(solution)/shard_map/ppermute | solution.py:39
  113.8 27.1 %all-to-all-start.2 = ((bf16[16,64,768]{2,1,0:T(8,128)(2,1)}), bf16[16,64,768]{2,1,0:T(8,128)(2,1)S(1)}, u32[]{:S(2)}, u32[]{:S(2)}) async-start(bf16[16,64,768]{2,1,0:T(8,128)(2,1)} %get-tuple-element.58), calls=%async_computation.2 | async-start | bytes 3145728 | tf_op jit(solution)/shard_map/all_to_all | solution.py:380
  123.3 8.9 %collective-permute-start.20 = (bf16[2,160,768]{2,1,0:T(8,128)(2,1)S(1)}, bf16[2,160,768]{2,1,0:T(8,128)(2,1)S(1)}, u32[]{:S(2)}, u32[]{:S(2)}) collective-permute-start(bf16[2,160,768]{2,1,0:T(8,128)(2,1)S(1)} %add_convert_fusion.1), channel_id=1, source_target_pairs={{0,8},{1,57},{8,0},{9,17},{16,24},{17,9},{24,16},{25,33},{32,40},{... | collective-permute-start | bytes 1474568 | tf_op jit(solution)/shard_map/ppermute | solution.py:39
  133.6 10.1 %collective-permute-start.21 = (bf16[2,160,768]{2,1,0:T(8,128)(2,1)S(1)}, bf16[2,160,768]{2,1,0:T(8,128)(2,1)S(1)}, u32[]{:S(2)}, u32[]{:S(2)}) collective-permute-start(bf16[2,160,768]{2,1,0:T(8,128)(2,1)S(1)} %add_convert_fusion), channel_id=1, source_target_pairs={{0,56},{1,9},{8,16},{9,1},{16,8},{17,25},{24,32},{25,17},{32,24},{... | collective-permute-start | bytes 1474568 | tf_op jit(solution)/shard_map/ppermute | solution.py:39
  144.9 6.3 %collective-permute-start.22 = (bf16[160,768]{1,0:T(8,128)(2,1)S(1)}, bf16[160,768]{1,0:T(8,128)(2,1)S(1)}, u32[]{:S(2)}, u32[]{:S(2)}) collective-permute-start(bf16[160,768]{1,0:T(8,128)(2,1)S(1)} %fusion.8), channel_id=1, source_target_pairs={{0,8},{1,57},{8,0},{9,17},{16,24},{17,9},{24,16},{25,33},{32,40},{... | collective-permute-start | bytes 737288 | tf_op jit(solution)/shard_map/ppermute | solution.py:39
  145.7 15.8 %copy-start.4 = (bf16[2,8,48,768]{3,2,1,0:T(8,128)(2,1)S(1)}, bf16[2,8,48,768]{3,2,1,0:T(8,128)(2,1)}, u32[]{:S(2)}) copy-start(bf16[2,8,48,768]{3,2,1,0:T(8,128)(2,1)} %get-tuple-element.63) | copy-start | bytes 3538948
  152.4 9.1 %collective-permute-start.23 = (bf16[64,768]{1,0:T(8,128)(2,1)S(1)}, bf16[64,768]{1,0:T(8,128)(2,1)S(1)}, u32[]{:S(2)}, u32[]{:S(2)}) collective-permute-start(bf16[64,768]{1,0:T(8,128)(2,1)S(1)} %get-tuple-element.65), channel_id=1, source_target_pairs={{0,128},{128,0},{1,129},{129,1},{2,130},{130,2},{3,131},{131,3},{4... | collective-permute-start | bytes 294920 | tf_op jit(solution)/shard_map/ppermute | solution.py:28
  153.3 16.2 %all-to-all-start.3 = ((f32[16,6,768]{2,1,0:T(8,128)}), f32[16,6,768]{2,1,0:T(8,128)S(1)}, u32[]{:S(2)}, u32[]{:S(2)}) async-start(f32[16,6,768]{2,1,0:T(8,128)} %reshape.119), calls=%async_computation.3 | async-start | bytes 786432 | tf_op jit(solution)/shard_map/all_to_all | solution.py:394

commit v4 on v2

--- a/solution.py
+++ b/solution.py
@@ -358,7 +358,7 @@
             came = across(col_sum)
         else:
             came = pair(col_sum, step)
-        return stage(mirror(row_sum, axes, mask), came)
+        return mirror(row_sum, axes, mask), came
 
     for step in range(3):
         row_came, col_came = exchange(row_sum, col_sum, step)

time: 170 us -> 168 us (0.988)
  waiting for transfers between devices: 72.1 us -> 66.4 us
  starting transfers between devices: 56.2 us -> 59.3 us
    ppermute x10, waiting for transfers between devices: 44.3 us -> 38.6 us  [pair(): return lax.ppermute(value, ('z', 'c'), route)]
    ppermute x10, starting transfers between devices: 19.4 us -> 22.2 us  [pair(): return lax.ppermute(value, ('z', 'c'), route)]
    ppermute x13, starting transfers between devices: 6.53 us -> 8.75 us  [mirror(): lax.ppermute(value, axes, [(i, i ^ mask) for i in range(count(axes))])]
    ppermute x1, waiting for transfers between devices: 2.06 us -> 3.89 us  [across(): return lax.ppermute(value, ('z', 'c'), route)]
  transfers between devices with their start and end apart: 28 -> 28, of which waited for: 20 -> 17; matrix products, arithmetic and copies ran while one was open for 6% -> 6% of each run, Pallas kernels for 0% -> 0%
where the time goes in v4:
time: 168 us; the launch traced here: 167 us
  waiting for transfers between devices  66.4 us (40%)
  starting transfers between devices  59.3 us (35%)
  Pallas kernels  25.9 us (15%)
  other arithmetic  5.65 us (3%)
  local copies, waits for them, and re-layouts  5.5 us (3%)
  matrix products  2.26 us (1%)
    ppermute x10, waiting for transfers between devices, pair(): return lax.ppermute(value, ('z', 'c'), route)  38.6 us
    pallas_call x2, Pallas kernels, call(): pl.pallas_call(kernel, in_specs=[smem, smem] + [spaces[own] for _, own in...  25.9 us
    ppermute x10, starting transfers between devices, pair(): return lax.ppermute(value, ('z', 'c'), route)  22.2 us
    ppermute x13, starting transfers between devices, mirror(): lax.ppermute(value, axes, [(i, i ^ mask) for i in range(count(axes))])  8.75 us
    all_to_all x1, starting transfers between devices, gather(): return lax.all_to_all(copies, axes, 0, 0)  7.18 us
    ppermute x13, waiting for transfers between devices, mirror(): lax.ppermute(value, axes, [(i, i ^ mask) for i in range(count(axes))])  7.11 us
    all_to_all x1, starting transfers between devices, per_device(): lax.all_to_all(d_weight, PLANE, 0, 0)  6.75 us
    all_to_all x1, waiting for transfers between devices, per_device(): lax.all_to_all(d_weight, PLANE, 0, 0)  6.36 us
  transfers between devices with their start and end apart: 28, of which 17 were waited for; matrix products, arithmetic and copies ran while one was open for 6% of the time, Pallas kernels for 0%

profile of v4, /device:TPU:2, one launch (start us, length us, event | category | flops | bytes accessed | tf_op | source)
XLA Modules:
  0.0 166.5 jit_solution(6533305517650672162)
XLA Ops:
  0.7 0.9 copy-done
  1.6 0.6 fusion.4
  2.2 1.7 collective-permute-start
  3.9 1.4 broadcast_in_dim.12
  5.3 7.2 %all-to-all-start.1 = ((bf16[16,6,768]{2,1,0:T(8,128)(2,1)}), bf16[16,6,768]{2,1,0:T(8,128)(2,1)S(1)}, u32[]{:S(2)}, u32[]{:S(2)}) async-start(bf16[16,6,768]{2,1,0:T(8,128)(2,1)} %broadcast_in_dim.12), calls=%async_computation.1 | async-start | bytes 393216 | tf_op jit(solution)/shard_map/all_to_all | solution.py:59
  12.5 1.3 broadcast_in_dim.10
  13.8 5.6 %all-to-all-done.1 = bf16[16,6,768]{2,1,0:T(8,128)(2,1)S(1)} async-done(((bf16[16,6,768]{2,1,0:T(8,128)(2,1)}), bf16[16,6,768]{2,1,0:T(8,128)(2,1)S(1)}, u32[]{:S(2)}, u32[]{:S(2)}) %all-to-all-start.1) | async-done | bytes 147488 | tf_op jit(solution)/shard_map/all_to_all | solution.py:59
  19.5 2.0 %collective-permute-start.1 = (bf16[160,768]{1,0:T(8,128)(2,1)S(1)}, bf16[160,768]{1,0:T(8,128)(2,1)S(1)}, u32[]{:S(2)}, u32[]{:S(2)}) collective-permute-start(bf16[160,768]{1,0:T(8,128)(2,1)S(1)} %pad_maximum_fusion), channel_id=1, source_target_pairs={{0,8},{1,57},{8,0},{9,17},{16,24},{17,9},{24,16},{25,33},{32,40},{... | collective-permute-start | bytes 737288 | tf_op jit(solution)/shard_map/ppermute | solution.py:39
  21.5 4.3 %collective-permute-done.1 = bf16[160,768]{1,0:T(8,128)(2,1)S(1)} collective-permute-done((bf16[160,768]{1,0:T(8,128)(2,1)S(1)}, bf16[160,768]{1,0:T(8,128)(2,1)S(1)}, u32[]{:S(2)}, u32[]{:S(2)}) %collective-permute-start.1) | collective-permute-done | bytes 245792 | tf_op jit(solution)/shard_map/ppermute | solution.py:39
  25.8 5.9 %collective-permute-start.2 = (bf16[320,768]{1,0:T(8,128)(2,1)S(1)}, bf16[320,768]{1,0:T(8,128)(2,1)S(1)}, u32[]{:S(2)}, u32[]{:S(2)}) collective-permute-start(bf16[320,768]{1,0:T(8,128)(2,1)S(1)} %constant_dynamic-update-slice_fusion.refs_0_), channel_id=1, source_target_pairs={{0,56},{1,9},{8,16},{9,1},{16,8},{17,25},{24,32},{25,17},{32,24},{... | collective-permute-start | bytes 1474568 | tf_op jit(solution)/shard_map/ppermute | solution.py:39
  31.8 5.6 %all-to-all-start = ((bf16[16,64,768]{2,1,0:T(8,128)(2,1)}), bf16[16,64,768]{2,1,0:T(8,128)(2,1)}, u32[]{:S(2)}, u32[]{:S(2)}) async-start(bf16[16,64,768]{2,1,0:T(8,128)(2,1)} %broadcast_in_dim.10), calls=%async_computation | async-start | bytes 3145728 | tf_op jit(solution)/shard_map/all_to_all | solution.py:333
  37.4 1.2 collective-permute-done.2.refs_1_
  38.6 9.3 %collective-permute-done.3.refs_2_ = bf16[320,768]{1,0:T(8,128)(2,1)S(1)} collective-permute-done((bf16[320,768]{1,0:T(8,128)(2,1)S(1)}, bf16[320,768]{1,0:T(8,128)(2,1)S(1)}, u32[]{:S(2)}, u32[]{:S(2)}) %collective-permute-start.3) | collective-permute-done | bytes 491552 | tf_op jit(solution)/shard_map/ppermute | solution.py:39
  47.8 3.5 %collective-permute-start.4 = (bf16[320,768]{1,0:T(8,128)(2,1)S(1)}, bf16[320,768]{1,0:T(8,128)(2,1)S(1)}, u32[]{:S(2)}, u32[]{:S(2)}) collective-permute-start(bf16[320,768]{1,0:T(8,128)(2,1)S(1)} %collective-permute-done.3.refs_2_), channel_id=1, source_target_pairs={{0,56},{1,9},{8,16},{9,1},{16,8},{17,25},{24,32},{25,17},{32,24},{... | collective-permute-start | bytes 1474568 | tf_op jit(solution)/shard_map/ppermute | solution.py:39
  51.8 6.3 %collective-permute-done.4.refs_3_ = bf16[320,768]{1,0:T(8,128)(2,1)S(1)} collective-permute-done((bf16[320,768]{1,0:T(8,128)(2,1)S(1)}, bf16[320,768]{1,0:T(8,128)(2,1)S(1)}, u32[]{:S(2)}, u32[]{:S(2)}) %collective-permute-start.4) | collective-permute-done | bytes 491552 | tf_op jit(solution)/shard_map/ppermute | solution.py:39
  58.9 1.2 collective-permute-done.8.refs_7_
  60.1 11.4 %shard_map.59 = (f32[8,128]{1,0:T(8,128)S(1)}, f32[8,128]{1,0:T(8,128)S(1)}, f32[1,1024]{1,0:T(1,128)S(1)}, f32[1,1024]{1,0:T(1,128)S(1)}, bf16[16,64,768]{2,1,0...) custom-call(s32[5]{0:T(128)S(1)} %stack.23.at, ...), custom_call_target="tpu_custom_call" | custom-call | flops 4026531840 | bytes 8388608 | tf_op jit(solution)/shard_map/pallas_call | solution.py:285
  71.6 1.6 collective-permute-start.9
  73.1 2.1 %collective-permute-done.9 = f32[8,128]{1,0:T(8,128)S(1)} collective-permute-done((f32[8,128]{1,0:T(8,128)S(1)}, f32[8,128]{1,0:T(8,128)S(1)}, u32[]{:S(2)}, u32[]{:S(2)}) %collective-permute-start.9) | collective-permute-done | bytes 4128 | tf_op jit(solution)/shard_map/ppermute | solution.py:28
  75.9 3.2 %collective-permute-start.14 = (f32[8,128]{1,0:T(8,128)S(1)}, f32[8,128]{1,0:T(8,128)S(1)}, u32[]{:S(2)}, u32[]{:S(2)}) collective-permute-start(f32[8,128]{1,0:T(8,128)S(1)} %add.189), channel_id=1, source_target_pairs={{0,56},{1,9},{8,16},{9,1},{16,8},{17,25},{24,32},{25,17},{32,24},{... | collective-permute-start | bytes 12296 | tf_op jit(solution)/shard_map/ppermute | solution.py:39
  79.1 0.7 collective-permute-start.11
  79.8 0.9 collective-permute-done.14
  80.8 1.9 %collective-permute-done.11 = f32[8,128]{1,0:T(8,128)S(1)} collective-permute-done((f32[8,128]{1,0:T(8,128)S(1)}, f32[8,128]{1,0:T(8,128)S(1)}, u32[]{:S(2)}, u32[]{:S(2)}) %collective-permute-start.11) | collective-permute-done | bytes 4128 | tf_op jit(solution)/shard_map/ppermute | solution.py:28
  82.7 2.1 %collective-permute-start.12 = (f32[8,128]{1,0:T(8,128)S(1)}, f32[8,128]{1,0:T(8,128)S(1)}, u32[]{:S(2)}, u32[]{:S(2)}) collective-permute-start(f32[8,128]{1,0:T(8,128)S(1)} %add.188.row_sum), channel_id=1, source_target_pairs={{0,192},{64,128},{128,64},{192,0},{1,193},{65,129},{129,65},{193,1... | collective-permute-start | bytes 12296 | tf_op jit(solution)/shard_map/ppermute | solution.py:28
  84.8 2.6 %collective-permute-start.16 = (f32[8,128]{1,0:T(8,128)S(1)}, f32[8,128]{1,0:T(8,128)S(1)}, u32[]{:S(2)}, u32[]{:S(2)}) collective-permute-start(f32[8,128]{1,0:T(8,128)S(1)} %add.191.col_sum), channel_id=1, source_target_pairs={{0,40},{1,25},{8,32},{9,49},{16,56},{17,41},{24,48},{25,1},{32,8},... | collective-permute-start | bytes 12296 | tf_op jit(solution)/shard_map/ppermute | solution.py:49
  87.5 3.9 %collective-permute-done.16.col_came = f32[8,128]{1,0:T(8,128)S(1)} collective-permute-done((f32[8,128]{1,0:T(8,128)S(1)}, f32[8,128]{1,0:T(8,128)S(1)}, u32[]{:S(2)}, u32[]{:S(2)}) %collective-permute-start.16) | collective-permute-done | bytes 4128 | tf_op jit(solution)/shard_map/ppermute | solution.py:49
  91.4 14.5 %shard_map.60 = (bf16[16,64,768]{2,1,0:T(8,128)(2,1)}, bf16[8,160,768]{2,1,0:T(8,128)(2,1)}, bf16[2,160,768]{2,1,0:T(8,128)(2,1)S(1)}, bf16[8,160,768]{2,1,0:T(8,128)(2,1)}) custom-call(s32[5]{0:T(128)S(1)} %stack.23.at, f32[1]{0:T(128)S(6)} %copy.9.scale, f32[8,128]{1,0:T(8,128)S(1)} %add.188.row_sum, f32[8,128]{1,0:T(8,128)S(1)} %collective-permute-done.12.row_came, ...), custom_call_target="tpu_custom_call" | custom-call | flops 5637144576 | bytes 8388608 | tf_op jit(solution)/shard_map/pallas_call | solution.py:285
  106.3 1.9 %collective-permute-done.17 = bf16[2,160,768]{2,1,0:T(8,128)(2,1)S(1)} collective-permute-done((bf16[2,160,768]{2,1,0:T(8,128)(2,1)S(1)}, bf16[2,160,768]{2,1,0:T(8,128)(2,1)S(1)}, u32[]{:S(2)}, u32[]{:S(2)}) %collective-permute-start.17) | collective-permute-done | bytes 491552 | tf_op jit(solution)/shard_map/ppermute | solution.py:28
  108.2 1.2 add_convert_fusion.2
  109.4 2.8 %collective-permute-start.19 = (bf16[2,160,768]{2,1,0:T(8,128)(2,1)S(1)}, bf16[2,160,768]{2,1,0:T(8,128)(2,1)S(1)}, u32[]{:S(2)}, u32[]{:S(2)}) collective-permute-start(bf16[2,160,768]{2,1,0:T(8,128)(2,1)S(1)} %add_convert_fusion.2), channel_id=1, source_target_pairs={{0,56},{1,9},{8,16},{9,1},{16,8},{17,25},{24,32},{25,17},{32,24},{... | collective-permute-start | bytes 1474568 | tf_op jit(solution)/shard_map/ppermute | solution.py:39
  112.2 6.2 %all-to-all-start.2 = ((bf16[16,64,768]{2,1,0:T(8,128)(2,1)}), bf16[16,64,768]{2,1,0:T(8,128)(2,1)S(1)}, u32[]{:S(2)}, u32[]{:S(2)}) async-start(bf16[16,64,768]{2,1,0:T(8,128)(2,1)} %get-tuple-element.40), calls=%async_computation.2 | async-start | bytes 3145728 | tf_op jit(solution)/shard_map/all_to_all | solution.py:380
  118.5 1.1 collective-permute-done.19
  119.6 1.4 add_convert_fusion.1
  120.9 0.8 collective-permute-start.20
  121.7 8.1 %collective-permute-done.20 = bf16[2,160,768]{2,1,0:T(8,128)(2,1)S(1)} collective-permute-done((bf16[2,160,768]{2,1,0:T(8,128)(2,1)S(1)}, bf16[2,160,768]{2,1,0:T(8,128)(2,1)S(1)}, u32[]{:S(2)}, u32[]{:S(2)}) %collective-permute-start.20) | collective-permute-done | bytes 491552 | tf_op jit(solution)/shard_map/ppermute | solution.py:39
  129.8 1.4 add_convert_fusion
  131.2 2.8 %collective-permute-start.21 = (bf16[2,160,768]{2,1,0:T(8,128)(2,1)S(1)}, bf16[2,160,768]{2,1,0:T(8,128)(2,1)S(1)}, u32[]{:S(2)}, u32[]{:S(2)}) collective-permute-start(bf16[2,160,768]{2,1,0:T(8,128)(2,1)S(1)} %add_convert_fusion), channel_id=1, source_target_pairs={{0,56},{1,9},{8,16},{9,1},{16,8},{17,25},{24,32},{25,17},{32,24},{... | collective-permute-start | bytes 1474568 | tf_op jit(solution)/shard_map/ppermute | solution.py:39
  134.0 4.8 %all-to-all-done.2 = bf16[16,64,768]{2,1,0:T(8,128)(2,1)S(1)} async-done(((bf16[16,64,768]{2,1,0:T(8,128)(2,1)}), bf16[16,64,768]{2,1,0:T(8,128)(2,1)S(1)}, u32[]{:S(2)}, u32[]{:S(2)}) %all-to-all-start.2) | async-done | bytes 1572896 | tf_op jit(solution)/shard_map/all_to_all | solution.py:380
  138.8 2.5 %collective-permute-done.21 = bf16[2,160,768]{2,1,0:T(8,128)(2,1)S(1)} collective-permute-done((bf16[2,160,768]{2,1,0:T(8,128)(2,1)S(1)}, bf16[2,160,768]{2,1,0:T(8,128)(2,1)S(1)}, u32[]{:S(2)}, u32[]{:S(2)}) %collective-permute-start.21) | collective-permute-done | bytes 491552 | tf_op jit(solution)/shard_map/ppermute | solution.py:39
  141.3 1.3 convert_add_fusion
  142.7 1.1 collective-permute-start.22
  144.1 4.9 %collective-permute-done.22 = bf16[160,768]{1,0:T(8,128)(2,1)S(1)} collective-permute-done((bf16[160,768]{1,0:T(8,128)(2,1)S(1)}, bf16[160,768]{1,0:T(8,128)(2,1)S(1)}, u32[]{:S(2)}, u32[]{:S(2)}) %collective-permute-start.22) | collective-permute-done | bytes 245792 | tf_op jit(solution)/shard_map/ppermute | solution.py:39
  149.1 1.2 collective-permute-start.23
  150.3 0.8 reshape.109
  151.1 6.7 %all-to-all-start.3 = ((f32[16,6,768]{2,1,0:T(8,128)}), f32[16,6,768]{2,1,0:T(8,128)S(1)}, u32[]{:S(2)}, u32[]{:S(2)}) async-start(f32[16,6,768]{2,1,0:T(8,128)} %reshape.109), calls=%async_computation.3 | async-start | bytes 786432 | tf_op jit(solution)/shard_map/all_to_all | solution.py:393
  157.9 1.7 fusion.6
  159.5 6.4 %all-to-all-done.3 = f32[16,6,768]{2,1,0:T(8,128)S(1)} async-done(((f32[16,6,768]{2,1,0:T(8,128)}), f32[16,6,768]{2,1,0:T(8,128)S(1)}, u32[]{:S(2)}, u32[]{:S(2)}) %all-to-all-start.3) | async-done | bytes 294944 | tf_op jit(solution)/shard_map/all_to_all | solution.py:393
  165.9 0.6 broadcast_in_dim.27
  (55 shorter events, 2.5 us)
Async XLA Ops:
  0.6 0.9 copy-start
  2.2 10.2 %collective-permute-start = (bf16[64,768]{1,0:T(8,128)(2,1)S(1)}, bf16[64,768]{1,0:T(8,128)(2,1)S(1)}, u32[]{:S(2)}, u32[]{:S(2)}) collective-permute-start(bf16[64,768]{1,0:T(8,128)(2,1)S(1)} %dynamic-slice_bitcast_fusion), channel_id=1, source_target_pairs={{0,128},{128,0},{1,129},{129,1},{2,130},{130,2},{3,131},{131,3},{4... | collective-permute-start | bytes 294920 | tf_op jit(solution)/shard_map/ppermute | solution.py:28
  5.3 14.2 %all-to-all-start.1 = ((bf16[16,6,768]{2,1,0:T(8,128)(2,1)}), bf16[16,6,768]{2,1,0:T(8,128)(2,1)S(1)}, u32[]{:S(2)}, u32[]{:S(2)}) async-start(bf16[16,6,768]{2,1,0:T(8,128)(2,1)} %broadcast_in_dim.12), calls=%async_computation.1 | async-start | bytes 393216 | tf_op jit(solution)/shard_map/all_to_all | solution.py:59
  19.5 6.3 %collective-permute-start.1 = (bf16[160,768]{1,0:T(8,128)(2,1)S(1)}, bf16[160,768]{1,0:T(8,128)(2,1)S(1)}, u32[]{:S(2)}, u32[]{:S(2)}) collective-permute-start(bf16[160,768]{1,0:T(8,128)(2,1)S(1)} %pad_maximum_fusion), channel_id=1, source_target_pairs={{0,8},{1,57},{8,0},{9,17},{16,24},{17,9},{24,16},{25,33},{32,40},{... | collective-permute-start | bytes 737288 | tf_op jit(solution)/shard_map/ppermute | solution.py:39
  25.8 12.8 %collective-permute-start.2 = (bf16[320,768]{1,0:T(8,128)(2,1)S(1)}, bf16[320,768]{1,0:T(8,128)(2,1)S(1)}, u32[]{:S(2)}, u32[]{:S(2)}) collective-permute-start(bf16[320,768]{1,0:T(8,128)(2,1)S(1)} %constant_dynamic-update-slice_fusion.refs_0_), channel_id=1, source_target_pairs={{0,56},{1,9},{8,16},{9,1},{16,8},{17,25},{24,32},{25,17},{32,24},{... | collective-permute-start | bytes 1474568 | tf_op jit(solution)/shard_map/ppermute | solution.py:39
  31.8 27.1 %all-to-all-start = ((bf16[16,64,768]{2,1,0:T(8,128)(2,1)}), bf16[16,64,768]{2,1,0:T(8,128)(2,1)}, u32[]{:S(2)}, u32[]{:S(2)}) async-start(bf16[16,64,768]{2,1,0:T(8,128)(2,1)} %broadcast_in_dim.10), calls=%async_computation | async-start | bytes 3145728 | tf_op jit(solution)/shard_map/all_to_all | solution.py:333
  38.6 9.3 %collective-permute-start.3 = (bf16[320,768]{1,0:T(8,128)(2,1)S(1)}, bf16[320,768]{1,0:T(8,128)(2,1)S(1)}, u32[]{:S(2)}, u32[]{:S(2)}) collective-permute-start(bf16[320,768]{1,0:T(8,128)(2,1)S(1)} %collective-permute-done.2.refs_1_), channel_id=1, source_target_pairs={{0,8},{1,57},{8,0},{9,17},{16,24},{17,9},{24,16},{25,33},{32,40},{... | collective-permute-start | bytes 1474568 | tf_op jit(solution)/shard_map/ppermute | solution.py:39
  47.8 10.3 %collective-permute-start.4 = (bf16[320,768]{1,0:T(8,128)(2,1)S(1)}, bf16[320,768]{1,0:T(8,128)(2,1)S(1)}, u32[]{:S(2)}, u32[]{:S(2)}) collective-permute-start(bf16[320,768]{1,0:T(8,128)(2,1)S(1)} %collective-permute-done.3.refs_2_), channel_id=1, source_target_pairs={{0,56},{1,9},{8,16},{9,1},{16,8},{17,25},{24,32},{25,17},{32,24},{... | collective-permute-start | bytes 1474568 | tf_op jit(solution)/shard_map/ppermute | solution.py:39
  51.3 7.6 %collective-permute-start.5 = (bf16[320,768]{1,0:T(8,128)(2,1)S(1)}, bf16[320,768]{1,0:T(8,128)(2,1)S(1)}, u32[]{:S(2)}, u32[]{:S(2)}) collective-permute-start(bf16[320,768]{1,0:T(8,128)(2,1)S(1)} %constant_dynamic-update-slice_fusion.refs_0_), channel_id=1, source_target_pairs={{0,1},{1,0},{2,3},{3,2},{4,5},{5,4},{6,7},{7,6},{8,9},{9,8},{10,11... | collective-permute-start | bytes 1474568 | tf_op jit(solution)/shard_map/ppermute | solution.py:28
  51.3 7.6 %collective-permute-start.6 = (bf16[320,768]{1,0:T(8,128)(2,1)S(1)}, bf16[320,768]{1,0:T(8,128)(2,1)S(1)}, u32[]{:S(2)}, u32[]{:S(2)}) collective-permute-start(bf16[320,768]{1,0:T(8,128)(2,1)S(1)} %collective-permute-done.2.refs_1_), channel_id=1, source_target_pairs={{0,1},{1,0},{2,3},{3,2},{4,5},{5,4},{6,7},{7,6},{8,9},{9,8},{10,11... | collective-permute-start | bytes 1474568 | tf_op jit(solution)/shard_map/ppermute | solution.py:28
  51.8 7.1 %collective-permute-start.7 = (bf16[320,768]{1,0:T(8,128)(2,1)S(1)}, bf16[320,768]{1,0:T(8,128)(2,1)}, u32[]{:S(2)}, u32[]{:S(2)}) collective-permute-start(bf16[320,768]{1,0:T(8,128)(2,1)S(1)} %collective-permute-done.3.refs_2_), channel_id=1, source_target_pairs={{0,1},{1,0},{2,3},{3,2},{4,5},{5,4},{6,7},{7,6},{8,9},{9,8},{10,11... | collective-permute-start | bytes 1474568 | tf_op jit(solution)/shard_map/ppermute | solution.py:28
  58.1 2.0 %collective-permute-start.8 = (bf16[320,768]{1,0:T(8,128)(2,1)S(1)}, bf16[320,768]{1,0:T(8,128)(2,1)}, u32[]{:S(2)}, u32[]{:S(2)}) collective-permute-start(bf16[320,768]{1,0:T(8,128)(2,1)S(1)} %collective-permute-done.4.refs_3_), channel_id=1, source_target_pairs={{0,1},{1,0},{2,3},{3,2},{4,5},{5,4},{6,7},{7,6},{8,9},{9,8},{10,11... | collective-permute-start | bytes 1474568 | tf_op jit(solution)/shard_map/ppermute | solution.py:28
  58.9 21.8 %copy-start.1 = (s32[16384]{0:T(1024)S(1)}, s32[16384]{0:T(1024)}, u32[]{:S(2)}) copy-start(s32[16384]{0:T(1024)} %param.6) | copy-start | bytes 196612
  58.9 1.3 copy-start.2
  58.9 1.2 copy-start.3
  71.6 3.7 %collective-permute-start.9 = (f32[8,128]{1,0:T(8,128)S(1)}, f32[8,128]{1,0:T(8,128)S(1)}, u32[]{:S(2)}, u32[]{:S(2)}) collective-permute-start(f32[8,128]{1,0:T(8,128)S(1)} %get-tuple-element.25), channel_id=1, source_target_pairs={{0,2},{2,0},{4,6},{6,4},{1,3},{3,1},{5,7},{7,5},{8,10},{10,8},{12,... | collective-permute-start | bytes 12296 | tf_op jit(solution)/shard_map/ppermute | solution.py:28
  73.1 2.7 %collective-permute-start.13 = (f32[8,128]{1,0:T(8,128)S(1)}, f32[8,128]{1,0:T(8,128)S(1)}, u32[]{:S(2)}, u32[]{:S(2)}) collective-permute-start(f32[8,128]{1,0:T(8,128)S(1)} %get-tuple-element.26), channel_id=1, source_target_pairs={{0,1},{1,0},{2,3},{3,2},{4,5},{5,4},{6,7},{7,6},{8,9},{9,8},{10,11... | collective-permute-start | bytes 12296 | tf_op jit(solution)/shard_map/ppermute | solution.py:28
  75.3 3.8 %collective-permute-start.10 = (f32[8,128]{1,0:T(8,128)S(1)}, f32[8,128]{1,0:T(8,128)S(1)}, u32[]{:S(2)}, u32[]{:S(2)}) collective-permute-start(f32[8,128]{1,0:T(8,128)S(1)} %add.186), channel_id=1, source_target_pairs={{0,6},{2,4},{4,2},{6,0},{1,7},{3,5},{5,3},{7,1},{8,14},{10,12},{12... | collective-permute-start | bytes 12296 | tf_op jit(solution)/shard_map/ppermute | solution.py:28
  75.9 4.8 %collective-permute-start.14 = (f32[8,128]{1,0:T(8,128)S(1)}, f32[8,128]{1,0:T(8,128)S(1)}, u32[]{:S(2)}, u32[]{:S(2)}) collective-permute-start(f32[8,128]{1,0:T(8,128)S(1)} %add.189), channel_id=1, source_target_pairs={{0,56},{1,9},{8,16},{9,1},{16,8},{17,25},{24,32},{25,17},{32,24},{... | collective-permute-start | bytes 12296 | tf_op jit(solution)/shard_map/ppermute | solution.py:39
  79.1 3.6 %collective-permute-start.11 = (f32[8,128]{1,0:T(8,128)S(1)}, f32[8,128]{1,0:T(8,128)S(1)}, u32[]{:S(2)}, u32[]{:S(2)}) collective-permute-start(f32[8,128]{1,0:T(8,128)S(1)} %add.187), channel_id=1, source_target_pairs={{0,128},{64,192},{128,0},{192,64},{1,129},{65,193},{129,1},{193,65... | collective-permute-start | bytes 12296 | tf_op jit(solution)/shard_map/ppermute | solution.py:28
  80.7 4.1 %collective-permute-start.15 = (f32[8,128]{1,0:T(8,128)S(1)}, f32[8,128]{1,0:T(8,128)S(1)}, u32[]{:S(2)}, u32[]{:S(2)}) collective-permute-start(f32[8,128]{1,0:T(8,128)S(1)} %add.190), channel_id=1, source_target_pairs={{0,8},{1,57},{8,0},{9,17},{16,24},{17,9},{24,16},{25,33},{32,40},{... | collective-permute-start | bytes 12296 | tf_op jit(solution)/shard_map/ppermute | solution.py:39
  82.7 4.8 %collective-permute-start.12 = (f32[8,128]{1,0:T(8,128)S(1)}, f32[8,128]{1,0:T(8,128)S(1)}, u32[]{:S(2)}, u32[]{:S(2)}) collective-permute-start(f32[8,128]{1,0:T(8,128)S(1)} %add.188.row_sum), channel_id=1, source_target_pairs={{0,192},{64,128},{128,64},{192,0},{1,193},{65,129},{129,65},{193,1... | collective-permute-start | bytes 12296 | tf_op jit(solution)/shard_map/ppermute | solution.py:28
  84.8 6.6 %collective-permute-start.16 = (f32[8,128]{1,0:T(8,128)S(1)}, f32[8,128]{1,0:T(8,128)S(1)}, u32[]{:S(2)}, u32[]{:S(2)}) collective-permute-start(f32[8,128]{1,0:T(8,128)S(1)} %add.191.col_sum), channel_id=1, source_target_pairs={{0,40},{1,25},{8,32},{9,49},{16,56},{17,41},{24,48},{25,1},{32,8},... | collective-permute-start | bytes 12296 | tf_op jit(solution)/shard_map/ppermute | solution.py:49
  105.9 2.2 %collective-permute-start.17 = (bf16[2,160,768]{2,1,0:T(8,128)(2,1)S(1)}, bf16[2,160,768]{2,1,0:T(8,128)(2,1)S(1)}, u32[]{:S(2)}, u32[]{:S(2)}) collective-permute-start(bf16[2,160,768]{2,1,0:T(8,128)(2,1)S(1)} %get-tuple-element.36), channel_id=1, source_target_pairs={{0,1},{1,0},{2,3},{3,2},{4,5},{5,4},{6,7},{7,6},{8,9},{9,8},{10,11... | collective-permute-start | bytes 1474568 | tf_op jit(solution)/shard_map/ppermute | solution.py:28
  108.1 11.4 %collective-permute-start.18 = (bf16[8,160,768]{2,1,0:T(8,128)(2,1)}, bf16[8,160,768]{2,1,0:T(8,128)(2,1)}, u32[]{:S(2)}, u32[]{:S(2)}) collective-permute-start(bf16[8,160,768]{2,1,0:T(8,128)(2,1)} %get-tuple-element.38), channel_id=1, source_target_pairs={{0,1},{1,0},{2,3},{3,2},{4,5},{5,4},{6,7},{7,6},{8,9},{9,8},{10,11... | collective-permute-start | bytes 5898248 | tf_op jit(solution)/shard_map/ppermute | solution.py:28
  109.4 10.1 %collective-permute-start.19 = (bf16[2,160,768]{2,1,0:T(8,128)(2,1)S(1)}, bf16[2,160,768]{2,1,0:T(8,128)(2,1)S(1)}, u32[]{:S(2)}, u32[]{:S(2)}) collective-permute-start(bf16[2,160,768]{2,1,0:T(8,128)(2,1)S(1)} %add_convert_fusion.2), channel_id=1, source_target_pairs={{0,56},{1,9},{8,16},{9,1},{16,8},{17,25},{24,32},{25,17},{32,24},{... | collective-permute-start | bytes 1474568 | tf_op jit(solution)/shard_map/ppermute | solution.py:39
  112.2 26.5 %all-to-all-start.2 = ((bf16[16,64,768]{2,1,0:T(8,128)(2,1)}), bf16[16,64,768]{2,1,0:T(8,128)(2,1)S(1)}, u32[]{:S(2)}, u32[]{:S(2)}) async-start(bf16[16,64,768]{2,1,0:T(8,128)(2,1)} %get-tuple-element.40), calls=%async_computation.2 | async-start | bytes 3145728 | tf_op jit(solution)/shard_map/all_to_all | solution.py:380
  120.9 8.9 %collective-permute-start.20 = (bf16[2,160,768]{2,1,0:T(8,128)(2,1)S(1)}, bf16[2,160,768]{2,1,0:T(8,128)(2,1)S(1)}, u32[]{:S(2)}, u32[]{:S(2)}) collective-permute-start(bf16[2,160,768]{2,1,0:T(8,128)(2,1)S(1)} %add_convert_fusion.1), channel_id=1, source_target_pairs={{0,8},{1,57},{8,0},{9,17},{16,24},{17,9},{24,16},{25,33},{32,40},{... | collective-permute-start | bytes 1474568 | tf_op jit(solution)/shard_map/ppermute | solution.py:39
  131.2 10.1 %collective-permute-start.21 = (bf16[2,160,768]{2,1,0:T(8,128)(2,1)S(1)}, bf16[2,160,768]{2,1,0:T(8,128)(2,1)S(1)}, u32[]{:S(2)}, u32[]{:S(2)}) collective-permute-start(bf16[2,160,768]{2,1,0:T(8,128)(2,1)S(1)} %add_convert_fusion), channel_id=1, source_target_pairs={{0,56},{1,9},{8,16},{9,1},{16,8},{17,25},{24,32},{25,17},{32,24},{... | collective-permute-start | bytes 1474568 | tf_op jit(solution)/shard_map/ppermute | solution.py:39
  142.7 6.3 %collective-permute-start.22 = (bf16[160,768]{1,0:T(8,128)(2,1)S(1)}, bf16[160,768]{1,0:T(8,128)(2,1)S(1)}, u32[]{:S(2)}, u32[]{:S(2)}) collective-permute-start(bf16[160,768]{1,0:T(8,128)(2,1)S(1)} %fusion.9), channel_id=1, source_target_pairs={{0,8},{1,57},{8,0},{9,17},{16,24},{17,9},{24,16},{25,33},{32,40},{... | collective-permute-start | bytes 737288 | tf_op jit(solution)/shard_map/ppermute | solution.py:39
  144.0 13.8 %copy-start.4 = (bf16[2,8,48,768]{3,2,1,0:T(8,128)(2,1)S(1)}, bf16[2,8,48,768]{3,2,1,0:T(8,128)(2,1)}, u32[]{:S(2)}) copy-start(bf16[2,8,48,768]{3,2,1,0:T(8,128)(2,1)} %get-tuple-element.43) | copy-start | bytes 3538948
  149.1 8.8 %collective-permute-start.23 = (bf16[64,768]{1,0:T(8,128)(2,1)S(1)}, bf16[64,768]{1,0:T(8,128)(2,1)S(1)}, u32[]{:S(2)}, u32[]{:S(2)}) collective-permute-start(bf16[64,768]{1,0:T(8,128)(2,1)S(1)} %get-tuple-element.45), channel_id=1, source_target_pairs={{0,128},{128,0},{1,129},{129,1},{2,130},{130,2},{3,131},{131,3},{4... | collective-permute-start | bytes 294920 | tf_op jit(solution)/shard_map/ppermute | solution.py:28
  151.1 14.8 %all-to-all-start.3 = ((f32[16,6,768]{2,1,0:T(8,128)}), f32[16,6,768]{2,1,0:T(8,128)S(1)}, u32[]{:S(2)}, u32[]{:S(2)}) async-start(f32[16,6,768]{2,1,0:T(8,128)} %reshape.109), calls=%async_computation.3 | async-start | bytes 786432 | tf_op jit(solution)/shard_map/all_to_all | solution.py:393
